TPU v7x, 256 devices: a whole 4x4x8 slice. The times are simulated.
256 devices in a mesh: seq: 32 (over x, y, core), head: 8 (over z).
Axes of the slice: x: 4, y: 4, z: 8, core: 2. Of those that a mesh axis runs over, the one named last changes fastest.
Arguments:
- video_feat: bfloat16 [128, 16, 64, 512], P('seq', 'head'), may hold values from -6 to 6
- clip_frames: int32 [64], replicated, may hold values from 1 to 3, as said below
- clip_offset: int32 [64], replicated, may hold values from 0 to 127, as said below
- conv_weight: bfloat16 [3, 3, 3, 512, 512], P(None, None, None, None, 'head'), may hold values from -0.0546875 to 0.0546875
- conv_bias: float32 [512], replicated, may hold values from -3 to 3
- latent_weight: bfloat16 [512, 16], replicated, may hold values from -0.25 to 0.25
- latent_bias: float32 [16], replicated, may hold values from -6 to 6
- embed_weight: bfloat16 [64, 3072], replicated, may hold values from -0.75 to 0.75
- embed_bias: float32 [3072], replicated, may hold values from -3 to 3
- modulation: bfloat16 [64, 6144], replicated, may hold values from -3 to 3
- qkv_weight: bfloat16 [3072, 6144], P(None, 'head'), may hold values from -1 to 1
- qkv_bias: float32 [6144], P('head'), may hold values from -3 to 3
- q_gain: float32 [128], replicated, may hold values from 0.5 to 5
- k_gain: float32 [128], replicated, may hold values from 0.5 to 5
Outputs:
- attn_out: bfloat16 [32768, 2048], P('seq', 'head')
Inputs may be any that keep to these rules, and one draw needn't show every extreme that they name: `clip_frames`: laid end to end in order the clips fill the 128 source frames exactly; every shard's 4 destination slots hold exactly two clips. Clip i takes the destination slots clip_offset[i] to clip_offset[i] + clip_frames[i] - 1, all inside one shard's slots q * 4 to (q + 1) * 4 - 1; the clips' slots cover all 128 slots once.
All inputs are finite; a program needn't handle non-finite values.
Results may differ from a plain program's by a relative error of at most 0.008.
Values may be sent and summed in bfloat16 or wider, within the bound.
No kernel may reach another device: no remote copies, remote signals or barrier semaphores. Data moves between devices by JAX's collectives and lax.ppermute only.
A program may use at most 192 MiB of HBM per device.

v0:
```python
import math

import jax
import jax.numpy as jnp
from jax import lax
from jax.sharding import PartitionSpec as P

latent_scale = 0.476986
norm_eps = 1e-06


def from_behind(value, axis, steps):
    count = lax.axis_size(axis)
    leading, last = (max(0, -steps), min(count, count - steps))
    return lax.ppermute(value, axis, [(source, source + steps) for source in range(leading, last)])


def with_halo(block, sides, width):
    for axis, dim in sides:
        count = lax.axis_size(axis)
        forward = [(i, i + 1) for i in range(count - 1)]
        backward = [(target, source) for source, target in forward]
        low = lax.ppermute(
            lax.slice_in_dim(block, block.shape[dim] - width, None, axis=dim), axis, forward
        )
        high = lax.ppermute(lax.slice_in_dim(block, 0, width, axis=dim), axis, backward)
        block = jnp.concatenate([low, block, high], axis=dim)
    return block


def frame_tables(clip_frames, clip_offset, count):
    ends = jnp.cumsum(clip_frames)
    starts = ends - clip_frames
    frame_ids = jnp.arange(count, dtype=jnp.int32)
    member = (frame_ids[:, None] >= starts[None, :]) & (frame_ids[:, None] < ends[None, :])
    first = jnp.sum(jnp.where(member, starts[None, :], 0), axis=1)
    target = jnp.sum(jnp.where(member, clip_offset[None, :], 0), axis=1) + frame_ids - first
    return (first, target)


def slot_tables(clip_frames, clip_offset, modulation, shard, frames):
    slots = shard * frames + jnp.arange(frames, dtype=jnp.int32)
    member = (slots[:, None] >= clip_offset[None, :]) & (
        slots[:, None] < (clip_offset + clip_frames)[None, :]
    )
    numbers = jnp.arange(clip_frames.shape[0], dtype=jnp.int32)
    clip_ids = jnp.sum(jnp.where(member, numbers[None, :], 0), axis=1)
    slot_mod = jnp.dot(member.astype(jnp.bfloat16), modulation, preferred_element_type=jnp.float32)
    return (clip_ids, slot_mod)


def modulate(tokens, frames, columns, slot_mod, embed_weight, embed_bias):
    width = embed_weight.shape[1]
    embedded = jnp.dot(tokens, embed_weight, preferred_element_type=jnp.float32) + embed_bias
    mean = jnp.mean(embedded, axis=-1, keepdims=True)
    centered = embedded - mean
    variance = jnp.mean(centered * centered, axis=-1, keepdims=True)
    normed = (centered * lax.rsqrt(variance + norm_eps)).reshape(-1, frames, columns, width)
    shift = slot_mod[None, :, None, :width]
    scale = slot_mod[None, :, None, width:]
    return (normed * (1.0 + scale) + shift).reshape(-1, width).astype(jnp.bfloat16)


def rms_scale(part, gain):
    factor = lax.rsqrt(jnp.mean(part * part, axis=-1, keepdims=True) + norm_eps)
    return (part * factor * gain).astype(jnp.bfloat16)


def attend(qkv, head_size, row_clip, q_gain, k_gain):
    rows = qkv.shape[0]
    split = qkv.reshape(rows, -1, 3, head_size)
    query = rms_scale(split[:, :, 0], q_gain)
    keys = rms_scale(split[:, :, 1], k_gain)
    values = split[:, :, 2].astype(jnp.bfloat16)
    scores = jnp.einsum(
        "qhd,khd->hqk", query, keys, preferred_element_type=jnp.float32
    ) / math.sqrt(head_size)
    same = row_clip[:, None] == row_clip[None, :]
    scores = jnp.where(same[None], scores, -jnp.inf)
    top = jnp.max(scores, axis=-1, keepdims=True)
    expo = jnp.exp(scores - top)
    weights = (expo / jnp.sum(expo, axis=-1, keepdims=True)).astype(jnp.bfloat16)
    output = jnp.einsum("hqk,khd->qhd", weights, values, preferred_element_type=jnp.float32)
    return output.astype(jnp.bfloat16).reshape(rows, -1)


def per_device(
    video_feat,
    clip_frames,
    clip_offset,
    conv_weight,
    conv_bias,
    latent_weight,
    latent_bias,
    embed_weight,
    embed_bias,
    modulation,
    qkv_weight,
    qkv_bias,
    q_gain,
    k_gain,
):
    seq_count = lax.axis_size("seq")
    band_count = lax.axis_size("head")
    seq_index = lax.axis_index("seq")
    frames = video_feat.shape[0]
    height = video_feat.shape[1]
    width = video_feat.shape[2]
    channels = video_feat.shape[3]
    columns = width // 2
    lat_count = latent_weight.shape[1]
    head_size = q_gain.shape[0]
    first, target = frame_tables(clip_frames, clip_offset, frames * seq_count)
    rim = from_behind(video_feat[frames - 2 :], "seq", 1)
    extended = jnp.concatenate([rim, video_feat], axis=0)
    act = jax.nn.silu(extended.astype(jnp.float32)).astype(jnp.bfloat16)
    padded = with_halo(act, (("head", 1),), 1)
    padded = jnp.pad(padded, ((0, 0), (0, 0), (1, 1), (0, 0)))
    base = seq_index * frames
    local_ids = base + jnp.arange(frames, dtype=jnp.int32)
    local_first = lax.dynamic_slice_in_dim(first, base, frames)
    windows = []
    for delay in range(3):
        source = jnp.maximum(local_ids - (2 - delay), local_first) - base + 2
        picked = jnp.take(padded, source, axis=0)
        for row_step in range(3):
            for col_step in range(3):
                windows.append(
                    picked[:, row_step : row_step + height, col_step : col_step + width, :]
                )
    stacked = jnp.concatenate(windows, axis=-1).reshape(frames * height * width, 27 * channels)
    conv = jnp.dot(
        stacked,
        lax.all_gather(conv_weight, "head", axis=4, tiled=True).reshape(27 * channels, -1),
        preferred_element_type=jnp.float32,
    )
    section = (video_feat.astype(jnp.float32).reshape(-1, channels) + conv + conv_bias).astype(
        jnp.bfloat16
    )
    latent = (
        (jnp.dot(section, latent_weight, preferred_element_type=jnp.float32) + latent_bias)
        * latent_scale
    ).astype(jnp.bfloat16)
    pieces = latent.reshape(frames, 2, columns, 2, lat_count).transpose(0, 2, 4, 1, 3)
    pieces = pieces.reshape(frames, columns * 4 * lat_count)
    clip_ids, slot_mod = slot_tables(clip_frames, clip_offset, modulation, seq_index, frames)
    group = band_count * frames * columns
    row_slots = jnp.arange(group, dtype=jnp.int32) // columns % frames
    row_clip = jnp.take(clip_ids, row_slots)
    piece = lax.all_gather(pieces, ("seq", "head"), axis=0, tiled=True)
    source_rows = jnp.arange(piece.shape[0], dtype=jnp.int32)
    source = source_rows // (band_count * frames) * frames + source_rows % frames
    band_ids = source_rows // frames % band_count
    destined = jnp.take(target, source)
    place = jnp.where(destined // frames == seq_index, band_ids * frames + destined % frames, -1)
    select = (jnp.arange(band_count * frames, dtype=jnp.int32)[:, None] == place[None, :]).astype(
        jnp.bfloat16
    )
    gathered = jnp.dot(select, piece, preferred_element_type=jnp.float32).astype(jnp.bfloat16)
    hidden = modulate(
        gathered.reshape(group, 4 * lat_count), frames, columns, slot_mod, embed_weight, embed_bias
    )
    qkv = jnp.dot(hidden, qkv_weight, preferred_element_type=jnp.float32) + qkv_bias
    return attend(qkv, head_size, row_clip, q_gain, k_gain)


def solution(mesh):
    placed = (
        P("seq", "head", None, None),
        P(),
        P(),
        P(None, None, None, None, "head"),
        P(),
        P(),
        P(),
        P(),
        P(),
        P(),
        P(None, "head"),
        P("head"),
        P(),
        P(),
    )
    return jax.shard_map(
        per_device, mesh=mesh, in_specs=placed, out_specs=P("seq", "head"), check_vma=False
    )
```

profile of v0, /device:TPU:1, one launch (start us, length us, event | category | flops | bytes accessed | tf_op | source)
XLA Modules:
  0.0 381.1 jit_solution(11670087594237235764)
XLA Ops:
  8.3 4.6 %collective-permute-start = (bf16[2,2,64,512]{3,2,1,0:T(8,128)(2,1)S(1)}, bf16[2,2,64,512]{3,2,1,0:T(8,128)(2,1)S(1)}, u32[]{:S(2)}, u32[]{:S(2)}) collective-permute-start(bf16[2,2,64,512]{3,2,1,0:T(8,128)(2,1)S(1)} %slice.106), channel_id=1, source_target_pairs={{0,8},{8,16},{16,24},{24,32},{32,40},{40,48},{48,56},{56,64},{64,7... | collective-permute-start | bytes 786440 | tf_op jit(solution)/shard_map/ppermute | solution.py:15
  17.8 3.6 collective-permute-start.1
  22.8 11.6 %collective-permute-done.1 = bf16[6,1,64,512]{3,2,1,0:T(8,128)(2,1)S(1)} collective-permute-done((bf16[6,1,64,512]{3,2,1,0:T(8,128)(2,1)S(1)}, bf16[6,1,64,512]{3,2,1,0:T(8,128)(2,1)S(1)}, u32[]{:S(2)}, u32[]{:S(2)}) %collective-permute-start.1) | collective-permute-done | bytes 393248 | tf_op jit(solution)/shard_map/ppermute | solution.py:23
  34.4 6.8 %collective-permute-done.2 = bf16[6,1,64,512]{3,2,1,0:T(8,128)(2,1)S(1)} collective-permute-done((bf16[6,1,64,512]{3,2,1,0:T(8,128)(2,1)S(1)}, bf16[6,1,64,512]{3,2,1,0:T(8,128)(2,1)S(1)}, u32[]{:S(2)}, u32[]{:S(2)}) %collective-permute-start.2) | collective-permute-done | bytes 393248 | tf_op jit(solution)/shard_map/ppermute | solution.py:26
  42.1 1.6 gather_fusion.1
  43.7 1.7 gather_fusion.2
  45.4 1.6 gather_fusion.3
  47.0 1.6 broadcast_select_fusion.2
  74.1 92.0 %all-gather.4.cloned.1.call-done = bf16[3,3,3,512,512]{3,4,2,1,0:T(8,128)(2,1)} async-done(((bf16[3,3,3,512,64]{3,4,2,1,0:T(8,128)(2,1)}), bf16[3,3,3,512,512]{3,4,2,1,0:T(8,128)(2,1)}) %all-gather.4.cloned.1.call-update) | async-done | bytes 14155792 | tf_op jit(solution)/shard_map/all_gather | solution.py:134
  166.1 18.6 %copy.51 = bf16[3,3,3,512,512]{4,3,2,1,0:T(8,128)(2,1)} copy(bf16[3,3,3,512,512]{3,4,2,1,0:T(8,128)(2,1)} %all-gather.4.cloned.1.call-done) | data formatting | bytes 28311552 | tf_op jit(solution)/shard_map/all_gather | solution.py:134
  184.8 14.7 %fusion.19 = bf16[512,512]{1,0:T(8,128)(2,1)S(1)} fusion(bf16[512,13824]{1,0:T(8,128)(2,1)} %bitcast.3, bf16[13824,512]{1,0:T(8,128)(2,1)} %bitcast.77, bf16[512,512]{1,0:T(8,128)(2,1)S(1)} %bitcast.81, f32[512]{0:T(512)S(1)} %copy-done.13), kind=kOutput, calls=%fused_computation.38 | convolution fusion | flops 7248805888 | bytes 29362176 | tf_op jit(solution)/shard_map/dot_general | solution.py:132
  201.8 6.6 %gather_fusion = s32[1024]{0:T(1024)S(1)} fusion(s32[128]{0:T(128)S(1)} %add_subtract_fusion, s32[1024]{0:T(1024)S(1)} %broadcast_clamp_fusion), kind=kCustom, calls=%fused_computation.3 | custom fusion | bytes 12288 | tf_op jit(solution)/shard_map/jit(_take)/gather | solution.py:154
  209.2 2.5 compare_select_fusion.4
  212.0 1.7 broadcast_compare_fusion
  213.6 106.0 %all-gather.6.cloned.1.call-done = bf16[256,4,2048]{2,1,0:T(4,128)(2,1)} async-done(((bf16[1,4,2048]{2,1,0:T(4,128)(2,1)}), bf16[256,4,2048]{2,1,0:T(4,128)(2,1)}) %all-gather.6.cloned.1.call-update) | async-done | bytes 4194320 | tf_op jit(solution)/shard_map/all_gather | solution.py:150
  319.6 6.9 %reshape.439 = bf16[1024,2048]{1,0:T(8,128)(2,1)} reshape(bf16[256,4,2048]{2,1,0:T(4,128)(2,1)} %all-gather.6.cloned.1.call-done) | data formatting | bytes 8388608
  326.6 3.0 convolution_convert_fusion
  329.8 1.9 add_reduce_fusion
  331.7 4.5 %copy-done.2 = f32[1024,3072]{1,0:T(8,128)} copy-done((f32[1024,3072]{1,0:T(8,128)}, f32[1024,3072]{1,0:T(8,128)S(1)}, u32[]{:S(2)}) %copy-start.2) | copy-done | bytes 12582936
  336.2 1.8 multiply_reduce_fusion
  338.1 10.6 %fusion.1 = bf16[1024,3072]{1,0:T(8,128)(2,1)} fusion(f32[1024,3072]{1,0:T(8,128)} %copy-done.2, f32[4,3072]{1,0:T(4,128)S(1)} %get-tuple-element.21, f32[4,3072]{1,0:T(4,128)S(1)} %get-tuple-element.20, f32[1024]{0:T(1024)S(1)} %add_rsqrt_fusion.2, f32[1024]{0:T(1024)S(1)} %broadcast_multiply_fusion, f32[3072]{0:T(1024)S(1)} %copy-done.8), kind=kLoop, calls=%fused_computation.6 | loop fusion | flops 18874368 | bytes 18993152 | tf_op jit(solution)/shard_map/convert_element_type | solution.py:61
  348.6 8.6 %convolution_add_fusion = f32[1024,768]{0,1:T(8,128)S(1)} fusion(bf16[1024,3072]{1,0:T(8,128)(2,1)} %fusion.1, bf16[3072,768]{1,0:T(8,128)(2,1)} %param.26, f32[768]{0:T(1024)S(1)} %copy-done.12), kind=kOutput, calls=%fused_computation.30 | convolution fusion | flops 4832624640 | bytes 14158848 | tf_op jit(solution)/shard_map/dot_general | solution.py:163
  361.9 6.9 %fusion.72 = (f32[2,1024]{1,0:T(2,128)S(1)}, f32[2,1024,1024]{1,2,0:T(8,128)}) fusion(pred[1024,1024]{0,1:T(8,128)(4,1)} %broadcast_compare_fusion, f32[1024,2,1,128]{3,0,1,2:T(8,128)S(1)} %copy.61, f32[128]{0:T(128)S(1)} %copy-done.14, f32[1024,2]{0,1:T(2,128)S(1)} %add_rsqrt_fusion.1, f32[1024,2,1,128]{3,0,1,2:T(8,128)S(1)} %copy.62, ...), kind=kOutput, calls=%fused_computation.174 | convolution fusion | flops 546833408 | bytes 11559936 | tf_op jit(solution)/shard_map/sub | solution.py:81
  368.7 4.5 %fusion.18 = bf16[2,128,1024]{2,1,0:T(8,128)(2,1)S(1)} fusion(f32[2,1024,1024]{1,2,0:T(8,128)} %get-tuple-element.35, f32[2,1024]{1,0:T(2,128)S(1)} %get-tuple-element.34, f32[1024,2,3,128]{0,3,2,1:T(8,128)} %bitcast.80), kind=kOutput, calls=%fused_computation.37 | convolution fusion | flops 541327360 | bytes 9445376 | tf_op jit(solution)/shard_map/hqk,khd->qhd/dot_general | solution.py:83
  (103 shorter events, 43.4 us)
Async XLA Ops:
  6.5 205.2 %copy-start = (bf16[64,6144]{1,0:T(8,128)(2,1)S(1)}, bf16[64,6144]{1,0:T(8,128)(2,1)}, u32[]{:S(2)}) copy-start(bf16[64,6144]{1,0:T(8,128)(2,1)} %param.25) | copy-start | bytes 2359300
  6.5 159.6 %all-gather.4.cloned.1.call-start = ((), (), s32[]{:S(2)}) async-start(), calls=%async_computation | async-start | bytes 15925248 | tf_op jit(solution)/shard_map/all_gather | solution.py:134
  7.3 312.4 %all-gather.6.cloned.1.call-start = ((), (), s32[]{:S(2)}) async-start(), calls=%async_computation.1 | async-start | bytes 4210688 | tf_op jit(solution)/shard_map/all_gather | solution.py:150
  8.3 7.9 %collective-permute-start = (bf16[2,2,64,512]{3,2,1,0:T(8,128)(2,1)S(1)}, bf16[2,2,64,512]{3,2,1,0:T(8,128)(2,1)S(1)}, u32[]{:S(2)}, u32[]{:S(2)}) collective-permute-start(bf16[2,2,64,512]{3,2,1,0:T(8,128)(2,1)S(1)} %slice.106), channel_id=1, source_target_pairs={{0,8},{8,16},{16,24},{24,32},{32,40},{40,48},{48,56},{56,64},{64,7... | collective-permute-start | bytes 786440 | tf_op jit(solution)/shard_map/ppermute | solution.py:15
  17.8 16.6 %collective-permute-start.1 = (bf16[6,1,64,512]{3,2,1,0:T(8,128)(2,1)S(1)}, bf16[6,1,64,512]{3,2,1,0:T(8,128)(2,1)S(1)}, u32[]{:S(2)}, u32[]{:S(2)}) collective-permute-start(bf16[6,1,64,512]{3,2,1,0:T(8,128)(2,1)S(1)} %get-tuple-element.18), channel_id=1, source_target_pairs={{0,1},{1,2},{2,3},{3,4},{4,5},{5,6},{6,7},{8,9},{9,10},{10,11},{11... | collective-permute-start | bytes 1179656 | tf_op jit(solution)/shard_map/ppermute | solution.py:23
  21.3 19.9 %collective-permute-start.2 = (bf16[6,1,64,512]{3,2,1,0:T(8,128)(2,1)S(1)}, bf16[6,1,64,512]{3,2,1,0:T(8,128)(2,1)S(1)}, u32[]{:S(2)}, u32[]{:S(2)}) collective-permute-start(bf16[6,1,64,512]{3,2,1,0:T(8,128)(2,1)S(1)} %get-tuple-element.19), channel_id=1, source_target_pairs={{1,0},{2,1},{3,2},{4,3},{5,4},{6,5},{7,6},{9,8},{10,9},{11,10},{12... | collective-permute-start | bytes 1179656 | tf_op jit(solution)/shard_map/ppermute | solution.py:26
  47.0 10.0 %copy-start.3 = (bf16[4,4,66,512]{3,2,1,0:T(8,128)(2,1)S(1)}, bf16[4,4,66,512]{3,2,1,0:T(8,128)(2,1)}, u32[]{:S(2)}) copy-start(bf16[4,4,66,512]{3,2,1,0:T(8,128)(2,1)} %gather_fusion.2) | copy-start | bytes 3244036
  47.0 10.0 %copy-start.4 = (bf16[4,4,66,512]{3,2,1,0:T(8,128)(2,1)S(1)}, bf16[4,4,66,512]{3,2,1,0:T(8,128)(2,1)}, u32[]{:S(2)}) copy-start(bf16[4,4,66,512]{3,2,1,0:T(8,128)(2,1)} %gather_fusion.3) | copy-start | bytes 3244036
  74.1 110.7 %copy-start.6 = (bf16[4,2,64,512]{3,2,1,0:T(8,128)(2,1)S(1)}, bf16[4,2,64,512]{3,2,1,0:T(8,128)(2,1)}, u32[]{:S(2)}) copy-start(bf16[4,2,64,512]{3,2,1,0:T(8,128)(2,1)} %param.16) | copy-start | bytes 1572868
  74.1 110.7 %copy-start.13 = (f32[512]{0:T(512)S(1)}, f32[512]{0:T(512)}, u32[]{:S(2)}) copy-start(f32[512]{0:T(512)} %param.20) | copy-start | bytes 6148
  184.7 14.8 %copy-start.9 = (bf16[512,16]{0,1:T(8,128)(2,1)S(1)}, bf16[512,16]{0,1:T(8,128)(2,1)}, u32[]{:S(2)}) copy-start(bf16[512,16]{0,1:T(8,128)(2,1)} %param.21) | copy-start | bytes 49156
  184.8 14.8 %copy-start.11 = (f32[16]{0:T(128)S(1)}, f32[16]{0:T(128)}, u32[]{:S(2)}) copy-start(f32[16]{0:T(128)} %param.22) | copy-start | bytes 196
  184.8 23.6 %copy-start.10 = (s32[64]{0:T(128)S(1)}, s32[64]{0:T(128)}, u32[]{:S(2)}) copy-start(s32[64]{0:T(128)} %param.18) | copy-start | bytes 772
  208.4 121.4 %copy-start.7 = (bf16[64,3072]{1,0:T(8,128)(2,1)S(1)}, bf16[64,3072]{1,0:T(8,128)(2,1)}, u32[]{:S(2)}) copy-start(bf16[64,3072]{1,0:T(8,128)(2,1)} %param.23) | copy-start | bytes 1179652
  208.4 121.4 %copy-start.8 = (f32[3072]{0:T(1024)S(1)}, f32[3072]{0:T(1024)}, u32[]{:S(2)}) copy-start(f32[3072]{0:T(1024)} %param.24) | copy-start | bytes 36868
  331.7 4.6 %copy-start.2 = (f32[1024,3072]{1,0:T(8,128)}, f32[1024,3072]{1,0:T(8,128)S(1)}, u32[]{:S(2)}) copy-start(f32[1024,3072]{1,0:T(8,128)S(1)} %get-tuple-element.33) | copy-start | bytes 37748740
  338.0 10.6 %copy-start.12 = (f32[768]{0:T(1024)S(1)}, f32[768]{0:T(1024)}, u32[]{:S(2)}) copy-start(f32[768]{0:T(1024)} %param.27) | copy-start | bytes 9220
  357.3 1.9 copy-start.5
  357.3 4.6 %copy-start.14 = (f32[128]{0:T(128)S(1)}, f32[128]{0:T(128)}, u32[]{:S(2)}) copy-start(f32[128]{0:T(128)} %param.28) | copy-start | bytes 1540
  357.3 4.6 %copy-start.15 = (f32[128]{0:T(128)S(1)}, f32[128]{0:T(128)}, u32[]{:S(2)}) copy-start(f32[128]{0:T(128)} %param.29) | copy-start | bytes 1540
  368.7 5.5 %copy-start.1 = (bf16[64,6144]{1,0:T(8,128)(2,1)S(1)}, bf16[64,6144]{1,0:T(8,128)(2,1)}, u32[]{:S(2)}) copy-start(bf16[64,6144]{1,0:T(8,128)(2,1)} %param.25) | copy-start | bytes 2359300
Sparse Core Ops, SparseCore 0:
  9.2 156.9 all-gather.3
  201.9 117.7 all-gather.5
where the time goes:
time: 382 us; the launch traced here: 381 us
  waiting for transfers between devices  218 us (57%)
  local copies, waits for them, and re-layouts  76.3 us (20%)
  matrix products  40 us (10%)
  other arithmetic  23.5 us (6%)
  between operations  13.8 us (4%)
  starting transfers between devices  9.49 us (2%)
    all_gather x1, waiting for transfers between devices, per_device(): piece = lax.all_gather(pieces, ('seq', 'head'), axis=0, tiled=True)  106 us
    all_gather x1, waiting for transfers between devices, per_device(): lax.all_gather(conv_weight, 'head', axis=4, tiled=True)  92 us
    unnamed x62, local copies, waits for them, and re-layouts  39.1 us
    all_gather x1, local copies, waits for them, and re-layouts, per_device(): lax.all_gather(conv_weight, 'head', axis=4, tiled=True)  18.6 us
    dot_general x1, matrix products, per_device(): jnp.dot(stacked, lax.all_gather(conv_weight, 'head', axis=4, tiled=True)....  14.7 us
    ppermute x1, waiting for transfers between devices, with_halo(): lax.ppermute(lax.slice_in_dim(block, block.shape[dim] - width, None, axis...  11.6 us
    convert_element_type x1, other arithmetic, modulate(): (normed * (1.0 + scale) + shift).reshape(-1, width).astype(jnp.bfloat16)  10.6 us
    dot_general x1, matrix products, per_device(): jnp.dot(hidden, qkv_weight, preferred_element_type=jnp.float32) + qkv_bias  8.62 us
  transfers between devices with their start and end apart: 5, of which 5 were waited for; matrix products, arithmetic and copies ran while one was open for 13% of the time, Pallas kernels for 0%

commit v1 on v0

v1 whole, which is shorter than its diff:
```python
import functools
import math

import jax
import jax.numpy as jnp
from jax import lax
from jax.experimental import pallas as pl
from jax.experimental.pallas import tpu as pltpu
from jax.sharding import PartitionSpec as P

latent_scale = 0.476986
norm_eps = 1e-06
f32 = jnp.float32
bf16 = jnp.bfloat16
MIB = 1024 * 1024
NT = (((1,), (1,)), ((), ()))


def dot(a, b, dims=(((1,), (0,)), ((), ()))):
    return lax.dot_general(a, b, dims, preferred_element_type=f32)


def split2(value):
    high = value.astype(bf16)
    return high, (value - high.astype(f32)).astype(bf16)


def iota(shape, dim):
    return lax.broadcasted_iota(jnp.int32, shape, dim)


def fold_kernel(place_ref, weight_ref, latent_ref, out_ref):
    out_ref[...] = dot(latent_ref[...], weight_ref[0], (((0,), (0,)), ((), ())))


def fold_tap(weight, latent_weight, tap, band):
    taps, outs, ins = weight.shape
    lats = latent_weight.shape[1]
    return pl.pallas_call(
        fold_kernel,
        grid_spec=pltpu.PrefetchScalarGridSpec(
            num_scalar_prefetch=1,
            grid=(1,),
            in_specs=[
                pl.BlockSpec((1, outs, ins), lambda i, place: (place[0], 0, 0)),
                pl.BlockSpec((outs, lats), lambda i, place: (place[1], 0)),
            ],
            out_specs=pl.BlockSpec((lats, ins), lambda i, place: (0, 0)),
        ),
        out_shape=jax.ShapeDtypeStruct((lats, ins), f32),
        cost_estimate=pl.CostEstimate(flops=10**6, bytes_accessed=150000, transcendentals=0),
        name="fold_tap",
    )(jnp.stack([tap, band]).astype(jnp.int32), weight, latent_weight)


def prep_kernel(main, prev, lowm, highm, lowp, highp, lat, cbias, lbias, act, base):
    def silu(value):
        value = value.astype(f32)
        half = 0.5 * value
        return (half * jnp.tanh(half) + half).astype(bf16)

    for frame in range(6):
        if frame < 2:
            rows = (lowp[frame], prev[frame, 0], prev[frame, 1], highp[frame])
        else:
            own = frame - 2
            rows = (lowm[own], main[own, 0], main[own, 1], highm[own])
        for row, value in enumerate(rows):
            at = (frame * 4 + row) * 64
            act[at : at + 64, :] = silu(value)
    weight = lat[...]
    const = jnp.sum(weight.astype(f32) * cbias[...], axis=1, keepdims=True) + lbias[...]
    for frame in range(4):
        own = main[frame].reshape(128, 512)
        base[:, frame * 128 : frame * 128 + 128] = dot(weight, own, NT) + const


def prepare(video, prev, lowm, highm, lowp, highp, lat, conv_bias, latent_bias):
    return pl.pallas_call(
        prep_kernel,
        out_shape=(
            jax.ShapeDtypeStruct((1536, 512), bf16),
            jax.ShapeDtypeStruct((16, 512), f32),
        ),
        compiler_params=pltpu.CompilerParams(vmem_limit_bytes=24 * MIB),
        cost_estimate=pl.CostEstimate(flops=2 * 10**7, bytes_accessed=3 * 10**6, transcendentals=800000),
        name="prepare",
    )(video, prev, lowm, highm, lowp, highp, lat, conv_bias.reshape(1, -1), latent_bias.reshape(-1, 1))


def conv_kernel(source, target, act, folded, base, out, taps):
    weight = folded[...]
    for frame in range(6):
        taps[frame] = dot(weight[:432], act[frame * 256 : frame * 256 + 256, :], NT)
    out[...] = jnp.zeros_like(out)
    lane = iota((16, 128), 1)
    column = lane % 64
    row = iota((128, 128), 0)
    pos = iota((128, 128), 1)
    own_half = (pos % 64) // 32 == row // 64
    own_cell = (pos // 64) * 2 + pos % 2 == row % 4
    keep = own_half & own_cell
    repeat = (iota((128, 16), 0) % 64 // 4 == iota((128, 16), 1)).astype(bf16)
    pick = ((lane % 32) // 2 == iota((16, 128), 0)).astype(bf16)
    for frame in range(4):
        total = None
        for delay in range(3):
            part = taps[source[frame * 3 + delay], delay * 144 : delay * 144 + 144, :]
            total = part if total is None else total + part
        sums = []
        for col in range(3):
            at = [total[(a * 3 + col) * 16 : (a * 3 + col) * 16 + 16] for a in range(3)]
            sums.append(at[0][:, 0:128] + at[1][:, 64:192] + at[2][:, 128:256])
        left = jnp.where(column == 0, 0.0, pltpu.roll(sums[0], 1, 1))
        right = jnp.where(column == 63, 0.0, pltpu.roll(sums[2], 127, 1))
        own = base[:, frame * 128 : frame * 128 + 128]
        latent = ((own + sums[1] + left + right) * latent_scale).astype(bf16)
        wide = jnp.where(keep, dot(repeat, latent), 0.0).astype(bf16)
        out[target[frame]] = dot(pick, wide, NT).astype(bf16)


def convolve(source, target, act, folded, base, slots):
    smem = pl.BlockSpec(memory_space=pltpu.SMEM)
    vmem = pl.BlockSpec(memory_space=pltpu.VMEM)
    return pl.pallas_call(
        conv_kernel,
        in_specs=[smem, smem, vmem, vmem, vmem],
        out_specs=vmem,
        out_shape=jax.ShapeDtypeStruct((slots, 16, 128), bf16),
        scratch_shapes=[pltpu.VMEM((6, 432, 256), f32)],
        compiler_params=pltpu.CompilerParams(vmem_limit_bytes=24 * MIB),
        cost_estimate=pl.CostEstimate(flops=7 * 10**8, bytes_accessed=3 * 10**6, transcendentals=0),
        name="convolve",
    )(source, target, act, folded, base)


def mix_kernel(
    member, modulation, embed, bias, qkv_w, qkv_b, mix, rows, gram, gvec, left
):
    step = pl.program_id(0)
    width = embed.shape[1]
    chunk = 512

    @pl.when(step == 0)
    def _():
        mean = jnp.sum(embed[...].astype(f32), axis=1, keepdims=True) / width
        bias_mean = jnp.sum(bias[...], axis=1, keepdims=True) / width
        whole = jnp.zeros((80, 80), f32)
        for at in range(0, width, chunk):
            here = slice(at, at + chunk)
            centred = embed[:, here].astype(f32) - mean
            cbias = bias[:, here] - bias_mean
            scale = 1.0 + dot(member[...], modulation[:, width + at : width + at + chunk])
            shift = dot(member[...], modulation[:, here])
            first, second = scale[0:1], scale[1:2]
            high, low = split2(centred * first)
            left[0:64, here] = high
            left[64:128, here] = low
            high, low = split2(centred * second)
            left[128:192, here] = high
            left[192:256, here] = low
            high, low = split2(jnp.concatenate([cbias * first, cbias * second], axis=0))
            left[256:272, here] = jnp.concatenate(
                [high.astype(f32), low.astype(f32), shift[0:2], jnp.zeros((10, chunk), f32)], axis=0
            ).astype(bf16)
            full = jnp.concatenate([centred, cbias, jnp.zeros((15, chunk), f32)], axis=0)
            high, low = split2(full)
            whole = whole + (dot(high, high, NT) + dot(high, low, NT) + dot(low, high, NT))
        whole = whole * (1.0 / width)
        square = whole[0:64, 0:64]
        blank = jnp.zeros((64, 64), f32)
        block = jnp.concatenate(
            [
                jnp.concatenate([square, blank], axis=1),
                jnp.concatenate([blank, square], axis=1),
            ],
            axis=0,
        )
        top = block.astype(bf16)
        rest = block - top.astype(f32)
        mid = rest.astype(bf16)
        gram[0] = top
        gram[1] = mid
        gram[2] = (rest - mid.astype(f32)).astype(bf16)
        cross = 2.0 * whole[64:65, 0:64]
        const = jnp.broadcast_to(whole[64:65, 64:65], (1, 128))
        gvec[...] = jnp.concatenate(
            [jnp.concatenate([cross, cross], axis=1), const, jnp.zeros((6, 128), f32)], axis=0
        )

    product = dot(left[...], qkv_w[...])
    cols = product.shape[1]
    empty = jnp.zeros((64, cols), bf16)
    for clip in range(2):
        at = clip * 128
        high, low = split2(product[at : at + 64] + product[at + 64 : at + 128])
        mix[clip, 0] = jnp.concatenate([high, empty, low, empty], axis=0)
        mix[clip, 1] = jnp.concatenate([empty, high, empty, low], axis=0)
    tail = product[256:272]
    rows[...] = jnp.concatenate(
        [tail[0:2] + tail[2:4], tail[4:6] + qkv_b[...], jnp.zeros((4, cols), f32)], axis=0
    )


def mix_weights(member, modulation, embed_weight, embed_bias, qkv_weight, qkv_bias):
    width = embed_weight.shape[1]
    cols = 256
    whole = lambda shape: pl.BlockSpec(shape, lambda n: (0,) * len(shape))
    return pl.pallas_call(
        mix_kernel,
        grid=(qkv_weight.shape[1] // cols,),
        in_specs=[
            whole((8, 64)),
            whole((64, 2 * width)),
            whole((64, width)),
            whole((1, width)),
            pl.BlockSpec((width, cols), lambda n: (0, n)),
            pl.BlockSpec((1, cols), lambda n: (0, n)),
        ],
        out_specs=[
            pl.BlockSpec((2, 2, 256, cols), lambda n: (0, 0, 0, n)),
            pl.BlockSpec((8, cols), lambda n: (0, n)),
            whole((3, 128, 128)),
            whole((8, 128)),
        ],
        out_shape=[
            jax.ShapeDtypeStruct((2, 2, 256, 768), bf16),
            jax.ShapeDtypeStruct((8, 768), f32),
            jax.ShapeDtypeStruct((3, 128, 128), bf16),
            jax.ShapeDtypeStruct((8, 128), f32),
        ],
        scratch_shapes=[pltpu.VMEM((272, width), bf16)],
        compiler_params=pltpu.CompilerParams(vmem_limit_bytes=24 * MIB),
        cost_estimate=pl.CostEstimate(flops=13 * 10**8, bytes_accessed=6 * 10**6, transcendentals=0),
        name="mix_weights",
    )(
        member, modulation, embed_weight, embed_bias.reshape(1, -1), qkv_weight, qkv_bias.reshape(1, -1)
    )


def attend_kernel(lead, tokens, mix, rows, gram, gvec, q_gain, k_gain, out, query, keys, values):
    factor = math.log2(math.e) / math.sqrt(128)
    gain_q = q_gain[...] * factor
    gain_k = k_gain[...]
    low_lane = iota((128, 128), 1) < 64
    for frame in range(4):
        later = frame >= lead[0]
        clip = later.astype(jnp.int32)
        slope = jnp.where(later, rows[1:2, :], rows[0:1, :])
        offset = jnp.where(later, rows[3:4, :], rows[2:3, :])
        own = tokens[:, frame].reshape(128, 128)
        twice = jnp.concatenate([own, own], axis=1)
        spread = dot(own, gram[0]) + dot(own, gram[1]) + dot(own, gram[2])
        terms = (spread + gvec[0:1, :]) * own.astype(f32)
        for half in range(2):
            mine = jnp.where(low_lane == (half == 0), terms, 0.0)
            variance = jnp.sum(mine, axis=1, keepdims=True) + gvec[1:2, 0:1]
            scale = lax.rsqrt(jnp.maximum(variance, 0.0) + norm_eps)
            qkv = scale * (dot(twice, mix[clip, half]) + slope) + offset
            at = frame * 256 + half * 128
            for head in range(2):
                part = qkv[:, head * 384 : head * 384 + 128]
                norm = lax.rsqrt(jnp.mean(part * part, axis=1, keepdims=True) + norm_eps)
                query[head, at : at + 128, :] = (part * norm * gain_q).astype(bf16)
                part = qkv[:, head * 384 + 128 : head * 384 + 256]
                norm = lax.rsqrt(jnp.mean(part * part, axis=1, keepdims=True) + norm_eps)
                keys[head, at : at + 128, :] = (part * norm * gain_k).astype(bf16)
                values[head, at : at + 128, :] = qkv[:, head * 384 + 256 : head * 384 + 384].astype(bf16)

    def group(begin, end):
        for head in range(2):
            key = keys[head, begin * 256 : end * 256, :]
            value = values[head, begin * 256 : end * 256, :]
            for frame in range(begin, end):
                score = dot(query[head, frame * 256 : frame * 256 + 256, :], key, NT)
                top = jnp.max(score, axis=1, keepdims=True)
                expo = jnp.exp2(score - top)
                total = jnp.sum(expo, axis=1, keepdims=True)
                result = (dot(expo.astype(bf16), value) / total).astype(bf16)
                for half in range(2):
                    out[:, frame, half, :, head * 128 : head * 128 + 128] = result[
                        half * 128 : half * 128 + 128
                    ].reshape(8, 16, 128)

    for first in (1, 2, 3):

        @pl.when(lead[0] == first)
        def _(first=first):
            group(0, first)
            group(first, 4)


def attend(lead, tokens, mix, rows, gram, gvec, q_gain, k_gain):
    smem = pl.BlockSpec(memory_space=pltpu.SMEM)
    vmem = pl.BlockSpec(memory_space=pltpu.VMEM)
    return pl.pallas_call(
        attend_kernel,
        in_specs=[smem] + [vmem] * 7,
        out_specs=vmem,
        out_shape=jax.ShapeDtypeStruct((8, 4, 2, 16, 256), bf16),
        scratch_shapes=[pltpu.VMEM((2, 1024, 128), bf16)] * 3,
        compiler_params=pltpu.CompilerParams(vmem_limit_bytes=32 * MIB),
        cost_estimate=pl.CostEstimate(flops=10**9, bytes_accessed=3 * 10**6, transcendentals=1300000),
        name="attend",
    )(lead, tokens, mix, rows, gram, gvec, q_gain.reshape(1, -1), k_gain.reshape(1, -1))


def shift_pairs(seqs, heads, seq_step, head_step):
    pairs = []
    for seq in range(seqs):
        for head in range(heads):
            to_seq, to_head = seq + seq_step, head + head_step
            if 0 <= to_seq < seqs and 0 <= to_head < heads:
                pairs.append((seq * heads + head, to_seq * heads + to_head))
    return pairs


def spread_all(value, axis):
    count = lax.axis_size(axis)
    return lax.all_to_all(jnp.broadcast_to(value[None], (count,) + value.shape), axis, 0, 0)


def per_device(
    video_feat,
    clip_frames,
    clip_offset,
    conv_weight,
    conv_bias,
    latent_weight,
    latent_bias,
    embed_weight,
    embed_bias,
    modulation,
    qkv_weight,
    qkv_bias,
    q_gain,
    k_gain,
):
    seqs, heads = lax.axis_size("seq"), lax.axis_size("head")
    seq, band = lax.axis_index("seq"), lax.axis_index("head")
    frames = video_feat.shape[0]
    send = lambda value, a, b: lax.ppermute(value, ("seq", "head"), shift_pairs(seqs, heads, a, b))

    weight = conv_weight.transpose(0, 1, 2, 4, 3).reshape(27, conv_weight.shape[4], -1)
    part = fold_tap(weight, latent_weight, jnp.minimum(seq, 26), band)
    tap = jnp.sum(spread_all(part, "head"), axis=0).astype(bf16)
    folded = spread_all(tap, "seq").reshape(seqs * 16, -1)

    prev = send(video_feat[2:], 1, 0)
    lowm = send(video_feat[:, 1], 0, 1)
    highm = send(video_feat[:, 0], 0, -1)
    lowp = send(video_feat[2:, 1], 1, 1)
    highp = send(video_feat[2:, 0], 1, -1)
    act, base = prepare(
        video_feat, prev, lowm, highm, lowp, highp, latent_weight.T, conv_bias, latent_bias
    )

    count = clip_frames.shape[0]
    numbers = jnp.arange(count, dtype=jnp.int32)
    starts = jnp.sum(jnp.where(numbers[None, :] < numbers[:, None], clip_frames[None, :], 0), axis=1)
    ids = seq * frames + jnp.arange(frames, dtype=jnp.int32)
    first = jnp.max(jnp.where(starts[None, :] <= ids[:, None], starts[None, :], 0), axis=1)
    offset = jnp.sum(jnp.where(starts[None, :] == first[:, None], clip_offset[None, :], 0), axis=1)
    target = jnp.clip(offset + ids - first, 0, seqs * frames - 1)
    delays = jnp.arange(3, dtype=jnp.int32)
    source = jnp.maximum(ids[:, None] - 2 + delays[None, :], first[:, None]) - seq * frames + 2
    source = jnp.clip(source, 0, frames + 1).reshape(-1)
    leading = clip_offset == seq * frames
    lead = jnp.sum(jnp.where(leading, clip_frames, 0)).reshape(1)
    trailing = (clip_offset > seq * frames) & (clip_offset < (seq + 1) * frames)
    member = jnp.concatenate(
        [leading[None], trailing[None], jnp.zeros((6, count), jnp.bool_)], axis=0
    ).astype(bf16)

    mix, rows, gram, gvec = mix_weights(
        member, modulation, embed_weight, embed_bias, qkv_weight, qkv_bias
    )

    placed = convolve(source, target, act, folded, base, seqs * frames)
    routed = lax.all_to_all(placed.reshape(seqs, frames, 16, 128), "seq", 0, 0)
    slots = jnp.sum(routed, axis=0)
    tokens = spread_all(slots, "head")
    out = attend(lead, tokens, mix, rows, gram, gvec, q_gain, k_gain)
    return out.reshape(heads * frames * 32, 256)


def solution(mesh):
    placed = (
        P("seq", "head", None, None),
        P(),
        P(),
        P(None, None, None, None, "head"),
        P(),
        P(),
        P(),
        P(),
        P(),
        P(),
        P(None, "head"),
        P("head"),
        P(),
        P(),
    )
    return jax.shard_map(
        per_device, mesh=mesh, in_specs=placed, out_specs=P("seq", "head"), check_vma=False
    )
```

time: 382 us -> 98.8 us (0.26)
  waiting for transfers between devices: 218 us -> 19.6 us
  local copies, waits for them, and re-layouts: 76.3 us -> 15 us
  matrix products: 40 us -> 0 us
  starting transfers between devices: 9.49 us -> 44.5 us
  other arithmetic: 23.5 us -> 2.7 us
  Pallas kernels: 0 us -> 15.7 us
  between operations: 13.8 us -> 0.23 us
    all_gather x2 -> x0, waiting for transfers between devices: 198 us -> none  [the longest x1 106 us: per_device(): piece = lax.all_gather(pieces, ('seq', 'head'), axis=0, tiled=True)]
    dot_general x7 -> x0, matrix products: 33.1 us -> none  [the longest x1 14.7 us: per_device(): jnp.dot(stacked, lax.all_gather(conv_weight, 'head', axis=4, tiled=True)....]
    unnamed x62 -> x45, local copies, waits for them, and re-layouts: 39.1 us -> 9.43 us
    all_to_all x0 -> x4, starting transfers between devices: none -> 29.5 us  [the longest x3 25.8 us: spread_all(): lax.all_to_all(jnp.broadcast_to(value[None], (count,) + value.shape), axi...]
    all_to_all x0 -> x4, waiting for transfers between devices: none -> 19.6 us  [the longest x1 11.4 us: per_device(): routed = lax.all_to_all(placed.reshape(seqs, frames, 16, 128), 'seq', 0, 0)]
    ppermute x3 -> x5, waiting for transfers between devices: 19.3 us -> 0.01 us  [per_device(): lax.ppermute(value, ('seq', 'head'), shift_pairs(seqs, heads, a, b))]
    all_gather x1 -> x0, local copies, waits for them, and re-layouts: 18.6 us -> none  [per_device(): lax.all_gather(conv_weight, 'head', axis=4, tiled=True)]
    pallas_call x0 -> x5, Pallas kernels: none -> 15.7 us  [the longest x1 6.22 us: attend(): pl.pallas_call(attend_kernel, in_specs=[smem] + [vmem] * 7, out_specs=vme...]
  transfers between devices with their start and end apart: 5 -> 9, of which waited for: 5 -> 4; matrix products, arithmetic and copies ran while one was open for 13% -> 8% of each run, Pallas kernels for 0% -> 7%
where the time goes in v1:
time: 98.8 us; the launch traced here: 97.6 us
  starting transfers between devices  44.5 us (45%)
  waiting for transfers between devices  19.6 us (20%)
  Pallas kernels  15.7 us (16%)
  local copies, waits for them, and re-layouts  15 us (15%)
  other arithmetic  2.7 us (3%)
    all_to_all x3, starting transfers between devices, spread_all(): lax.all_to_all(jnp.broadcast_to(value[None], (count,) + value.shape), axi...  25.8 us
    ppermute x5, starting transfers between devices, per_device(): lax.ppermute(value, ('seq', 'head'), shift_pairs(seqs, heads, a, b))  14.9 us
    all_to_all x1, waiting for transfers between devices, per_device(): routed = lax.all_to_all(placed.reshape(seqs, frames, 16, 128), 'seq', 0, 0)  11.4 us
    unnamed x45, local copies, waits for them, and re-layouts  9.43 us
    all_to_all x3, waiting for transfers between devices, spread_all(): lax.all_to_all(jnp.broadcast_to(value[None], (count,) + value.shape), axi...  8.22 us
    pallas_call x1, Pallas kernels, attend(): pl.pallas_call(attend_kernel, in_specs=[smem] + [vmem] * 7, out_specs=vme...  6.22 us
    all_to_all x1, starting transfers between devices, per_device(): routed = lax.all_to_all(placed.reshape(seqs, frames, 16, 128), 'seq', 0, 0)  3.68 us
    pallas_call x1, Pallas kernels, mix_weights(): pl.pallas_call(mix_kernel, grid=(qkv_weight.shape[1] // cols,), in_specs=...  3.31 us
  transfers between devices with their start and end apart: 9, of which 4 were waited for; matrix products, arithmetic and copies ran while one was open for 8% of the time, Pallas kernels for 7%

profile of v1, /device:TPU:1, one launch (start us, length us, event | category | flops | bytes accessed | tf_op | source)
XLA Modules:
  0.0 97.6 jit_solution(5684519039152560126)
XLA Ops:
  0.0 1.1 %slice_bitcast_fusion = (bf16[4,64,512]{2,1,0:T(8,128)(2,1)S(1)}, bf16[4,64,512]{2,1,0:T(8,128)(2,1)S(1)}) fusion(bf16[4,2,64,512]{3,2,1,0:T(8,128)(2,1)} %main.1), kind=kLoop, calls=%fused_computation | loop fusion | bytes 1048576 | tf_op jit(solution)/shard_map/squeeze | solution.py:351
  1.1 4.4 %collective-permute-start.1 = (bf16[4,64,512]{2,1,0:T(8,128)(2,1)S(1)}, bf16[4,64,512]{2,1,0:T(8,128)(2,1)S(1)}, u32[]{:S(2)}, u32[]{:S(2)}) collective-permute-start(bf16[4,64,512]{2,1,0:T(8,128)(2,1)S(1)} %get-tuple-element.20), channel_id=1, source_target_pairs={{0,1},{1,2},{2,3},{3,4},{4,5},{5,6},{6,7},{8,9},{9,10},{10,11},{11... | collective-permute-start | bytes 786440 | tf_op jit(solution)/shard_map/ppermute | solution.py:342
  5.5 1.3 %collective-permute-start.2 = (bf16[4,64,512]{2,1,0:T(8,128)(2,1)S(1)}, bf16[4,64,512]{2,1,0:T(8,128)(2,1)S(1)}, u32[]{:S(2)}, u32[]{:S(2)}) collective-permute-start(bf16[4,64,512]{2,1,0:T(8,128)(2,1)S(1)} %get-tuple-element.19), channel_id=1, source_target_pairs={{1,0},{2,1},{3,2},{4,3},{5,4},{6,5},{7,6},{9,8},{10,9},{11,10},{12... | collective-permute-start | bytes 786440 | tf_op jit(solution)/shard_map/ppermute | solution.py:342
  6.8 1.5 %copy.26.latent_ref = bf16[512,16]{1,0:T(8,128)(2,1)} copy(bf16[512,16]{0,1:T(8,128)(2,1)} %param.19) | data formatting | bytes 32768 | tf_op args[5]
  9.0 2.4 %fold_tap.1 = f32[16,512]{1,0:T(8,128)} custom-call(s32[2]{0:T(128)} %pad_add_fusion.place_ref, bf16[27,64,512]{2,1,0:T(8,128)(2,1)} %bitcast.41, bf16[512,16]{1,0:T(8,128)(2,1)} %copy.26.latent_ref), custom_call_target="tpu_custom_call" | custom-call | flops 1000000 | bytes 150000 | tf_op jit(solution)/shard_map/fold_tap/pallas_call | solution.py:39
  11.4 1.5 %broadcast_in_dim.76 = f32[8,16,512]{2,1,0:T(8,128)} broadcast(f32[16,512]{1,0:T(8,128)} %fold_tap.1), dimensions={1,2} | broadcast | bytes 294912 | tf_op jit(solution)/shard_map/broadcast_in_dim | solution.py:320
  12.9 10.0 %all-to-all-start = ((f32[8,16,512]{2,1,0:T(8,128)}), f32[8,16,512]{2,1,0:T(8,128)S(1)}, u32[]{:S(2)}, u32[]{:S(2)}) async-start(f32[8,16,512]{2,1,0:T(8,128)} %broadcast_in_dim.76), calls=%async_computation | async-start | bytes 524288 | tf_op jit(solution)/shard_map/all_to_all | solution.py:320
  22.9 6.1 %collective-permute-start.3 = (bf16[2,64,512]{2,1,0:T(8,128)(2,1)S(1)}, bf16[2,64,512]{2,1,0:T(8,128)(2,1)S(1)}, u32[]{:S(2)}, u32[]{:S(2)}) collective-permute-start(bf16[2,64,512]{2,1,0:T(8,128)(2,1)S(1)} %get-tuple-element.18), channel_id=1, source_target_pairs={{0,9},{1,10},{2,11},{3,12},{4,13},{5,14},{6,15},{8,17},{9,18},{10,... | collective-permute-start | bytes 393224 | tf_op jit(solution)/shard_map/ppermute | solution.py:342
  28.9 1.3 %collective-permute-start.4 = (bf16[2,64,512]{2,1,0:T(8,128)(2,1)S(1)}, bf16[2,64,512]{2,1,0:T(8,128)(2,1)S(1)}, u32[]{:S(2)}, u32[]{:S(2)}) collective-permute-start(bf16[2,64,512]{2,1,0:T(8,128)(2,1)S(1)} %get-tuple-element.17), channel_id=1, source_target_pairs={{1,8},{2,9},{3,10},{4,11},{5,12},{6,13},{7,14},{9,16},{10,17},{11,... | collective-permute-start | bytes 393224 | tf_op jit(solution)/shard_map/ppermute | solution.py:342
  30.3 1.9 %collective-permute-start = (bf16[2,2,64,512]{3,2,1,0:T(8,128)(2,1)S(1)}, bf16[2,2,64,512]{3,2,1,0:T(8,128)(2,1)S(1)}, u32[]{:S(2)}, u32[]{:S(2)}) collective-permute-start(bf16[2,2,64,512]{3,2,1,0:T(8,128)(2,1)S(1)} %slice.15), channel_id=1, source_target_pairs={{0,8},{1,9},{2,10},{3,11},{4,12},{5,13},{6,14},{7,15},{8,16},{9,17... | collective-permute-start | bytes 786440 | tf_op jit(solution)/shard_map/ppermute | solution.py:342
  33.0 0.9 broadcast_in_dim.77
  33.9 10.2 %all-to-all-start.1 = ((bf16[32,16,512]{2,1,0:T(8,128)(2,1)}), bf16[32,16,512]{2,1,0:T(8,128)(2,1)S(1)}, u32[]{:S(2)}, u32[]{:S(2)}) async-start(bf16[32,16,512]{2,1,0:T(8,128)(2,1)} %broadcast_in_dim.77), calls=%async_computation.1 | async-start | bytes 1048576 | tf_op jit(solution)/shard_map/all_to_all | solution.py:320
  46.9 0.9 copy-done.5
  49.1 0.8 prepare.1
  50.5 5.1 %all-to-all-done.1 = bf16[32,16,512]{2,1,0:T(8,128)(2,1)S(1)} async-done(((bf16[32,16,512]{2,1,0:T(8,128)(2,1)}), bf16[32,16,512]{2,1,0:T(8,128)(2,1)S(1)}, u32[]{:S(2)}, u32[]{:S(2)}) %all-to-all-start.1) | async-done | bytes 524320 | tf_op jit(solution)/shard_map/all_to_all | solution.py:320
  55.7 0.8 copy-done.8
  57.7 2.9 %convolve.1 = bf16[128,16,128]{2,1,0:T(8,128)(2,1)} custom-call(s32[12]{0:T(128)S(1)} %copy-done.12, s32[4]{0:T(128)S(1)} %copy-done.13, bf16[1536,512]{1,0:T(8,128)(2,1)S(1)} %get-tuple-element.11.act, bf16[512,512]{1,0:T(8,128)(2,1)S(1)} %bitcast.35, f32[16,512]{1,0:T(8,128)S(1)} %copy-done.8), custom_call_target="tpu_custom_call" | custom-call | flops 700000000 | bytes 3000000 | tf_op jit(solution)/shard_map/convolve/pallas_call | solution.py:125
  60.7 3.7 %all-to-all-start.2 = ((bf16[32,4,16,128]{3,2,1,0:T(8,128)(2,1)}), bf16[32,4,16,128]{3,2,1,0:T(8,128)(2,1)S(1)}, u32[]{:S(2)}, u32[]{:S(2)}) async-start(bf16[32,4,16,128]{3,2,1,0:T(8,128)(2,1)} %bitcast.13), calls=%async_computation.2 | async-start | bytes 1048576 | tf_op jit(solution)/shard_map/all_to_all | solution.py:380
  64.6 11.4 %all-to-all-done.2 = bf16[32,4,16,128]{3,2,1,0:T(8,128)(2,1)S(1)} async-done(((bf16[32,4,16,128]{3,2,1,0:T(8,128)(2,1)}), bf16[32,4,16,128]{3,2,1,0:T(8,128)(2,1)S(1)}, u32[]{:S(2)}, u32[]{:S(2)}) %all-to-all-start.2) | async-done | bytes 524320 | tf_op jit(solution)/shard_map/all_to_all | solution.py:380
  76.7 5.7 %all-to-all-start.3 = ((bf16[8,4,16,128]{3,2,1,0:T(8,128)(2,1)}), bf16[8,4,16,128]{3,2,1,0:T(8,128)(2,1)S(1)}, u32[]{:S(2)}, u32[]{:S(2)}) async-start(bf16[8,4,16,128]{3,2,1,0:T(8,128)(2,1)} %broadcast_in_dim.78), calls=%async_computation.3 | async-start | bytes 262144 | tf_op jit(solution)/shard_map/all_to_all | solution.py:320
  83.1 2.3 %copy-done = bf16[3072,768]{1,0:T(8,128)(2,1)S(1)} copy-done((bf16[3072,768]{1,0:T(8,128)(2,1)S(1)}, bf16[3072,768]{1,0:T(8,128)(2,1)}, u32[]{:S(2)}) %copy-start) | copy-done | bytes 4718616
  85.5 3.3 %mix_weights.1 = (bf16[2,2,256,768]{3,2,1,0:T(8,128)(2,1)S(1)}, f32[8,768]{1,0:T(8,128)S(1)}, bf16[3,128,128]{2,1,0:T(8,128)(2,1)S(1)}, f32[8,128]{1,0:T(8,128)S(1)}) custom-call(bf16[8,64]{1,0:T(8,128)(2,1)S(1)} %add_convert_fusion.member, bf16[64,6144]{1,0:T(8,128)(2,1)S(1)} %copy-done.2, bf16[64,3072]{1,0:T(8,128)(2,1)S(1)} %copy-done.3, ...), custom_call_target="tpu_custom_call" | custom-call | flops 1300000000 | bytes 6000000 | tf_op jit(solution)/shard_map/mix_weights/pallas_call | solution.py:209
  88.8 2.6 %all-to-all-done.3.tokens = bf16[8,4,16,128]{3,2,1,0:T(8,128)(2,1)S(1)} async-done(((bf16[8,4,16,128]{3,2,1,0:T(8,128)(2,1)}), bf16[8,4,16,128]{3,2,1,0:T(8,128)(2,1)S(1)}, u32[]{:S(2)}, u32[]{:S(2)}) %all-to-all-start.3) | async-done | bytes 131104 | tf_op jit(solution)/shard_map/all_to_all | solution.py:320
  91.4 6.2 %attend.1 = bf16[8,4,2,16,256]{4,3,2,1,0:T(8,128)(2,1)} custom-call(s32[1]{0:T(128)} %bitcast.lead, bf16[8,4,16,128]{3,2,1,0:T(8,128)(2,1)S(1)} %all-to-all-done.3.tokens, bf16[2,2,256,768]{3,2,1,0:T(8,128)(2,1)S(1)} %get-tuple-element.13.mix, f32[8,768]{1,0:T(8,128)S(1)} %get-tuple-element.14.rows, bf16[3,128,128]{2,1,0:T(8,128)(2,1)S(1)} %get-tuple-element.15.gram, ...), custom_call_target="tpu_custom_call" | custom-call | flops 1000000000 | bytes 3000000 | tf_op jit(solution)/shard_map/attend/pallas_call | solution.py:296
  (67 shorter events, 9.2 us)
Async XLA Ops:
  0.0 22.9 %copy-start.1 = (bf16[4,2,64,512]{3,2,1,0:T(8,128)(2,1)S(1)}, bf16[4,2,64,512]{3,2,1,0:T(8,128)(2,1)}, u32[]{:S(2)}) copy-start(bf16[4,2,64,512]{3,2,1,0:T(8,128)(2,1)} %main.1) | copy-start | bytes 1572868
  1.1 45.7 %collective-permute-start.1 = (bf16[4,64,512]{2,1,0:T(8,128)(2,1)S(1)}, bf16[4,64,512]{2,1,0:T(8,128)(2,1)S(1)}, u32[]{:S(2)}, u32[]{:S(2)}) collective-permute-start(bf16[4,64,512]{2,1,0:T(8,128)(2,1)S(1)} %get-tuple-element.20), channel_id=1, source_target_pairs={{0,1},{1,2},{2,3},{3,4},{4,5},{5,6},{6,7},{8,9},{9,10},{10,11},{11... | collective-permute-start | bytes 786440 | tf_op jit(solution)/shard_map/ppermute | solution.py:342
  5.5 41.3 %collective-permute-start.2 = (bf16[4,64,512]{2,1,0:T(8,128)(2,1)S(1)}, bf16[4,64,512]{2,1,0:T(8,128)(2,1)S(1)}, u32[]{:S(2)}, u32[]{:S(2)}) collective-permute-start(bf16[4,64,512]{2,1,0:T(8,128)(2,1)S(1)} %get-tuple-element.19), channel_id=1, source_target_pairs={{1,0},{2,1},{3,2},{4,3},{5,4},{6,5},{7,6},{9,8},{10,9},{11,10},{12... | collective-permute-start | bytes 786440 | tf_op jit(solution)/shard_map/ppermute | solution.py:342
  9.0 23.2 %copy-start.20 = (s32[64]{0:T(128)S(1)}, s32[64]{0:T(128)}, u32[]{:S(2)}) copy-start(s32[64]{0:T(128)} %param.15) | copy-start | bytes 772
  12.9 31.3 %copy-start.16 = (s32[64]{0:T(128)S(1)}, s32[64]{0:T(128)}, u32[]{:S(2)}) copy-start(s32[64]{0:T(128)} %param.16) | copy-start | bytes 772
  12.9 32.0 %copy-start.19 = (f32[16]{0:T(128)S(1)}, f32[16]{0:T(128)}, u32[]{:S(2)}) copy-start(f32[16]{0:T(128)} %param.20) | copy-start | bytes 196
  12.9 34.0 %copy-start.6 = (bf16[512,16]{0,1:T(8,128)(2,1)S(1)}, bf16[512,16]{0,1:T(8,128)(2,1)}, u32[]{:S(2)}) copy-start(bf16[512,16]{0,1:T(8,128)(2,1)} %param.19) | copy-start | bytes 49156
  12.9 20.1 %all-to-all-start = ((f32[8,16,512]{2,1,0:T(8,128)}), f32[8,16,512]{2,1,0:T(8,128)S(1)}, u32[]{:S(2)}, u32[]{:S(2)}) async-start(f32[8,16,512]{2,1,0:T(8,128)} %broadcast_in_dim.76), calls=%async_computation | async-start | bytes 524288 | tf_op jit(solution)/shard_map/all_to_all | solution.py:320
  22.9 23.3 %collective-permute-start.3 = (bf16[2,64,512]{2,1,0:T(8,128)(2,1)S(1)}, bf16[2,64,512]{2,1,0:T(8,128)(2,1)S(1)}, u32[]{:S(2)}, u32[]{:S(2)}) collective-permute-start(bf16[2,64,512]{2,1,0:T(8,128)(2,1)S(1)} %get-tuple-element.18), channel_id=1, source_target_pairs={{0,9},{1,10},{2,11},{3,12},{4,13},{5,14},{6,15},{8,17},{9,18},{10,... | collective-permute-start | bytes 393224 | tf_op jit(solution)/shard_map/ppermute | solution.py:342
  28.9 17.2 %collective-permute-start.4 = (bf16[2,64,512]{2,1,0:T(8,128)(2,1)S(1)}, bf16[2,64,512]{2,1,0:T(8,128)(2,1)S(1)}, u32[]{:S(2)}, u32[]{:S(2)}) collective-permute-start(bf16[2,64,512]{2,1,0:T(8,128)(2,1)S(1)} %get-tuple-element.17), channel_id=1, source_target_pairs={{1,8},{2,9},{3,10},{4,11},{5,12},{6,13},{7,14},{9,16},{10,17},{11,... | collective-permute-start | bytes 393224 | tf_op jit(solution)/shard_map/ppermute | solution.py:342
  30.3 16.6 %collective-permute-start = (bf16[2,2,64,512]{3,2,1,0:T(8,128)(2,1)S(1)}, bf16[2,2,64,512]{3,2,1,0:T(8,128)(2,1)S(1)}, u32[]{:S(2)}, u32[]{:S(2)}) collective-permute-start(bf16[2,2,64,512]{3,2,1,0:T(8,128)(2,1)S(1)} %slice.15), channel_id=1, source_target_pairs={{0,8},{1,9},{2,10},{3,11},{4,12},{5,13},{6,14},{7,15},{8,16},{9,17... | collective-permute-start | bytes 786440 | tf_op jit(solution)/shard_map/ppermute | solution.py:342
  33.9 21.8 %all-to-all-start.1 = ((bf16[32,16,512]{2,1,0:T(8,128)(2,1)}), bf16[32,16,512]{2,1,0:T(8,128)(2,1)S(1)}, u32[]{:S(2)}, u32[]{:S(2)}) async-start(bf16[32,16,512]{2,1,0:T(8,128)(2,1)} %broadcast_in_dim.77), calls=%async_computation.1 | async-start | bytes 1048576 | tf_op jit(solution)/shard_map/all_to_all | solution.py:320
  46.8 0.9 copy-start.5
  57.7 6.8 %copy-start.18 = (f32[768]{0:T(1024)S(1)}, f32[768]{0:T(1024)}, u32[]{:S(2)}) copy-start(f32[768]{0:T(1024)} %param.25) | copy-start | bytes 9220
  57.7 6.8 %copy-start.17 = (s32[64]{0:T(128)S(1)}, s32[64]{0:T(128)}, u32[]{:S(2)}) copy-start(s32[64]{0:T(128)} %param.16) | copy-start | bytes 772
  57.7 24.7 %copy-start.21 = (s32[64]{0:T(128)S(1)}, s32[64]{0:T(128)}, u32[]{:S(2)}) copy-start(s32[64]{0:T(128)} %param.15) | copy-start | bytes 772
  57.7 25.4 %copy-start.2 = (bf16[64,6144]{1,0:T(8,128)(2,1)S(1)}, bf16[64,6144]{1,0:T(8,128)(2,1)}, u32[]{:S(2)}) copy-start(bf16[64,6144]{1,0:T(8,128)(2,1)} %modulation.1) | copy-start | bytes 2359300
  57.7 25.4 %copy-start.3 = (bf16[64,3072]{1,0:T(8,128)(2,1)S(1)}, bf16[64,3072]{1,0:T(8,128)(2,1)}, u32[]{:S(2)}) copy-start(bf16[64,3072]{1,0:T(8,128)(2,1)} %embed.1) | copy-start | bytes 1179652
  57.7 25.4 %copy-start.10 = (f32[3072]{0:T(1024)S(1)}, f32[3072]{0:T(1024)}, u32[]{:S(2)}) copy-start(f32[3072]{0:T(1024)} %param.22) | copy-start | bytes 36868
  60.7 15.3 %all-to-all-start.2 = ((bf16[32,4,16,128]{3,2,1,0:T(8,128)(2,1)}), bf16[32,4,16,128]{3,2,1,0:T(8,128)(2,1)S(1)}, u32[]{:S(2)}, u32[]{:S(2)}) async-start(bf16[32,4,16,128]{3,2,1,0:T(8,128)(2,1)} %bitcast.13), calls=%async_computation.2 | async-start | bytes 1048576 | tf_op jit(solution)/shard_map/all_to_all | solution.py:380
  76.7 14.7 %all-to-all-start.3 = ((bf16[8,4,16,128]{3,2,1,0:T(8,128)(2,1)}), bf16[8,4,16,128]{3,2,1,0:T(8,128)(2,1)S(1)}, u32[]{:S(2)}, u32[]{:S(2)}) async-start(bf16[8,4,16,128]{3,2,1,0:T(8,128)(2,1)} %broadcast_in_dim.78), calls=%async_computation.3 | async-start | bytes 262144 | tf_op jit(solution)/shard_map/all_to_all | solution.py:320
  83.1 2.3 %copy-start = (bf16[3072,768]{1,0:T(8,128)(2,1)S(1)}, bf16[3072,768]{1,0:T(8,128)(2,1)}, u32[]{:S(2)}) copy-start(bf16[3072,768]{1,0:T(8,128)(2,1)} %qkv_w.1) | copy-start | bytes 14155780
  85.5 5.9 %copy-start.14 = (f32[128]{0:T(128)S(1)}, f32[128]{0:T(128)}, u32[]{:S(2)}) copy-start(f32[128]{0:T(128)} %param.26) | copy-start | bytes 1540
  85.5 5.9 %copy-start.15 = (f32[128]{0:T(128)S(1)}, f32[128]{0:T(128)}, u32[]{:S(2)}) copy-start(f32[128]{0:T(128)} %param.27) | copy-start | bytes 1540
  (7 other events, 4.7 us)

commit v2 on v1

v2 whole, which is shorter than its diff:
```python
import functools
import math

import jax
import jax.numpy as jnp
from jax import lax
from jax.experimental import pallas as pl
from jax.experimental.pallas import tpu as pltpu
from jax.sharding import PartitionSpec as P

latent_scale = 0.476986
norm_eps = 1e-06
f32 = jnp.float32
bf16 = jnp.bfloat16
MIB = 1024 * 1024
NT = (((1,), (1,)), ((), ()))


def dot(a, b, dims=(((1,), (0,)), ((), ()))):
    return lax.dot_general(a, b, dims, preferred_element_type=f32)


def split2(value):
    high = value.astype(bf16)
    return high, (value - high.astype(f32)).astype(bf16)


def iota(shape, dim):
    return lax.broadcasted_iota(jnp.int32, shape, dim)


def fold_kernel(weight, latent, out, tap_buf, lat_buf, sems):
    band = lax.axis_index("head")
    last = weight.shape[0] - 1
    base = lax.axis_index("seq") // 2 * 2
    copies = [
        pltpu.make_async_copy(weight.at[jnp.minimum(base, last)], tap_buf.at[0], sems.at[0]),
        pltpu.make_async_copy(weight.at[jnp.minimum(base + 1, last)], tap_buf.at[1], sems.at[1]),
        pltpu.make_async_copy(latent, lat_buf, sems.at[2]),
    ]
    for copy in copies:
        copy.start()
    copies[2].wait()
    own = jnp.where(iota((16, 512), 1) // 64 == band, lat_buf[...].astype(f32), 0.0)
    pair = own[:, 0:128] + own[:, 128:256] + own[:, 256:384] + own[:, 384:512]
    left = (pair[:, 0:64] + pair[:, 64:128]).astype(bf16)
    for tap in range(2):
        copies[tap].wait()
        out[tap * 16 : tap * 16 + 16, :] = dot(left, tap_buf[tap]).astype(bf16)


def fold_taps(weight, latent_rows):
    taps, outs, ins = weight.shape
    lats = latent_rows.shape[0]
    whole = pl.BlockSpec(memory_space=pl.ANY)
    return pl.pallas_call(
        fold_kernel,
        in_specs=[whole, whole],
        out_specs=pl.BlockSpec(memory_space=pltpu.VMEM),
        out_shape=jax.ShapeDtypeStruct((2 * lats, ins), bf16),
        scratch_shapes=[
            pltpu.VMEM((2, outs, ins), bf16),
            pltpu.VMEM((lats, ins), bf16),
            pltpu.SemaphoreType.DMA((3,)),
        ],
        compiler_params=pltpu.CompilerParams(vmem_limit_bytes=56 * MIB),
        cost_estimate=pl.CostEstimate(flops=10**6, bytes_accessed=150000, transcendentals=0),
        name="fold_taps",
    )(weight, latent_rows)


def prep_kernel(main, prev, lat, cbias, lbias, act, base):
    def silu(value):
        value = value.astype(f32)
        half = 0.5 * value
        return (half * jnp.tanh(half) + half).astype(bf16)

    for frame in range(6):
        rows = prev[frame] if frame < 2 else main[frame - 2]
        act[frame * 128 : frame * 128 + 128, :] = silu(rows.reshape(128, 512))
    weight = lat[...]
    const = jnp.sum(weight.astype(f32) * cbias[...], axis=1, keepdims=True) + lbias[...]
    for frame in range(4):
        own = main[frame].reshape(128, 512)
        base[:, frame * 128 : frame * 128 + 128] = dot(weight, own, NT) + const


def prepare(video, prev, lat, conv_bias, latent_bias):
    return pl.pallas_call(
        prep_kernel,
        out_shape=(
            jax.ShapeDtypeStruct((768, 512), bf16),
            jax.ShapeDtypeStruct((16, 512), f32),
        ),
        compiler_params=pltpu.CompilerParams(vmem_limit_bytes=8 * MIB),
        cost_estimate=pl.CostEstimate(flops=2 * 10**7, bytes_accessed=3 * 10**6, transcendentals=800000),
        name="prepare",
    )(video, prev, lat, conv_bias.reshape(1, -1), latent_bias.reshape(-1, 1))


def conv_kernel(table, act, near, far1, far2, far3, base, own, first, second, weight, taps):
    even = lax.axis_index("head") % 2 == 0
    chip = lax.axis_index("seq") // 2
    for high, group in enumerate((near, far1, far2, far3)):
        for low in range(4):
            at = pl.multiple_of((chip ^ (high * 4 + low)) * 32, 32)
            weight[pl.ds(at, 32), :] = group[low]
    for frame in range(6):
        taps[frame] = dot(weight[0:432, :], act[frame * 128 : frame * 128 + 128, :], NT)
    column = iota((16, 128), 1) % 64

    def across(parts):
        left = jnp.where(column == 0, 0.0, pltpu.roll(parts[0], 1, 1))
        right = jnp.where(column == 63, 0.0, pltpu.roll(parts[2], 127, 1))
        return parts[1] + left + right

    upper = iota((16, 128), 1) < 64
    for frame in range(4):
        total = None
        for delay in range(3):
            part = taps[table[frame * 3 + delay], delay * 144 : delay * 144 + 144, :]
            total = part if total is None else total + part
        step = [
            across([total[(a * 3 + col) * 16 : (a * 3 + col) * 16 + 16] for col in range(3)])
            for a in range(3)
        ]
        from_above = jnp.where(upper, 0.0, pltpu.roll(step[0], 64, 1))
        from_below = jnp.where(upper, pltpu.roll(step[2], 64, 1), 0.0)
        here = slice(frame * 128, frame * 128 + 128)
        own[:, here] = base[:, here] + step[1] + from_above + from_below
        half = slice(frame * 64, frame * 64 + 64)
        above, below = step[2][:, 0:64], step[0][:, 64:128]
        first[:, half] = jnp.where(even, below, above)
        second[:, half] = jnp.where(even, above, below)


def convolve(table, act, folded, base):
    smem = pl.BlockSpec(memory_space=pltpu.SMEM)
    vmem = pl.BlockSpec(memory_space=pltpu.VMEM)
    return pl.pallas_call(
        conv_kernel,
        in_specs=[smem] + [vmem] * 6,
        out_specs=(vmem, vmem, vmem),
        out_shape=(
            jax.ShapeDtypeStruct((16, 512), f32),
            jax.ShapeDtypeStruct((16, 256), f32),
            jax.ShapeDtypeStruct((16, 256), f32),
        ),
        scratch_shapes=[pltpu.VMEM((512, 512), bf16), pltpu.VMEM((6, 432, 128), f32)],
        compiler_params=pltpu.CompilerParams(vmem_limit_bytes=10 * MIB),
        cost_estimate=pl.CostEstimate(flops=4 * 10**8, bytes_accessed=2 * 10**6, transcendentals=0),
        name="convolve",
    )(table, act, *folded, base)


def finish_kernel(own, first, second, out):
    even = lax.axis_index("head") % 2 == 0
    lane = iota((16, 128), 1)
    row = iota((128, 128), 0)
    pos = iota((128, 128), 1)
    own_half = (pos % 64) // 32 == row // 64
    own_cell = (pos // 64) * 2 + pos % 2 == row % 4
    keep = own_half & own_cell
    repeat = (iota((128, 16), 0) % 64 // 4 == iota((128, 16), 1)).astype(bf16)
    pick = ((lane % 32) // 2 == iota((16, 128), 0)).astype(bf16)
    for frame in range(4):
        half = slice(frame * 64, frame * 64 + 64)
        one, two = first[:, half], second[:, half]
        edge = jnp.concatenate([jnp.where(even, two, one), jnp.where(even, one, two)], axis=1)
        latent = ((own[:, frame * 128 : frame * 128 + 128] + edge) * latent_scale).astype(bf16)
        wide = jnp.where(keep, dot(repeat, latent), 0.0).astype(bf16)
        out[frame] = dot(pick, wide, NT).astype(bf16)


def finish(own, first, second):
    vmem = pl.BlockSpec(memory_space=pltpu.VMEM)
    return pl.pallas_call(
        finish_kernel,
        in_specs=[vmem, vmem, vmem],
        out_specs=vmem,
        out_shape=jax.ShapeDtypeStruct((4, 16, 128), bf16),
        compiler_params=pltpu.CompilerParams(vmem_limit_bytes=6 * MIB),
        cost_estimate=pl.CostEstimate(flops=10**7, bytes_accessed=10**6, transcendentals=0),
        name="finish",
    )(own, first, second)


def route_kernel(table, near, far1, far2, far3, mine, other, frames):
    seq = lax.axis_index("seq")
    chip, core = seq // 2, seq % 2
    for high, group in enumerate((near, far1, far2, far3)):
        for low in range(4):
            frames[high * 4 + low] = group[low]
    for out, owner in ((mine, core), (other, 1 - core)):
        for slot in range(4):
            frame = table[12 + owner * 4 + slot]
            here = (frame // 4) % 2 == core
            piece = frames[(frame // 8) ^ chip, frame % 4]
            out[slot] = jnp.where(here, piece, jnp.zeros_like(piece))


def route(table, groups):
    smem = pl.BlockSpec(memory_space=pltpu.SMEM)
    vmem = pl.BlockSpec(memory_space=pltpu.VMEM)
    shape = jax.ShapeDtypeStruct((4, 16, 128), bf16)
    return pl.pallas_call(
        route_kernel,
        in_specs=[smem] + [vmem] * 4,
        out_specs=(vmem, vmem),
        out_shape=(shape, shape),
        scratch_shapes=[pltpu.VMEM((16, 4, 16, 128), bf16)],
        compiler_params=pltpu.CompilerParams(vmem_limit_bytes=4 * MIB),
        cost_estimate=pl.CostEstimate(flops=1, bytes_accessed=10**6, transcendentals=0),
        name="route",
    )(table, *groups)


def scale_kernel(member, modulation, embed, bias, left, gram, gvec):
    width = embed.shape[1]
    chunk = 512
    mean = jnp.sum(embed[...].astype(f32), axis=1, keepdims=True) / width
    bias_mean = jnp.sum(bias[...], axis=1, keepdims=True) / width
    whole = jnp.zeros((80, 80), f32)
    for at in range(0, width, chunk):
        here = slice(at, at + chunk)
        centred = embed[:, here].astype(f32) - mean
        cbias = bias[:, here] - bias_mean
        scale = 1.0 + dot(member[...], modulation[:, width + at : width + at + chunk])
        shift = dot(member[...], modulation[:, here])
        first, second = scale[0:1], scale[1:2]
        high, low = split2(centred * first)
        left[0:64, here] = high
        left[64:128, here] = low
        high, low = split2(centred * second)
        left[128:192, here] = high
        left[192:256, here] = low
        high, low = split2(jnp.concatenate([cbias * first, cbias * second], axis=0))
        left[256:272, here] = jnp.concatenate(
            [high.astype(f32), low.astype(f32), shift[0:2], jnp.zeros((10, chunk), f32)], axis=0
        ).astype(bf16)
        full = jnp.concatenate([centred, cbias, jnp.zeros((15, chunk), f32)], axis=0)
        high, low = split2(full)
        whole = whole + (dot(high, high, NT) + dot(high, low, NT) + dot(low, high, NT))
    whole = whole * (1.0 / width)
    square = whole[0:64, 0:64]
    blank = jnp.zeros((64, 64), f32)
    block = jnp.concatenate(
        [jnp.concatenate([square, blank], axis=1), jnp.concatenate([blank, square], axis=1)], axis=0
    )
    top = block.astype(bf16)
    rest = block - top.astype(f32)
    mid = rest.astype(bf16)
    gram[0] = top
    gram[1] = mid
    gram[2] = (rest - mid.astype(f32)).astype(bf16)
    cross = 2.0 * whole[64:65, 0:64]
    const = jnp.broadcast_to(whole[64:65, 64:65], (1, 128))
    gvec[...] = jnp.concatenate(
        [jnp.concatenate([cross, cross], axis=1), const, jnp.zeros((6, 128), f32)], axis=0
    )


def scale_embedding(member, modulation, embed_weight, embed_bias):
    width = embed_weight.shape[1]
    vmem = pl.BlockSpec(memory_space=pltpu.VMEM)
    return pl.pallas_call(
        scale_kernel,
        in_specs=[vmem] * 4,
        out_specs=[vmem] * 3,
        out_shape=[
            jax.ShapeDtypeStruct((272, width), bf16),
            jax.ShapeDtypeStruct((3, 128, 128), bf16),
            jax.ShapeDtypeStruct((8, 128), f32),
        ],
        compiler_params=pltpu.CompilerParams(vmem_limit_bytes=8 * MIB),
        cost_estimate=pl.CostEstimate(flops=10**8, bytes_accessed=3 * 10**6, transcendentals=0),
        name="scale_embedding",
    )(member, modulation, embed_weight, embed_bias.reshape(1, -1))


def mix_kernel(left, qkv_w, qkv_b, mix, rows):
    product = dot(left[...], qkv_w[...])
    cols = product.shape[1]
    empty = jnp.zeros((64, cols), bf16)
    for clip in range(2):
        at = clip * 128
        high, low = split2(product[at : at + 64] + product[at + 64 : at + 128])
        mix[clip, 0] = jnp.concatenate([high, empty, low, empty], axis=0)
        mix[clip, 1] = jnp.concatenate([empty, high, empty, low], axis=0)
    tail = product[256:272]
    rows[...] = jnp.concatenate(
        [tail[0:2] + tail[2:4], tail[4:6] + qkv_b[...], jnp.zeros((4, cols), f32)], axis=0
    )


def mix_weights(left, qkv_weight, qkv_bias):
    width = left.shape[1]
    cols = 256
    return pl.pallas_call(
        mix_kernel,
        grid=(qkv_weight.shape[1] // cols,),
        in_specs=[
            pl.BlockSpec(left.shape, lambda n: (0, 0)),
            pl.BlockSpec((width, cols), lambda n: (0, n)),
            pl.BlockSpec((1, cols), lambda n: (0, n)),
        ],
        out_specs=[
            pl.BlockSpec((2, 2, 256, cols), lambda n: (0, 0, 0, n)),
            pl.BlockSpec((8, cols), lambda n: (0, n)),
        ],
        out_shape=[
            jax.ShapeDtypeStruct((2, 2, 256, 768), bf16),
            jax.ShapeDtypeStruct((8, 768), f32),
        ],
        compiler_params=pltpu.CompilerParams(vmem_limit_bytes=12 * MIB),
        cost_estimate=pl.CostEstimate(flops=13 * 10**8, bytes_accessed=6 * 10**6, transcendentals=0),
        name="mix_weights",
    )(left, qkv_weight, qkv_bias.reshape(1, -1))


def project(lead, own, mix, rows, gram, gvec, q_gain, k_gain, write):
    factor = math.log2(math.e) / math.sqrt(128)
    gains = q_gain[...] * factor, k_gain[...]
    count = own.shape[0]
    later = iota((count, 1), 0) // 16 % 4 >= lead
    twice = jnp.concatenate([own, own], axis=1)
    spread = dot(own, gram[0]) + dot(own, gram[1]) + dot(own, gram[2])
    terms = (spread + gvec[0:1, :]) * own.astype(f32)
    low_lane = iota((count, 128), 1) < 64
    slope = jnp.where(later, rows[1:2, :], rows[0:1, :])
    offset = jnp.where(later, rows[3:4, :], rows[2:3, :])
    for half in range(2):
        mine = jnp.where(low_lane == (half == 0), terms, 0.0)
        variance = jnp.sum(mine, axis=1, keepdims=True) + gvec[1:2, 0:1]
        scale = lax.rsqrt(jnp.maximum(variance, 0.0) + norm_eps)
        mixed = jnp.where(later, dot(twice, mix[1, half]), dot(twice, mix[0, half]))
        qkv = scale * (mixed + slope) + offset
        for head in range(2):
            at = head * 384
            for kind in range(2):
                part = qkv[:, at + kind * 128 : at + kind * 128 + 128]
                norm = lax.rsqrt(jnp.mean(part * part, axis=1, keepdims=True) + norm_eps)
                write(kind, head, half, (part * norm * gains[kind]).astype(bf16))
            write(2, head, half, qkv[:, at + 256 : at + 384].astype(bf16))


def project_kernel(table, tokens, mix, rows, gram, gvec, q_gain, k_gain, out):
    bands = tokens.shape[0]

    def write(kind, head, half, value):
        for band in range(bands):
            for frame in range(4):
                at = (half * bands + band) * 16
                out[kind, head, frame, at : at + 16, :] = value[
                    (band * 4 + frame) * 16 : (band * 4 + frame) * 16 + 16
                ]

    own = tokens[...].reshape(bands * 64, 128)
    project(table[20], own, mix, rows, gram, gvec, q_gain, k_gain, write)


def project_near(table, tokens, mix, rows, gram, gvec, q_gain, k_gain):
    smem = pl.BlockSpec(memory_space=pltpu.SMEM)
    vmem = pl.BlockSpec(memory_space=pltpu.VMEM)
    return pl.pallas_call(
        project_kernel,
        in_specs=[smem] + [vmem] * 7,
        out_specs=vmem,
        out_shape=jax.ShapeDtypeStruct((3, 2, 4, 128, 128), bf16),
        compiler_params=pltpu.CompilerParams(vmem_limit_bytes=10 * MIB),
        cost_estimate=pl.CostEstimate(flops=2 * 10**8, bytes_accessed=2 * 10**6, transcendentals=0),
        name="project_near",
    )(table, tokens, mix, rows, gram, gvec, q_gain, k_gain)


def attend_kernel(
    table, near, far, mix, rows, gram, gvec, q_gain, k_gain, out, parts
):
    lead = table[20]
    own_band = lax.axis_index("head")
    for kind in range(3):
        for head in range(2):
            for frame in range(4):
                parts[kind, head, frame * 256 : frame * 256 + 128, :] = near[kind, head, frame]

    def write(kind, head, half, value):
        for band in range(4):
            for frame in range(4):
                at = frame * 256 + 128 + (half * 4 + band) * 16
                parts[kind, head, at : at + 16, :] = value[
                    (band * 4 + frame) * 16 : (band * 4 + frame) * 16 + 16
                ]

    own = far[...].reshape(256, 128)
    project(lead, own, mix, rows, gram, gvec, q_gain, k_gain, write)

    def group(begin, end):
        for head in range(2):
            key = parts[1, head, begin * 256 : end * 256, :]
            value = parts[2, head, begin * 256 : end * 256, :]
            for frame in range(begin, end):
                score = dot(parts[0, head, frame * 256 : frame * 256 + 256, :], key, NT)
                top = jnp.max(score, axis=1, keepdims=True)
                expo = jnp.exp2(score - top)
                total = jnp.sum(expo, axis=1, keepdims=True)
                result = (dot(expo.astype(bf16), value) / total).astype(bf16)
                lanes = slice(head * 128, head * 128 + 128)
                for half in range(2):
                    for place in range(8):
                        at = place // 4 * 128 + (half * 4 + place % 4) * 16
                        out[own_band ^ place, frame, half, :, lanes] = result[at : at + 16]

    for first in (1, 2, 3):

        @pl.when(lead == first)
        def _(first=first):
            group(0, first)
            group(first, 4)


def attend(table, near, far, mix, rows, gram, gvec, q_gain, k_gain):
    smem = pl.BlockSpec(memory_space=pltpu.SMEM)
    vmem = pl.BlockSpec(memory_space=pltpu.VMEM)
    return pl.pallas_call(
        attend_kernel,
        in_specs=[smem] + [vmem] * 8,
        out_specs=vmem,
        out_shape=jax.ShapeDtypeStruct((8, 4, 2, 16, 256), bf16),
        scratch_shapes=[pltpu.VMEM((3, 2, 1024, 128), bf16)],
        compiler_params=pltpu.CompilerParams(vmem_limit_bytes=14 * MIB),
        cost_estimate=pl.CostEstimate(flops=10**9, bytes_accessed=3 * 10**6, transcendentals=1300000),
        name="attend",
    )(table, near, far, mix, rows, gram, gvec, q_gain, k_gain)


def neighbour(value, axis, step):
    count = lax.axis_size(axis)
    pairs = [(i, i + step) for i in range(count) if 0 <= i + step < count]
    return lax.ppermute(value, axis, pairs)


def swap(value, axis, mask):
    return lax.ppermute(value, axis, [(i, i ^ mask) for i in range(lax.axis_size(axis))])


def swap_pairs(value, axis, begin):
    pairs = [(i, i + 1) for i in range(begin, lax.axis_size(axis) - 1, 2)]
    return lax.ppermute(value, axis, pairs + [(b, a) for a, b in pairs])


def swap3(value, axis, unit):
    return [value] + [swap(value, axis, unit * step) for step in (3, 2, 1)][::-1]


def gather_chips(value):
    row = jnp.stack(swap3(value, "seq", 2))
    return swap3(row, "seq", 8)


def per_device(
    video_feat,
    clip_frames,
    clip_offset,
    conv_weight,
    conv_bias,
    latent_weight,
    latent_bias,
    embed_weight,
    embed_bias,
    modulation,
    qkv_weight,
    qkv_bias,
    q_gain,
    k_gain,
):
    seqs, heads = lax.axis_size("seq"), lax.axis_size("head")
    seq = lax.axis_index("seq")
    frames = video_feat.shape[0]
    latent_rows = latent_weight.T

    weight = conv_weight.transpose(0, 1, 2, 4, 3).reshape(27, conv_weight.shape[4], -1)
    part = fold_taps(weight, latent_rows)
    prev = neighbour(video_feat[2:], "seq", 1)
    add = lambda values: sum(value.astype(f32) for value in values).astype(bf16)
    four = add(swap3(part, "head", 1))
    taps = add([four, swap(four, "head", 4)])

    count = clip_frames.shape[0]
    numbers = jnp.arange(count, dtype=jnp.int32)
    starts = jnp.sum(jnp.where(numbers[None, :] < numbers[:, None], clip_frames[None, :], 0), axis=1)
    ids = seq * frames + jnp.arange(frames, dtype=jnp.int32)
    first = jnp.max(jnp.where(starts[None, :] <= ids[:, None], starts[None, :], 0), axis=1)
    slot = seq // 2 * 2 * frames + jnp.arange(2 * frames, dtype=jnp.int32)
    inside = (clip_offset[None, :] <= slot[:, None]) & (
        slot[:, None] < (clip_offset + clip_frames)[None, :]
    )
    origin = jnp.sum(jnp.where(inside, (starts - clip_offset)[None, :] + slot[:, None], 0), axis=1)
    origin = jnp.clip(origin, 0, seqs * frames - 1)
    delays = jnp.arange(3, dtype=jnp.int32)
    source = jnp.maximum(ids[:, None] - 2 + delays[None, :], first[:, None]) - seq * frames + 2
    source = jnp.clip(source, 0, frames + 1).reshape(-1)
    leading = clip_offset == seq * frames
    lead = jnp.sum(jnp.where(leading, clip_frames, 0)).reshape(1)
    table = jnp.concatenate([source, origin, lead])
    trailing = (clip_offset > seq * frames) & (clip_offset < (seq + 1) * frames)
    member = jnp.concatenate(
        [leading[None], trailing[None], jnp.zeros((6, count), jnp.bool_)], axis=0
    ).astype(bf16)

    left, gram, gvec = scale_embedding(member, modulation, embed_weight, embed_bias)

    taps, table, prev = lax.optimization_barrier((taps, table, prev))
    row = jnp.stack(swap3(taps, "seq", 2))
    folded = swap3(row, "seq", 8)
    mix, rows = mix_weights(left, qkv_weight, qkv_bias)
    mixed = mix, rows, gram, gvec
    act, base = prepare(video_feat, prev, latent_rows, conv_bias, latent_bias)

    own, first, second = convolve(table, act, folded, base)
    first = swap_pairs(first, "head", 0)
    second = swap_pairs(second, "head", 1)
    pieces = finish(own, first, second)

    mine, other = route(table, gather_chips(pieces))
    mine, other, mixed = lax.optimization_barrier((mine, other, mixed))
    slots = mine + swap(other, "seq", 1)
    near = jnp.stack(swap3(slots, "head", 1))
    far = swap(near, "head", 4)
    gains = q_gain.reshape(1, -1), k_gain.reshape(1, -1)
    ready = project_near(table, near, *mixed, *gains)
    out = attend(table, ready, far, *mixed, *gains)
    return out.reshape(heads * frames * 32, 256)


def solution(mesh):
    placed = (
        P("seq", "head", None, None),
        P(),
        P(),
        P(None, None, None, None, "head"),
        P(),
        P(),
        P(),
        P(),
        P(),
        P(),
        P(None, "head"),
        P("head"),
        P(),
        P(),
    )
    return jax.shard_map(
        per_device, mesh=mesh, in_specs=placed, out_specs=P("seq", "head"), check_vma=False
    )
```

time: 98.8 us -> 87.4 us (0.88)
  the two profiles are of different devices: /device:TPU:1 before, /device:TPU:8 now
where the time goes in v2:
time: 87.4 us; the launch traced here: 86.9 us
  starting transfers between devices  41.8 us (48%)
  waiting for transfers between devices  24.1 us (28%)
  Pallas kernels  15.1 us (17%)
  other arithmetic  2.9 us (3%)
  local copies, waits for them, and re-layouts  2.66 us (3%)
    ppermute x21, starting transfers between devices, swap(): lax.ppermute(value, axis, [(i, i ^ mask) for i in range(lax.axis_size(axi...  39 us
    ppermute x21, waiting for transfers between devices, swap(): lax.ppermute(value, axis, [(i, i ^ mask) for i in range(lax.axis_size(axi...  21.3 us
    pallas_call x1, Pallas kernels, attend(): pl.pallas_call(attend_kernel, in_specs=[smem] + [vmem] * 8, out_specs=vme...  5.2 us
    ppermute x2, waiting for transfers between devices, swap_pairs(): return lax.ppermute(value, axis, pairs + [(b, a) for a, b in pairs])  2.76 us
    unnamed x26, local copies, waits for them, and re-layouts  2.39 us
    pallas_call x1, Pallas kernels, mix_weights(): pl.pallas_call(mix_kernel, grid=(qkv_weight.shape[1] // cols,), in_specs=...  2.26 us
    ppermute x1, starting transfers between devices, neighbour(): return lax.ppermute(value, axis, pairs)  1.92 us
    pallas_call x1, Pallas kernels, fold_taps(): pl.pallas_call(fold_kernel, in_specs=[whole, whole], out_specs=pl.BlockSp...  1.82 us
  transfers between devices with their start and end apart: 24, of which 12 were waited for; matrix products, arithmetic and copies ran while one was open for 4% of the time, Pallas kernels for 6%

profile of v2, /device:TPU:8, one launch (start us, length us, event | category | flops | bytes accessed | tf_op | source)
XLA Modules:
  0.0 86.9 jit_solution(5634923866037467631)
XLA Ops:
  0.0 1.8 %fold_taps.1 = bf16[32,512]{1,0:T(8,128)(2,1)} custom-call(bf16[27,64,512]{2,1,0:T(8,128)(2,1)} %bitcast.36, bf16[16,512]{1,0:T(8,128)(2,1)} %bitcast.28), custom_call_target="tpu_custom_call" | custom-call | flops 1000000 | bytes 150000 | tf_op jit(solution)/shard_map/fold_taps/pallas_call | solution.py:56
  1.9 4.7 %collective-permute-start.2 = (bf16[32,512]{1,0:T(8,128)(2,1)}, bf16[32,512]{1,0:T(8,128)(2,1)S(1)}, u32[]{:S(2)}, u32[]{:S(2)}) collective-permute-start(bf16[32,512]{1,0:T(8,128)(2,1)} %fold_taps.1), channel_id=1, source_target_pairs={{0,3},{1,2},{2,1},{3,0},{4,7},{5,6},{6,5},{7,4},{8,11},{9,10},{10,... | collective-permute-start | bytes 98312 | tf_op jit(solution)/shard_map/ppermute | solution.py:443
  7.3 1.9 %collective-permute-start.4 = (bf16[2,2,64,512]{3,2,1,0:T(8,128)(2,1)S(1)}, bf16[2,2,64,512]{3,2,1,0:T(8,128)(2,1)S(1)}, u32[]{:S(2)}, u32[]{:S(2)}) collective-permute-start(bf16[2,2,64,512]{3,2,1,0:T(8,128)(2,1)S(1)} %slice.3), channel_id=1, source_target_pairs={{0,8},{8,16},{16,24},{24,32},{32,40},{40,48},{48,56},{56,64},{64,7... | collective-permute-start | bytes 786440 | tf_op jit(solution)/shard_map/ppermute | solution.py:439
  12.4 5.4 %collective-permute-start.3 = (bf16[32,512]{1,0:T(8,128)(2,1)S(1)}, bf16[32,512]{1,0:T(8,128)(2,1)S(1)}, u32[]{:S(2)}, u32[]{:S(2)}) collective-permute-start(bf16[32,512]{1,0:T(8,128)(2,1)S(1)} %add_convert_fusion.1), channel_id=1, source_target_pairs={{0,4},{1,5},{2,6},{3,7},{4,0},{5,1},{6,2},{7,3},{8,12},{9,13},{10,... | collective-permute-start | bytes 98312 | tf_op jit(solution)/shard_map/ppermute | solution.py:443
  18.5 1.9 %collective-permute-done.3 = bf16[32,512]{1,0:T(8,128)(2,1)S(1)} collective-permute-done((bf16[32,512]{1,0:T(8,128)(2,1)S(1)}, bf16[32,512]{1,0:T(8,128)(2,1)S(1)}, u32[]{:S(2)}, u32[]{:S(2)}) %collective-permute-start.3) | collective-permute-done | bytes 32800 | tf_op jit(solution)/shard_map/ppermute | solution.py:443
  20.5 1.9 %collective-permute-start.7 = (bf16[32,512]{1,0:T(8,128)(2,1)S(1)}, bf16[32,512]{1,0:T(8,128)(2,1)S(1)}, u32[]{:S(2)}, u32[]{:S(2)}) collective-permute-start(bf16[32,512]{1,0:T(8,128)(2,1)S(1)} %add_convert_fusion), channel_id=1, source_target_pairs={{0,48},{8,56},{16,32},{24,40},{32,16},{40,24},{48,0},{56,8},{64,11... | collective-permute-start | bytes 98312 | tf_op jit(solution)/shard_map/ppermute | solution.py:443
  23.2 1.4 %collective-permute-start.5 = (bf16[32,512]{1,0:T(8,128)(2,1)S(1)}, bf16[32,512]{1,0:T(8,128)(2,1)S(1)}, u32[]{:S(2)}, u32[]{:S(2)}) collective-permute-start(bf16[32,512]{1,0:T(8,128)(2,1)S(1)} %add_convert_fusion), channel_id=1, source_target_pairs={{0,16},{8,24},{16,0},{24,8},{32,48},{40,56},{48,32},{56,40},{64,80... | collective-permute-start | bytes 98312 | tf_op jit(solution)/shard_map/ppermute | solution.py:443
  24.7 3.2 %collective-permute-done.6 = bf16[32,512]{1,0:T(8,128)(2,1)S(1)} collective-permute-done((bf16[32,512]{1,0:T(8,128)(2,1)S(1)}, bf16[32,512]{1,0:T(8,128)(2,1)S(1)}, u32[]{:S(2)}, u32[]{:S(2)}) %collective-permute-start.6) | collective-permute-done | bytes 32800 | tf_op jit(solution)/shard_map/ppermute | solution.py:443
  27.9 2.7 %collective-permute-start.10 = (bf16[4,32,512]{2,1,0:T(8,128)(2,1)S(1)}, bf16[4,32,512]{2,1,0:T(8,128)(2,1)S(1)}, u32[]{:S(2)}, u32[]{:S(2)}) collective-permute-start(bf16[4,32,512]{2,1,0:T(8,128)(2,1)S(1)} %pad_maximum_fusion.near), channel_id=1, source_target_pairs={{0,192},{8,200},{16,208},{24,216},{32,224},{40,232},{48,240},{56,2... | collective-permute-start | bytes 393224 | tf_op jit(solution)/shard_map/ppermute | solution.py:443
  32.6 2.9 %collective-permute-done.10.far3 = bf16[4,32,512]{2,1,0:T(8,128)(2,1)S(1)} collective-permute-done((bf16[4,32,512]{2,1,0:T(8,128)(2,1)S(1)}, bf16[4,32,512]{2,1,0:T(8,128)(2,1)S(1)}, u32[]{:S(2)}, u32[]{:S(2)}) %collective-permute-start.10) | collective-permute-done | bytes 131104 | tf_op jit(solution)/shard_map/ppermute | solution.py:443
  35.6 1.8 %collective-permute-done.9.far2 = bf16[4,32,512]{2,1,0:T(8,128)(2,1)S(1)} collective-permute-done((bf16[4,32,512]{2,1,0:T(8,128)(2,1)S(1)}, bf16[4,32,512]{2,1,0:T(8,128)(2,1)S(1)}, u32[]{:S(2)}, u32[]{:S(2)}) %collective-permute-start.9) | collective-permute-done | bytes 131104 | tf_op jit(solution)/shard_map/ppermute | solution.py:443
  37.4 1.6 %convolve.1 = (f32[16,512]{1,0:T(8,128)S(1)}, f32[16,256]{1,0:T(8,128)S(1)}, f32[16,256]{1,0:T(8,128)S(1)}) custom-call(s32[21]{0:T(128)S(1)} %pad_add_fusion.table, bf16[768,512]{1,0:T(8,128)(2,1)S(1)} %get-tuple-element.28.act, bf16[4,32,512]{2,1,0:T(8,128)(2,1)S(1)} %pad_maximum_fusion.near, bf16[4,32,512]{2,1,0:T(8,128)(2,1)S(1)} %collective-permute-done.8.far1, ...), custom_call_target="tpu_custom_call" | custom-call | flops 400000000 | bytes 2000000 | tf_op jit(solution)/shard_map/convolve/pallas_call | solution.py:140
  40.1 2.8 %collective-permute-done.11.first = f32[16,256]{1,0:T(8,128)S(1)} collective-permute-done((f32[16,256]{1,0:T(8,128)S(1)}, f32[16,256]{1,0:T(8,128)S(1)}, u32[]{:S(2)}, u32[]{:S(2)}) %collective-permute-start.11) | collective-permute-done | bytes 16416 | tf_op jit(solution)/shard_map/ppermute | solution.py:448
  43.3 1.3 %collective-permute-start.15 = (bf16[4,16,128]{2,1,0:T(8,128)(2,1)S(1)}, bf16[4,16,128]{2,1,0:T(8,128)(2,1)S(1)}, u32[]{:S(2)}, u32[]{:S(2)}) collective-permute-start(bf16[4,16,128]{2,1,0:T(8,128)(2,1)S(1)} %finish.1), channel_id=1, source_target_pairs={{0,48},{8,56},{16,32},{24,40},{32,16},{40,24},{48,0},{56,8},{64,11... | collective-permute-start | bytes 49160 | tf_op jit(solution)/shard_map/ppermute | solution.py:443
  44.6 2.1 %collective-permute-start.14 = (bf16[4,16,128]{2,1,0:T(8,128)(2,1)S(1)}, bf16[4,16,128]{2,1,0:T(8,128)(2,1)S(1)}, u32[]{:S(2)}, u32[]{:S(2)}) collective-permute-start(bf16[4,16,128]{2,1,0:T(8,128)(2,1)S(1)} %finish.1), channel_id=1, source_target_pairs={{0,32},{8,40},{16,48},{24,56},{32,0},{40,8},{48,16},{56,24},{64,96... | collective-permute-start | bytes 49160 | tf_op jit(solution)/shard_map/ppermute | solution.py:443
  50.5 2.1 %collective-permute-start.18 = (bf16[4,4,16,128]{3,2,1,0:T(8,128)(2,1)S(1)}, bf16[4,4,16,128]{3,2,1,0:T(8,128)(2,1)S(1)}, u32[]{:S(2)}, u32[]{:S(2)}) collective-permute-start(bf16[4,4,16,128]{3,2,1,0:T(8,128)(2,1)S(1)} %pad_maximum_fusion.1.near), channel_id=1, source_target_pairs={{0,192},{8,200},{16,208},{24,216},{32,224},{40,232},{48,240},{56,2... | collective-permute-start | bytes 196616 | tf_op jit(solution)/shard_map/ppermute | solution.py:443
  54.7 2.3 %copy-done = bf16[3072,768]{1,0:T(8,128)(2,1)S(1)} copy-done((bf16[3072,768]{1,0:T(8,128)(2,1)S(1)}, bf16[3072,768]{1,0:T(8,128)(2,1)}, u32[]{:S(2)}) %copy-start) | copy-done | bytes 4718616
  57.0 2.3 %mix_weights.1 = (bf16[2,2,256,768]{3,2,1,0:T(8,128)(2,1)S(1)}, f32[8,768]{1,0:T(8,128)S(1)}) custom-call(bf16[272,3072]{1,0:T(8,128)(2,1)S(1)} %get-tuple-element.36.left, bf16[3072,768]{1,0:T(8,128)(2,1)S(1)} %copy-done, f32[1,768]{1,0:T(1,128)S(1)} %reshape.60.qkv_b), custom_call_target="tpu_custom_call" | custom-call | flops 1300000000 | bytes 6000000 | tf_op jit(solution)/shard_map/mix_weights/pallas_call | solution.py:299
  61.3 7.4 %collective-permute-start.22 = (bf16[4,16,128]{2,1,0:T(8,128)(2,1)S(1)}, bf16[4,16,128]{2,1,0:T(8,128)(2,1)S(1)}, u32[]{:S(2)}, u32[]{:S(2)}) collective-permute-start(bf16[4,16,128]{2,1,0:T(8,128)(2,1)S(1)} %add.101), channel_id=1, source_target_pairs={{0,3},{1,2},{2,1},{3,0},{4,7},{5,6},{6,5},{7,4},{8,11},{9,10},{10,... | collective-permute-start | bytes 49160 | tf_op jit(solution)/shard_map/ppermute | solution.py:443
  70.4 2.9 %collective-permute-done.21 = bf16[4,16,128]{2,1,0:T(8,128)(2,1)S(1)} collective-permute-done((bf16[4,16,128]{2,1,0:T(8,128)(2,1)S(1)}, bf16[4,16,128]{2,1,0:T(8,128)(2,1)S(1)}, u32[]{:S(2)}, u32[]{:S(2)}) %collective-permute-start.21) | collective-permute-done | bytes 16416 | tf_op jit(solution)/shard_map/ppermute | solution.py:443
  73.3 3.4 %collective-permute-start.23 = (bf16[4,4,16,128]{3,2,1,0:T(8,128)(2,1)S(1)}, bf16[4,4,16,128]{3,2,1,0:T(8,128)(2,1)S(1)}, u32[]{:S(2)}, u32[]{:S(2)}) collective-permute-start(bf16[4,4,16,128]{3,2,1,0:T(8,128)(2,1)S(1)} %pad_maximum_fusion.2.tokens), channel_id=1, source_target_pairs={{0,4},{1,5},{2,6},{3,7},{4,0},{5,1},{6,2},{7,3},{8,12},{9,13},{10,... | collective-permute-start | bytes 196616 | tf_op jit(solution)/shard_map/ppermute | solution.py:443
  76.7 1.6 %project_near.1.near = bf16[3,2,4,128,128]{4,3,2,1,0:T(8,128)(2,1)S(1)} custom-call(s32[21]{0:T(128)S(1)} %pad_add_fusion.table, bf16[4,4,16,128]{3,2,1,0:T(8,128)(2,1)S(1)} %pad_maximum_fusion.2.tokens, bf16[2,2,256,768]{3,2,1,0:T(8,128)(2,1)S(1)} %get-tuple-element.43.mix, f32[8,768]{1,0:T(8,128)S(1)} %get-tuple-element.44.rows, ...), custom_call_target="tpu_custom_call" | custom-call | flops 200000000 | bytes 2000000 | tf_op jit(solution)/shard_map/project_near/pallas_call | solution.py:365
  78.3 3.4 %collective-permute-done.23.far = bf16[4,4,16,128]{3,2,1,0:T(8,128)(2,1)S(1)} collective-permute-done((bf16[4,4,16,128]{3,2,1,0:T(8,128)(2,1)S(1)}, bf16[4,4,16,128]{3,2,1,0:T(8,128)(2,1)S(1)}, u32[]{:S(2)}, u32[]{:S(2)}) %collective-permute-start.23) | collective-permute-done | bytes 65568 | tf_op jit(solution)/shard_map/ppermute | solution.py:443
  81.7 5.2 %attend.1 = bf16[8,4,2,16,256]{4,3,2,1,0:T(8,128)(2,1)} custom-call(s32[21]{0:T(128)S(1)} %pad_add_fusion.table, bf16[3,2,4,128,128]{4,3,2,1,0:T(8,128)(2,1)S(1)} %project_near.1.near, bf16[4,4,16,128]{3,2,1,0:T(8,128)(2,1)S(1)} %collective-permute-done.23.far, bf16[2,2,256,768]{3,2,1,0:T(8,128)(2,1)S(1)} %get-tuple-element.43.mix, ...), custom_call_target="tpu_custom_call" | custom-call | flops 1000000000 | bytes 3000000 | tf_op jit(solution)/shard_map/attend/pallas_call | solution.py:424
  (82 shorter events, 18.5 us)
Async XLA Ops:
  1.9 8.7 %collective-permute-start.2 = (bf16[32,512]{1,0:T(8,128)(2,1)}, bf16[32,512]{1,0:T(8,128)(2,1)S(1)}, u32[]{:S(2)}, u32[]{:S(2)}) collective-permute-start(bf16[32,512]{1,0:T(8,128)(2,1)} %fold_taps.1), channel_id=1, source_target_pairs={{0,3},{1,2},{2,1},{3,0},{4,7},{5,6},{6,5},{7,4},{8,11},{9,10},{10,... | collective-permute-start | bytes 98312 | tf_op jit(solution)/shard_map/ppermute | solution.py:443
  6.6 5.0 %collective-permute-start.1 = (bf16[32,512]{1,0:T(8,128)(2,1)}, bf16[32,512]{1,0:T(8,128)(2,1)S(1)}, u32[]{:S(2)}, u32[]{:S(2)}) collective-permute-start(bf16[32,512]{1,0:T(8,128)(2,1)} %fold_taps.1), channel_id=1, source_target_pairs={{0,2},{1,3},{2,0},{3,1},{4,6},{5,7},{6,4},{7,5},{8,10},{9,11},{10,... | collective-permute-start | bytes 98312 | tf_op jit(solution)/shard_map/ppermute | solution.py:443
  6.6 5.0 %collective-permute-start = (bf16[32,512]{1,0:T(8,128)(2,1)}, bf16[32,512]{1,0:T(8,128)(2,1)S(1)}, u32[]{:S(2)}, u32[]{:S(2)}) collective-permute-start(bf16[32,512]{1,0:T(8,128)(2,1)} %fold_taps.1), channel_id=1, source_target_pairs={{0,1},{1,0},{2,3},{3,2},{4,5},{5,4},{6,7},{7,6},{8,9},{9,8},{10,11... | collective-permute-start | bytes 98312 | tf_op jit(solution)/shard_map/ppermute | solution.py:443
  7.3 13.2 %collective-permute-start.4 = (bf16[2,2,64,512]{3,2,1,0:T(8,128)(2,1)S(1)}, bf16[2,2,64,512]{3,2,1,0:T(8,128)(2,1)S(1)}, u32[]{:S(2)}, u32[]{:S(2)}) collective-permute-start(bf16[2,2,64,512]{3,2,1,0:T(8,128)(2,1)S(1)} %slice.3), channel_id=1, source_target_pairs={{0,8},{8,16},{16,24},{24,32},{32,40},{40,48},{48,56},{56,64},{64,7... | collective-permute-start | bytes 786440 | tf_op jit(solution)/shard_map/ppermute | solution.py:439
  12.4 8.0 %collective-permute-start.3 = (bf16[32,512]{1,0:T(8,128)(2,1)S(1)}, bf16[32,512]{1,0:T(8,128)(2,1)S(1)}, u32[]{:S(2)}, u32[]{:S(2)}) collective-permute-start(bf16[32,512]{1,0:T(8,128)(2,1)S(1)} %add_convert_fusion.1), channel_id=1, source_target_pairs={{0,4},{1,5},{2,6},{3,7},{4,0},{5,1},{6,2},{7,3},{8,12},{9,13},{10,... | collective-permute-start | bytes 98312 | tf_op jit(solution)/shard_map/ppermute | solution.py:443
  20.5 4.2 %collective-permute-start.7 = (bf16[32,512]{1,0:T(8,128)(2,1)S(1)}, bf16[32,512]{1,0:T(8,128)(2,1)S(1)}, u32[]{:S(2)}, u32[]{:S(2)}) collective-permute-start(bf16[32,512]{1,0:T(8,128)(2,1)S(1)} %add_convert_fusion), channel_id=1, source_target_pairs={{0,48},{8,56},{16,32},{24,40},{32,16},{40,24},{48,0},{56,8},{64,11... | collective-permute-start | bytes 98312 | tf_op jit(solution)/shard_map/ppermute | solution.py:443
  22.4 5.5 %collective-permute-start.6 = (bf16[32,512]{1,0:T(8,128)(2,1)S(1)}, bf16[32,512]{1,0:T(8,128)(2,1)S(1)}, u32[]{:S(2)}, u32[]{:S(2)}) collective-permute-start(bf16[32,512]{1,0:T(8,128)(2,1)S(1)} %add_convert_fusion), channel_id=1, source_target_pairs={{0,32},{8,40},{16,48},{24,56},{32,0},{40,8},{48,16},{56,24},{64,96... | collective-permute-start | bytes 98312 | tf_op jit(solution)/shard_map/ppermute | solution.py:443
  23.2 4.7 %collective-permute-start.5 = (bf16[32,512]{1,0:T(8,128)(2,1)S(1)}, bf16[32,512]{1,0:T(8,128)(2,1)S(1)}, u32[]{:S(2)}, u32[]{:S(2)}) collective-permute-start(bf16[32,512]{1,0:T(8,128)(2,1)S(1)} %add_convert_fusion), channel_id=1, source_target_pairs={{0,16},{8,24},{16,0},{24,8},{32,48},{40,56},{48,32},{56,40},{64,80... | collective-permute-start | bytes 98312 | tf_op jit(solution)/shard_map/ppermute | solution.py:443
  27.9 7.7 %collective-permute-start.10 = (bf16[4,32,512]{2,1,0:T(8,128)(2,1)S(1)}, bf16[4,32,512]{2,1,0:T(8,128)(2,1)S(1)}, u32[]{:S(2)}, u32[]{:S(2)}) collective-permute-start(bf16[4,32,512]{2,1,0:T(8,128)(2,1)S(1)} %pad_maximum_fusion.near), channel_id=1, source_target_pairs={{0,192},{8,200},{16,208},{24,216},{32,224},{40,232},{48,240},{56,2... | collective-permute-start | bytes 393224 | tf_op jit(solution)/shard_map/ppermute | solution.py:443
  30.6 6.7 %collective-permute-start.9 = (bf16[4,32,512]{2,1,0:T(8,128)(2,1)S(1)}, bf16[4,32,512]{2,1,0:T(8,128)(2,1)S(1)}, u32[]{:S(2)}, u32[]{:S(2)}) collective-permute-start(bf16[4,32,512]{2,1,0:T(8,128)(2,1)S(1)} %pad_maximum_fusion.near), channel_id=1, source_target_pairs={{0,128},{8,136},{16,144},{24,152},{32,160},{40,168},{48,176},{56,1... | collective-permute-start | bytes 393224 | tf_op jit(solution)/shard_map/ppermute | solution.py:443
  31.6 5.8 %collective-permute-start.8 = (bf16[4,32,512]{2,1,0:T(8,128)(2,1)S(1)}, bf16[4,32,512]{2,1,0:T(8,128)(2,1)S(1)}, u32[]{:S(2)}, u32[]{:S(2)}) collective-permute-start(bf16[4,32,512]{2,1,0:T(8,128)(2,1)S(1)} %pad_maximum_fusion.near), channel_id=1, source_target_pairs={{0,64},{8,72},{16,80},{24,88},{32,96},{40,104},{48,112},{56,120},{... | collective-permute-start | bytes 393224 | tf_op jit(solution)/shard_map/ppermute | solution.py:443
  39.0 3.8 %collective-permute-start.11 = (f32[16,256]{1,0:T(8,128)S(1)}, f32[16,256]{1,0:T(8,128)S(1)}, u32[]{:S(2)}, u32[]{:S(2)}) collective-permute-start(f32[16,256]{1,0:T(8,128)S(1)} %get-tuple-element.32), channel_id=1, source_target_pairs={{0,1},{2,3},{4,5},{6,7},{1,0},{3,2},{5,4},{7,6},{8,9},{10,11},{12,... | collective-permute-start | bytes 49160 | tf_op jit(solution)/shard_map/ppermute | solution.py:448
  39.3 3.5 %collective-permute-start.12 = (f32[16,256]{1,0:T(8,128)S(1)}, f32[16,256]{1,0:T(8,128)S(1)}, u32[]{:S(2)}, u32[]{:S(2)}) collective-permute-start(f32[16,256]{1,0:T(8,128)S(1)} %get-tuple-element.33), channel_id=1, source_target_pairs={{1,2},{3,4},{5,6},{2,1},{4,3},{6,5},{9,10},{11,12},{13,14},{10,9},... | collective-permute-start | bytes 49160 | tf_op jit(solution)/shard_map/ppermute | solution.py:448
  43.3 5.3 %collective-permute-start.15 = (bf16[4,16,128]{2,1,0:T(8,128)(2,1)S(1)}, bf16[4,16,128]{2,1,0:T(8,128)(2,1)S(1)}, u32[]{:S(2)}, u32[]{:S(2)}) collective-permute-start(bf16[4,16,128]{2,1,0:T(8,128)(2,1)S(1)} %finish.1), channel_id=1, source_target_pairs={{0,48},{8,56},{16,32},{24,40},{32,16},{40,24},{48,0},{56,8},{64,11... | collective-permute-start | bytes 49160 | tf_op jit(solution)/shard_map/ppermute | solution.py:443
  44.6 5.2 %collective-permute-start.14 = (bf16[4,16,128]{2,1,0:T(8,128)(2,1)S(1)}, bf16[4,16,128]{2,1,0:T(8,128)(2,1)S(1)}, u32[]{:S(2)}, u32[]{:S(2)}) collective-permute-start(bf16[4,16,128]{2,1,0:T(8,128)(2,1)S(1)} %finish.1), channel_id=1, source_target_pairs={{0,32},{8,40},{16,48},{24,56},{32,0},{40,8},{48,16},{56,24},{64,96... | collective-permute-start | bytes 49160 | tf_op jit(solution)/shard_map/ppermute | solution.py:443
  46.7 3.7 %collective-permute-start.13 = (bf16[4,16,128]{2,1,0:T(8,128)(2,1)S(1)}, bf16[4,16,128]{2,1,0:T(8,128)(2,1)S(1)}, u32[]{:S(2)}, u32[]{:S(2)}) collective-permute-start(bf16[4,16,128]{2,1,0:T(8,128)(2,1)S(1)} %finish.1), channel_id=1, source_target_pairs={{0,16},{8,24},{16,0},{24,8},{32,48},{40,56},{48,32},{56,40},{64,80... | collective-permute-start | bytes 49160 | tf_op jit(solution)/shard_map/ppermute | solution.py:443
  50.5 8.8 %collective-permute-start.18 = (bf16[4,4,16,128]{3,2,1,0:T(8,128)(2,1)S(1)}, bf16[4,4,16,128]{3,2,1,0:T(8,128)(2,1)S(1)}, u32[]{:S(2)}, u32[]{:S(2)}) collective-permute-start(bf16[4,4,16,128]{3,2,1,0:T(8,128)(2,1)S(1)} %pad_maximum_fusion.1.near), channel_id=1, source_target_pairs={{0,192},{8,200},{16,208},{24,216},{32,224},{40,232},{48,240},{56,2... | collective-permute-start | bytes 196616 | tf_op jit(solution)/shard_map/ppermute | solution.py:443
  52.5 6.7 %collective-permute-start.17 = (bf16[4,4,16,128]{3,2,1,0:T(8,128)(2,1)S(1)}, bf16[4,4,16,128]{3,2,1,0:T(8,128)(2,1)S(1)}, u32[]{:S(2)}, u32[]{:S(2)}) collective-permute-start(bf16[4,4,16,128]{3,2,1,0:T(8,128)(2,1)S(1)} %pad_maximum_fusion.1.near), channel_id=1, source_target_pairs={{0,128},{8,136},{16,144},{24,152},{32,160},{40,168},{48,176},{56,1... | collective-permute-start | bytes 196616 | tf_op jit(solution)/shard_map/ppermute | solution.py:443
  53.8 5.5 %collective-permute-start.16 = (bf16[4,4,16,128]{3,2,1,0:T(8,128)(2,1)S(1)}, bf16[4,4,16,128]{3,2,1,0:T(8,128)(2,1)S(1)}, u32[]{:S(2)}, u32[]{:S(2)}) collective-permute-start(bf16[4,4,16,128]{3,2,1,0:T(8,128)(2,1)S(1)} %pad_maximum_fusion.1.near), channel_id=1, source_target_pairs={{0,64},{8,72},{16,80},{24,88},{32,96},{40,104},{48,112},{56,120},{... | collective-permute-start | bytes 196616 | tf_op jit(solution)/shard_map/ppermute | solution.py:443
  60.0 1.3 %collective-permute-start.19 = (bf16[4,16,128]{2,1,0:T(8,128)(2,1)S(1)}, bf16[4,16,128]{2,1,0:T(8,128)(2,1)S(1)}, u32[]{:S(2)}, u32[]{:S(2)}) collective-permute-start(bf16[4,16,128]{2,1,0:T(8,128)(2,1)S(1)} %get-tuple-element.42), channel_id=1, source_target_pairs={{0,8},{8,0},{16,24},{24,16},{32,40},{40,32},{48,56},{56,48},{64,72... | collective-permute-start | bytes 49160 | tf_op jit(solution)/shard_map/ppermute | solution.py:443
  61.3 9.1 %collective-permute-start.22 = (bf16[4,16,128]{2,1,0:T(8,128)(2,1)S(1)}, bf16[4,16,128]{2,1,0:T(8,128)(2,1)S(1)}, u32[]{:S(2)}, u32[]{:S(2)}) collective-permute-start(bf16[4,16,128]{2,1,0:T(8,128)(2,1)S(1)} %add.101), channel_id=1, source_target_pairs={{0,3},{1,2},{2,1},{3,0},{4,7},{5,6},{6,5},{7,4},{8,11},{9,10},{10,... | collective-permute-start | bytes 49160 | tf_op jit(solution)/shard_map/ppermute | solution.py:443
  68.7 4.6 %collective-permute-start.21 = (bf16[4,16,128]{2,1,0:T(8,128)(2,1)S(1)}, bf16[4,16,128]{2,1,0:T(8,128)(2,1)S(1)}, u32[]{:S(2)}, u32[]{:S(2)}) collective-permute-start(bf16[4,16,128]{2,1,0:T(8,128)(2,1)S(1)} %add.101), channel_id=1, source_target_pairs={{0,2},{1,3},{2,0},{3,1},{4,6},{5,7},{6,4},{7,5},{8,10},{9,11},{10,... | collective-permute-start | bytes 49160 | tf_op jit(solution)/shard_map/ppermute | solution.py:443
  68.7 4.6 %collective-permute-start.20 = (bf16[4,16,128]{2,1,0:T(8,128)(2,1)S(1)}, bf16[4,16,128]{2,1,0:T(8,128)(2,1)S(1)}, u32[]{:S(2)}, u32[]{:S(2)}) collective-permute-start(bf16[4,16,128]{2,1,0:T(8,128)(2,1)S(1)} %add.101), channel_id=1, source_target_pairs={{0,1},{1,0},{2,3},{3,2},{4,5},{5,4},{6,7},{7,6},{8,9},{9,8},{10,11... | collective-permute-start | bytes 49160 | tf_op jit(solution)/shard_map/ppermute | solution.py:443
  73.3 8.4 %collective-permute-start.23 = (bf16[4,4,16,128]{3,2,1,0:T(8,128)(2,1)S(1)}, bf16[4,4,16,128]{3,2,1,0:T(8,128)(2,1)S(1)}, u32[]{:S(2)}, u32[]{:S(2)}) collective-permute-start(bf16[4,4,16,128]{3,2,1,0:T(8,128)(2,1)S(1)} %pad_maximum_fusion.2.tokens), channel_id=1, source_target_pairs={{0,4},{1,5},{2,6},{3,7},{4,0},{5,1},{6,2},{7,3},{8,12},{9,13},{10,... | collective-permute-start | bytes 196616 | tf_op jit(solution)/shard_map/ppermute | solution.py:443
  (13 other events, 304.6 us)

commit v3 on v2

--- a/solution.py
+++ b/solution.py
@@ -31,25 +31,22 @@
 
 def fold_kernel(weight, latent, out, tap_buf, lat_buf, sems):
     band = lax.axis_index("head")
-    last = weight.shape[0] - 1
-    base = lax.axis_index("seq") // 2 * 2
-    copies = [
-        pltpu.make_async_copy(weight.at[jnp.minimum(base, last)], tap_buf.at[0], sems.at[0]),
-        pltpu.make_async_copy(weight.at[jnp.minimum(base + 1, last)], tap_buf.at[1], sems.at[1]),
-        pltpu.make_async_copy(latent, lat_buf, sems.at[2]),
-    ]
-    for copy in copies:
-        copy.start()
-    copies[2].wait()
+    tap = jnp.minimum(lax.axis_index("seq"), weight.shape[0] - 1)
+    first = pltpu.make_async_copy(weight.at[tap], tap_buf, sems.at[0])
+    second = pltpu.make_async_copy(latent, lat_buf, sems.at[1])
+    first.start()
+    second.start()
+    second.wait()
     own = jnp.where(iota((16, 512), 1) // 64 == band, lat_buf[...].astype(f32), 0.0)
     pair = own[:, 0:128] + own[:, 128:256] + own[:, 256:384] + own[:, 384:512]
     left = (pair[:, 0:64] + pair[:, 64:128]).astype(bf16)
-    for tap in range(2):
-        copies[tap].wait()
-        out[tap * 16 : tap * 16 + 16, :] = dot(left, tap_buf[tap]).astype(bf16)
-
-
-def fold_taps(weight, latent_rows):
+    first.wait()
+    part = dot(left, tap_buf[...]).astype(bf16)
+    for peer in range(out.shape[0]):
+        out[peer] = part
+
+
+def fold_tap(weight, latent_rows, copies):
     taps, outs, ins = weight.shape
     lats = latent_rows.shape[0]
     whole = pl.BlockSpec(memory_space=pl.ANY)
@@ -57,15 +54,15 @@
         fold_kernel,
         in_specs=[whole, whole],
         out_specs=pl.BlockSpec(memory_space=pltpu.VMEM),
-        out_shape=jax.ShapeDtypeStruct((2 * lats, ins), bf16),
+        out_shape=jax.ShapeDtypeStruct((copies, lats, ins), bf16),
         scratch_shapes=[
-            pltpu.VMEM((2, outs, ins), bf16),
+            pltpu.VMEM((outs, ins), bf16),
             pltpu.VMEM((lats, ins), bf16),
-            pltpu.SemaphoreType.DMA((3,)),
+            pltpu.SemaphoreType.DMA((2,)),
         ],
         compiler_params=pltpu.CompilerParams(vmem_limit_bytes=56 * MIB),
         cost_estimate=pl.CostEstimate(flops=10**6, bytes_accessed=150000, transcendentals=0),
-        name="fold_taps",
+        name="fold_tap",
     )(weight, latent_rows)
 
 
@@ -98,13 +95,14 @@
     )(video, prev, lat, conv_bias.reshape(1, -1), latent_bias.reshape(-1, 1))
 
 
-def conv_kernel(table, act, near, far1, far2, far3, base, own, first, second, weight, taps):
+def conv_kernel(table, act, same, other, base, own, first, second, weight, taps):
     even = lax.axis_index("head") % 2 == 0
-    chip = lax.axis_index("seq") // 2
-    for high, group in enumerate((near, far1, far2, far3)):
-        for low in range(4):
-            at = pl.multiple_of((chip ^ (high * 4 + low)) * 32, 32)
-            weight[pl.ds(at, 32), :] = group[low]
+    core = lax.axis_index("seq") % 2
+    for chip in range(16):
+        own_at = pl.multiple_of(chip * 32 + core * 16, 16)
+        pair_at = pl.multiple_of(chip * 32 + 16 - core * 16, 16)
+        weight[pl.ds(own_at, 16), :] = same[chip]
+        weight[pl.ds(pair_at, 16), :] = other[chip]
     for frame in range(6):
         taps[frame] = dot(weight[0:432, :], act[frame * 128 : frame * 128 + 128, :], NT)
     column = iota((16, 128), 1) % 64
@@ -139,7 +137,7 @@
     vmem = pl.BlockSpec(memory_space=pltpu.VMEM)
     return pl.pallas_call(
         conv_kernel,
-        in_specs=[smem] + [vmem] * 6,
+        in_specs=[smem] + [vmem] * 4,
         out_specs=(vmem, vmem, vmem),
         out_shape=(
             jax.ShapeDtypeStruct((16, 512), f32),
@@ -169,50 +167,47 @@
         edge = jnp.concatenate([jnp.where(even, two, one), jnp.where(even, one, two)], axis=1)
         latent = ((own[:, frame * 128 : frame * 128 + 128] + edge) * latent_scale).astype(bf16)
         wide = jnp.where(keep, dot(repeat, latent), 0.0).astype(bf16)
-        out[frame] = dot(pick, wide, NT).astype(bf16)
-
-
-def finish(own, first, second):
+        piece = dot(pick, wide, NT).astype(bf16)
+        for peer in range(out.shape[0]):
+            out[peer, frame] = piece
+
+
+def finish(own, first, second, copies):
     vmem = pl.BlockSpec(memory_space=pltpu.VMEM)
     return pl.pallas_call(
         finish_kernel,
         in_specs=[vmem, vmem, vmem],
         out_specs=vmem,
-        out_shape=jax.ShapeDtypeStruct((4, 16, 128), bf16),
+        out_shape=jax.ShapeDtypeStruct((copies, 4, 16, 128), bf16),
         compiler_params=pltpu.CompilerParams(vmem_limit_bytes=6 * MIB),
         cost_estimate=pl.CostEstimate(flops=10**7, bytes_accessed=10**6, transcendentals=0),
         name="finish",
     )(own, first, second)
 
 
-def route_kernel(table, near, far1, far2, far3, mine, other, frames):
-    seq = lax.axis_index("seq")
-    chip, core = seq // 2, seq % 2
-    for high, group in enumerate((near, far1, far2, far3)):
-        for low in range(4):
-            frames[high * 4 + low] = group[low]
+def route_kernel(table, frames, mine, other):
+    core = lax.axis_index("seq") % 2
     for out, owner in ((mine, core), (other, 1 - core)):
         for slot in range(4):
             frame = table[12 + owner * 4 + slot]
             here = (frame // 4) % 2 == core
-            piece = frames[(frame // 8) ^ chip, frame % 4]
+            piece = frames[frame // 8, frame % 4]
             out[slot] = jnp.where(here, piece, jnp.zeros_like(piece))
 
 
-def route(table, groups):
+def route(table, frames):
     smem = pl.BlockSpec(memory_space=pltpu.SMEM)
     vmem = pl.BlockSpec(memory_space=pltpu.VMEM)
     shape = jax.ShapeDtypeStruct((4, 16, 128), bf16)
     return pl.pallas_call(
         route_kernel,
-        in_specs=[smem] + [vmem] * 4,
+        in_specs=[smem, vmem],
         out_specs=(vmem, vmem),
         out_shape=(shape, shape),
-        scratch_shapes=[pltpu.VMEM((16, 4, 16, 128), bf16)],
         compiler_params=pltpu.CompilerParams(vmem_limit_bytes=4 * MIB),
         cost_estimate=pl.CostEstimate(flops=1, bytes_accessed=10**6, transcendentals=0),
         name="route",
-    )(table, *groups)
+    )(table, frames)
 
 
 def scale_kernel(member, modulation, embed, bias, left, gram, gvec):
@@ -452,11 +447,6 @@
     return [value] + [swap(value, axis, unit * step) for step in (3, 2, 1)][::-1]
 
 
-def gather_chips(value):
-    row = jnp.stack(swap3(value, "seq", 2))
-    return swap3(row, "seq", 8)
-
-
 def per_device(
     video_feat,
     clip_frames,
@@ -479,11 +469,9 @@
     latent_rows = latent_weight.T
 
     weight = conv_weight.transpose(0, 1, 2, 4, 3).reshape(27, conv_weight.shape[4], -1)
-    part = fold_taps(weight, latent_rows)
+    parts = lax.all_to_all(fold_tap(weight, latent_rows, heads), "head", 0, 0)
     prev = neighbour(video_feat[2:], "seq", 1)
-    add = lambda values: sum(value.astype(f32) for value in values).astype(bf16)
-    four = add(swap3(part, "head", 1))
-    taps = add([four, swap(four, "head", 4)])
+    tap = jnp.sum(parts.astype(f32), axis=0).astype(bf16)
 
     count = clip_frames.shape[0]
     numbers = jnp.arange(count, dtype=jnp.int32)
@@ -509,9 +497,12 @@
 
     left, gram, gvec = scale_embedding(member, modulation, embed_weight, embed_bias)
 
-    taps, table, prev = lax.optimization_barrier((taps, table, prev))
-    row = jnp.stack(swap3(taps, "seq", 2))
-    folded = swap3(row, "seq", 8)
+    tap, table, prev = lax.optimization_barrier((tap, table, prev))
+    chips = seqs // 2
+    cores = [[2 * chip + core for chip in range(chips)] for core in range(2)]
+    over_chips = lambda value: lax.all_to_all(value, "seq", 0, 0, axis_index_groups=cores)
+    same = over_chips(jnp.broadcast_to(tap[None], (chips,) + tap.shape))
+    folded = same, swap(same, "seq", 1)
     mix, rows = mix_weights(left, qkv_weight, qkv_bias)
     mixed = mix, rows, gram, gvec
     act, base = prepare(video_feat, prev, latent_rows, conv_bias, latent_bias)
@@ -519,9 +510,9 @@
     own, first, second = convolve(table, act, folded, base)
     first = swap_pairs(first, "head", 0)
     second = swap_pairs(second, "head", 1)
-    pieces = finish(own, first, second)
-
-    mine, other = route(table, gather_chips(pieces))
+    pieces = finish(own, first, second, chips)
+    frames_all = over_chips(pieces)
+    mine, other = route(table, frames_all)
     mine, other, mixed = lax.optimization_barrier((mine, other, mixed))
     slots = mine + swap(other, "seq", 1)
     near = jnp.stack(swap3(slots, "head", 1))

time: 87.4 us -> 81.7 us (0.935)
  the two profiles are of different devices: /device:TPU:8 before, /device:TPU:1 now
where the time goes in v3:
time: 81.7 us; the launch traced here: 80.1 us
  starting transfers between devices  34 us (42%)
  Pallas kernels  15.9 us (19%)
  blocking collectives  14 us (17%)
  waiting for transfers between devices  11.1 us (14%)
  local copies, waits for them, and re-layouts  2.67 us (3%)
  other arithmetic  2.18 us (3%)
    ppermute x6, starting transfers between devices, swap(): lax.ppermute(value, axis, [(i, i ^ mask) for i in range(lax.axis_size(axi...  16.4 us
    all_to_all x1, blocking collectives, per_device(): lax.all_to_all(value, 'seq', 0, 0, axis_index_groups=cores)  14 us
    all_to_all x1, starting transfers between devices, per_device(): parts = lax.all_to_all(fold_tap(weight, latent_rows, heads), 'head', 0, 0)  9.03 us
    ppermute x6, waiting for transfers between devices, swap(): lax.ppermute(value, axis, [(i, i ^ mask) for i in range(lax.axis_size(axi...  6.49 us
    pallas_call x1, Pallas kernels, attend(): pl.pallas_call(attend_kernel, in_specs=[smem] + [vmem] * 8, out_specs=vme...  5.39 us
    ppermute x1, starting transfers between devices, neighbour(): return lax.ppermute(value, axis, pairs)  4.05 us
    all_to_all x1, starting transfers between devices, per_device(): lax.all_to_all(value, 'seq', 0, 0, axis_index_groups=cores)  3.53 us
    unnamed x26, local copies, waits for them, and re-layouts  2.38 us
  transfers between devices with their start and end apart: 11, of which 8 were waited for; matrix products, arithmetic and copies ran while one was open for 3% of the time, Pallas kernels for 7%

profile of v3, /device:TPU:1, one launch (start us, length us, event | category | flops | bytes accessed | tf_op | source)
XLA Modules:
  0.0 80.1 jit_solution(9390671860076032753)
XLA Ops:
  0.0 1.7 %fold_tap.1 = bf16[8,16,512]{2,1,0:T(8,128)(2,1)} custom-call(bf16[27,64,512]{2,1,0:T(8,128)(2,1)} %bitcast.27, bf16[16,512]{1,0:T(8,128)(2,1)} %bitcast.19), custom_call_target="tpu_custom_call" | custom-call | flops 1000000 | bytes 150000 | tf_op jit(solution)/shard_map/fold_tap/pallas_call | solution.py:53
  1.8 9.0 %all-to-all-start = ((bf16[8,16,512]{2,1,0:T(8,128)(2,1)}), bf16[8,16,512]{2,1,0:T(8,128)(2,1)S(1)}, u32[]{:S(2)}, u32[]{:S(2)}) async-start(bf16[8,16,512]{2,1,0:T(8,128)(2,1)} %fold_tap.1), calls=%async_computation | async-start | bytes 262144 | tf_op jit(solution)/shard_map/all_to_all | solution.py:472
  10.8 4.0 %collective-permute-start = (bf16[2,2,64,512]{3,2,1,0:T(8,128)(2,1)S(1)}, bf16[2,2,64,512]{3,2,1,0:T(8,128)(2,1)S(1)}, u32[]{:S(2)}, u32[]{:S(2)}) collective-permute-start(bf16[2,2,64,512]{3,2,1,0:T(8,128)(2,1)S(1)} %slice.3), channel_id=1, source_target_pairs={{0,8},{8,16},{16,24},{24,32},{32,40},{40,48},{48,56},{56,64},{64,7... | collective-permute-start | bytes 786440 | tf_op jit(solution)/shard_map/ppermute | solution.py:434
  16.3 0.8 pad_add_fusion.table
  17.0 1.5 %all-to-all-done = bf16[8,16,512]{2,1,0:T(8,128)(2,1)S(1)} async-done(((bf16[8,16,512]{2,1,0:T(8,128)(2,1)}), bf16[8,16,512]{2,1,0:T(8,128)(2,1)S(1)}, u32[]{:S(2)}, u32[]{:S(2)}) %all-to-all-start) | async-done | bytes 131104 | tf_op jit(solution)/shard_map/all_to_all | solution.py:472
  18.6 14.0 %all_to_all.15.same = bf16[16,16,512]{2,1,0:T(8,128)(2,1)S(1)} all-to-all(bf16[16,16,512]{2,1,0:T(8,128)(2,1)S(1)} %broadcast_in_dim.65), channel_id=1, replica_groups={{0,16,32,48,64,80,96,112,128,144,160,176,192,208,224,240},{8,24,40,56,7..., dimensions={0} | all-to-all | bytes 524288 | tf_op jit(solution)/shard_map/all_to_all | solution.py:503
  32.6 3.6 %collective-permute-start.1 = (bf16[16,16,512]{2,1,0:T(8,128)(2,1)S(1)}, bf16[16,16,512]{2,1,0:T(8,128)(2,1)S(1)}, u32[]{:S(2)}, u32[]{:S(2)}) collective-permute-start(bf16[16,16,512]{2,1,0:T(8,128)(2,1)S(1)} %all_to_all.15.same), channel_id=1, source_target_pairs={{0,8},{8,0},{16,24},{24,16},{32,40},{40,32},{48,56},{56,48},{64,72... | collective-permute-start | bytes 786440 | tf_op jit(solution)/shard_map/ppermute | solution.py:438
  37.4 1.6 %convolve.1 = (f32[16,512]{1,0:T(8,128)S(1)}, f32[16,256]{1,0:T(8,128)S(1)}, f32[16,256]{1,0:T(8,128)S(1)}) custom-call(s32[21]{0:T(128)S(1)} %pad_add_fusion.table, bf16[768,512]{1,0:T(8,128)(2,1)S(1)} %get-tuple-element.28.act, bf16[16,16,512]{2,1,0:T(8,128)(2,1)S(1)} %all_to_all.15.same, bf16[16,16,512]{2,1,0:T(8,128)(2,1)S(1)} %collective-permute-done.1.other, ...), custom_call_target="tpu_custom_call" | custom-call | flops 400000000 | bytes 2000000 | tf_op jit(solution)/shard_map/convolve/pallas_call | solution.py:138
  40.2 1.5 %collective-permute-done.2.first = f32[16,256]{1,0:T(8,128)S(1)} collective-permute-done((f32[16,256]{1,0:T(8,128)S(1)}, f32[16,256]{1,0:T(8,128)S(1)}, u32[]{:S(2)}, u32[]{:S(2)}) %collective-permute-start.2) | collective-permute-done | bytes 16416 | tf_op jit(solution)/shard_map/ppermute | solution.py:443
  41.7 1.2 %finish.1 = bf16[16,4,16,128]{3,2,1,0:T(8,128)(2,1)} custom-call(f32[16,512]{1,0:T(8,128)S(1)} %get-tuple-element.31.own, f32[16,256]{1,0:T(8,128)S(1)} %collective-permute-done.2.first, f32[16,256]{1,0:T(8,128)S(1)} %collective-permute-done.3.second), custom_call_target="tpu_custom_call" | custom-call | flops 10000000 | bytes 1000000 | tf_op jit(solution)/shard_map/finish/pallas_call | solution.py:177
  42.9 3.5 %all-to-all-start.2 = ((bf16[16,4,16,128]{3,2,1,0:T(8,128)(2,1)}), bf16[16,4,16,128]{3,2,1,0:T(8,128)(2,1)S(1)}, u32[]{:S(2)}, u32[]{:S(2)}) async-start(bf16[16,4,16,128]{3,2,1,0:T(8,128)(2,1)} %finish.1), calls=%async_computation.2 | async-start | bytes 524288 | tf_op jit(solution)/shard_map/all_to_all | solution.py:503
  46.5 1.0 %scale_embedding.1 = (bf16[272,3072]{1,0:T(8,128)(2,1)S(1)}, bf16[3,128,128]{2,1,0:T(8,128)(2,1)S(1)}, f32[8,128]{1,0:T(8,128)S(1)}) custom-call(bf16[8,64]{1,0:T(8,128)(2,1)S(1)} %add_convert_fusion.member, bf16[64,6144]{1,0:T(8,128)(2,1)S(1)} %copy-done.1, bf16[64,3072]{1,0:T(8,128)(2,1)S(1)} %copy-done.2, f32[1,3072]{1,0:T(1,128)S(1)} %bitcast.21), custom_call_target="tpu_custom_call" | custom-call | flops 100000000 | bytes 3000000 | tf_op jit(solution)/shard_map/scale_embedding/pallas_call | solution.py:261
  47.6 2.3 %copy-done = bf16[3072,768]{1,0:T(8,128)(2,1)S(1)} copy-done((bf16[3072,768]{1,0:T(8,128)(2,1)S(1)}, bf16[3072,768]{1,0:T(8,128)(2,1)}, u32[]{:S(2)}) %copy-start) | copy-done | bytes 4718616
  49.9 2.3 %mix_weights.1 = (bf16[2,2,256,768]{3,2,1,0:T(8,128)(2,1)S(1)}, f32[8,768]{1,0:T(8,128)S(1)}) custom-call(bf16[272,3072]{1,0:T(8,128)(2,1)S(1)} %get-tuple-element.36.left, bf16[3072,768]{1,0:T(8,128)(2,1)S(1)} %copy-done, f32[1,768]{1,0:T(1,128)S(1)} %reshape.61.qkv_b), custom_call_target="tpu_custom_call" | custom-call | flops 1300000000 | bytes 6000000 | tf_op jit(solution)/shard_map/mix_weights/pallas_call | solution.py:294
  52.2 1.6 %all-to-all-done.2.frames = bf16[16,4,16,128]{3,2,1,0:T(8,128)(2,1)S(1)} async-done(((bf16[16,4,16,128]{3,2,1,0:T(8,128)(2,1)}), bf16[16,4,16,128]{3,2,1,0:T(8,128)(2,1)S(1)}, u32[]{:S(2)}, u32[]{:S(2)}) %all-to-all-start.2) | async-done | bytes 262176 | tf_op jit(solution)/shard_map/all_to_all | solution.py:503
  54.4 2.9 %collective-permute-start.4 = (bf16[4,16,128]{2,1,0:T(8,128)(2,1)S(1)}, bf16[4,16,128]{2,1,0:T(8,128)(2,1)S(1)}, u32[]{:S(2)}, u32[]{:S(2)}) collective-permute-start(bf16[4,16,128]{2,1,0:T(8,128)(2,1)S(1)} %get-tuple-element.42), channel_id=1, source_target_pairs={{0,8},{8,0},{16,24},{24,16},{32,40},{40,32},{48,56},{56,48},{64,72... | collective-permute-start | bytes 49160 | tf_op jit(solution)/shard_map/ppermute | solution.py:438
  57.3 0.8 %collective-permute-done.4 = bf16[4,16,128]{2,1,0:T(8,128)(2,1)S(1)} collective-permute-done((bf16[4,16,128]{2,1,0:T(8,128)(2,1)S(1)}, bf16[4,16,128]{2,1,0:T(8,128)(2,1)S(1)}, u32[]{:S(2)}, u32[]{:S(2)}) %collective-permute-start.4) | collective-permute-done | bytes 16416 | tf_op jit(solution)/shard_map/ppermute | solution.py:438
  58.2 5.9 %collective-permute-start.7 = (bf16[4,16,128]{2,1,0:T(8,128)(2,1)S(1)}, bf16[4,16,128]{2,1,0:T(8,128)(2,1)S(1)}, u32[]{:S(2)}, u32[]{:S(2)}) collective-permute-start(bf16[4,16,128]{2,1,0:T(8,128)(2,1)S(1)} %add.85), channel_id=1, source_target_pairs={{0,3},{1,2},{2,1},{3,0},{4,7},{5,6},{6,5},{7,4},{8,11},{9,10},{10,... | collective-permute-start | bytes 49160 | tf_op jit(solution)/shard_map/ppermute | solution.py:438
  64.4 0.8 collective-permute-done.7
  65.2 2.4 %collective-permute-done.6 = bf16[4,16,128]{2,1,0:T(8,128)(2,1)S(1)} collective-permute-done((bf16[4,16,128]{2,1,0:T(8,128)(2,1)S(1)}, bf16[4,16,128]{2,1,0:T(8,128)(2,1)S(1)}, u32[]{:S(2)}, u32[]{:S(2)}) %collective-permute-start.6) | collective-permute-done | bytes 16416 | tf_op jit(solution)/shard_map/ppermute | solution.py:438
  67.6 3.6 %collective-permute-start.8 = (bf16[4,4,16,128]{3,2,1,0:T(8,128)(2,1)S(1)}, bf16[4,4,16,128]{3,2,1,0:T(8,128)(2,1)S(1)}, u32[]{:S(2)}, u32[]{:S(2)}) collective-permute-start(bf16[4,4,16,128]{3,2,1,0:T(8,128)(2,1)S(1)} %pad_maximum_fusion.tokens), channel_id=1, source_target_pairs={{0,4},{1,5},{2,6},{3,7},{4,0},{5,1},{6,2},{7,3},{8,12},{9,13},{10,... | collective-permute-start | bytes 196616 | tf_op jit(solution)/shard_map/ppermute | solution.py:438
  71.2 1.6 %project_near.1.near = bf16[3,2,4,128,128]{4,3,2,1,0:T(8,128)(2,1)S(1)} custom-call(s32[21]{0:T(128)S(1)} %pad_add_fusion.table, bf16[4,4,16,128]{3,2,1,0:T(8,128)(2,1)S(1)} %pad_maximum_fusion.tokens, bf16[2,2,256,768]{3,2,1,0:T(8,128)(2,1)S(1)} %get-tuple-element.43.mix, f32[8,768]{1,0:T(8,128)S(1)} %get-tuple-element.44.rows, ...), custom_call_target="tpu_custom_call" | custom-call | flops 200000000 | bytes 2000000 | tf_op jit(solution)/shard_map/project_near/pallas_call | solution.py:360
  72.8 1.9 %collective-permute-done.8.far = bf16[4,4,16,128]{3,2,1,0:T(8,128)(2,1)S(1)} collective-permute-done((bf16[4,4,16,128]{3,2,1,0:T(8,128)(2,1)S(1)}, bf16[4,4,16,128]{3,2,1,0:T(8,128)(2,1)S(1)}, u32[]{:S(2)}, u32[]{:S(2)}) %collective-permute-start.8) | collective-permute-done | bytes 65568 | tf_op jit(solution)/shard_map/ppermute | solution.py:438
  74.7 5.4 %attend.1 = bf16[8,4,2,16,256]{4,3,2,1,0:T(8,128)(2,1)} custom-call(s32[21]{0:T(128)S(1)} %pad_add_fusion.table, bf16[3,2,4,128,128]{4,3,2,1,0:T(8,128)(2,1)S(1)} %project_near.1.near, bf16[4,4,16,128]{3,2,1,0:T(8,128)(2,1)S(1)} %collective-permute-done.8.far, bf16[2,2,256,768]{3,2,1,0:T(8,128)(2,1)S(1)} %get-tuple-element.43.mix, ...), custom_call_target="tpu_custom_call" | custom-call | flops 1000000000 | bytes 3000000 | tf_op jit(solution)/shard_map/attend/pallas_call | solution.py:419
  (55 shorter events, 4.9 us)
Async XLA Ops:
  0.0 10.8 %copy-start.3 = (bf16[4,2,64,512]{3,2,1,0:T(8,128)(2,1)S(1)}, bf16[4,2,64,512]{3,2,1,0:T(8,128)(2,1)}, u32[]{:S(2)}) copy-start(bf16[4,2,64,512]{3,2,1,0:T(8,128)(2,1)} %main.1) | copy-start | bytes 1572868
  0.0 14.9 %copy-start.11 = (s32[64]{0:T(128)S(1)}, s32[64]{0:T(128)}, u32[]{:S(2)}) copy-start(s32[64]{0:T(128)} %param.15) | copy-start | bytes 772
  0.0 15.4 %copy-start.9 = (s32[64]{0:T(128)S(1)}, s32[64]{0:T(128)}, u32[]{:S(2)}) copy-start(s32[64]{0:T(128)} %param.16) | copy-start | bytes 772
  0.0 36.2 %copy-start.12 = (f32[16]{0:T(128)S(1)}, f32[16]{0:T(128)}, u32[]{:S(2)}) copy-start(f32[16]{0:T(128)} %param.20) | copy-start | bytes 196
  0.0 36.3 %copy-start.4 = (bf16[512,16]{0,1:T(8,128)(2,1)S(1)}, bf16[512,16]{0,1:T(8,128)(2,1)}, u32[]{:S(2)}) copy-start(bf16[512,16]{0,1:T(8,128)(2,1)} %param.19) | copy-start | bytes 49156
  0.0 36.3 %copy-start.8 = (f32[512]{0:T(512)S(1)}, f32[512]{0:T(512)}, u32[]{:S(2)}) copy-start(f32[512]{0:T(512)} %param.18) | copy-start | bytes 6148
  1.8 16.8 %all-to-all-start = ((bf16[8,16,512]{2,1,0:T(8,128)(2,1)}), bf16[8,16,512]{2,1,0:T(8,128)(2,1)S(1)}, u32[]{:S(2)}, u32[]{:S(2)}) async-start(bf16[8,16,512]{2,1,0:T(8,128)(2,1)} %fold_tap.1), calls=%async_computation | async-start | bytes 262144 | tf_op jit(solution)/shard_map/all_to_all | solution.py:472
  10.8 7.8 %collective-permute-start = (bf16[2,2,64,512]{3,2,1,0:T(8,128)(2,1)S(1)}, bf16[2,2,64,512]{3,2,1,0:T(8,128)(2,1)S(1)}, u32[]{:S(2)}, u32[]{:S(2)}) collective-permute-start(bf16[2,2,64,512]{3,2,1,0:T(8,128)(2,1)S(1)} %slice.3), channel_id=1, source_target_pairs={{0,8},{8,16},{16,24},{24,32},{32,40},{40,48},{48,56},{56,64},{64,7... | collective-permute-start | bytes 786440 | tf_op jit(solution)/shard_map/ppermute | solution.py:434
  18.6 21.5 %copy-start.10 = (f32[768]{0:T(1024)S(1)}, f32[768]{0:T(1024)}, u32[]{:S(2)}) copy-start(f32[768]{0:T(1024)} %param.25) | copy-start | bytes 9220
  32.6 4.8 %collective-permute-start.1 = (bf16[16,16,512]{2,1,0:T(8,128)(2,1)S(1)}, bf16[16,16,512]{2,1,0:T(8,128)(2,1)S(1)}, u32[]{:S(2)}, u32[]{:S(2)}) collective-permute-start(bf16[16,16,512]{2,1,0:T(8,128)(2,1)S(1)} %all_to_all.15.same), channel_id=1, source_target_pairs={{0,8},{8,0},{16,24},{24,16},{32,40},{40,32},{48,56},{56,48},{64,72... | collective-permute-start | bytes 786440 | tf_op jit(solution)/shard_map/ppermute | solution.py:438
  36.3 10.2 %copy-start.1 = (bf16[64,6144]{1,0:T(8,128)(2,1)S(1)}, bf16[64,6144]{1,0:T(8,128)(2,1)}, u32[]{:S(2)}) copy-start(bf16[64,6144]{1,0:T(8,128)(2,1)} %modulation.1) | copy-start | bytes 2359300
  36.3 10.2 %copy-start.2 = (bf16[64,3072]{1,0:T(8,128)(2,1)S(1)}, bf16[64,3072]{1,0:T(8,128)(2,1)}, u32[]{:S(2)}) copy-start(bf16[64,3072]{1,0:T(8,128)(2,1)} %embed.1) | copy-start | bytes 1179652
  36.3 10.2 %copy-start.5 = (f32[3072]{0:T(1024)S(1)}, f32[3072]{0:T(1024)}, u32[]{:S(2)}) copy-start(f32[3072]{0:T(1024)} %param.22) | copy-start | bytes 36868
  39.0 2.7 %collective-permute-start.2 = (f32[16,256]{1,0:T(8,128)S(1)}, f32[16,256]{1,0:T(8,128)S(1)}, u32[]{:S(2)}, u32[]{:S(2)}) collective-permute-start(f32[16,256]{1,0:T(8,128)S(1)} %get-tuple-element.32), channel_id=1, source_target_pairs={{0,1},{2,3},{4,5},{6,7},{1,0},{3,2},{5,4},{7,6},{8,9},{10,11},{12,... | collective-permute-start | bytes 49160 | tf_op jit(solution)/shard_map/ppermute | solution.py:443
  39.4 2.3 %collective-permute-start.3 = (f32[16,256]{1,0:T(8,128)S(1)}, f32[16,256]{1,0:T(8,128)S(1)}, u32[]{:S(2)}, u32[]{:S(2)}) collective-permute-start(f32[16,256]{1,0:T(8,128)S(1)} %get-tuple-element.33), channel_id=1, source_target_pairs={{1,2},{3,4},{5,6},{2,1},{4,3},{6,5},{9,10},{11,12},{13,14},{10,9},... | collective-permute-start | bytes 49160 | tf_op jit(solution)/shard_map/ppermute | solution.py:443
  42.9 10.8 %all-to-all-start.2 = ((bf16[16,4,16,128]{3,2,1,0:T(8,128)(2,1)}), bf16[16,4,16,128]{3,2,1,0:T(8,128)(2,1)S(1)}, u32[]{:S(2)}, u32[]{:S(2)}) async-start(bf16[16,4,16,128]{3,2,1,0:T(8,128)(2,1)} %finish.1), calls=%async_computation.2 | async-start | bytes 524288 | tf_op jit(solution)/shard_map/all_to_all | solution.py:503
  47.6 2.3 %copy-start = (bf16[3072,768]{1,0:T(8,128)(2,1)S(1)}, bf16[3072,768]{1,0:T(8,128)(2,1)}, u32[]{:S(2)}) copy-start(bf16[3072,768]{1,0:T(8,128)(2,1)} %qkv_w.1) | copy-start | bytes 14155780
  49.9 21.3 %copy-start.6 = (f32[128]{0:T(128)S(1)}, f32[128]{0:T(128)}, u32[]{:S(2)}) copy-start(f32[128]{0:T(128)} %param.26) | copy-start | bytes 1540
  49.9 21.3 %copy-start.7 = (f32[128]{0:T(128)S(1)}, f32[128]{0:T(128)}, u32[]{:S(2)}) copy-start(f32[128]{0:T(128)} %param.27) | copy-start | bytes 1540
  54.4 3.8 %collective-permute-start.4 = (bf16[4,16,128]{2,1,0:T(8,128)(2,1)S(1)}, bf16[4,16,128]{2,1,0:T(8,128)(2,1)S(1)}, u32[]{:S(2)}, u32[]{:S(2)}) collective-permute-start(bf16[4,16,128]{2,1,0:T(8,128)(2,1)S(1)} %get-tuple-element.42), channel_id=1, source_target_pairs={{0,8},{8,0},{16,24},{24,16},{32,40},{40,32},{48,56},{56,48},{64,72... | collective-permute-start | bytes 49160 | tf_op jit(solution)/shard_map/ppermute | solution.py:438
  58.2 7.0 %collective-permute-start.7 = (bf16[4,16,128]{2,1,0:T(8,128)(2,1)S(1)}, bf16[4,16,128]{2,1,0:T(8,128)(2,1)S(1)}, u32[]{:S(2)}, u32[]{:S(2)}) collective-permute-start(bf16[4,16,128]{2,1,0:T(8,128)(2,1)S(1)} %add.85), channel_id=1, source_target_pairs={{0,3},{1,2},{2,1},{3,0},{4,7},{5,6},{6,5},{7,4},{8,11},{9,10},{10,... | collective-permute-start | bytes 49160 | tf_op jit(solution)/shard_map/ppermute | solution.py:438
  64.0 3.5 %collective-permute-start.6 = (bf16[4,16,128]{2,1,0:T(8,128)(2,1)S(1)}, bf16[4,16,128]{2,1,0:T(8,128)(2,1)S(1)}, u32[]{:S(2)}, u32[]{:S(2)}) collective-permute-start(bf16[4,16,128]{2,1,0:T(8,128)(2,1)S(1)} %add.85), channel_id=1, source_target_pairs={{0,2},{1,3},{2,0},{3,1},{4,6},{5,7},{6,4},{7,5},{8,10},{9,11},{10,... | collective-permute-start | bytes 49160 | tf_op jit(solution)/shard_map/ppermute | solution.py:438
  64.0 3.5 %collective-permute-start.5 = (bf16[4,16,128]{2,1,0:T(8,128)(2,1)S(1)}, bf16[4,16,128]{2,1,0:T(8,128)(2,1)S(1)}, u32[]{:S(2)}, u32[]{:S(2)}) collective-permute-start(bf16[4,16,128]{2,1,0:T(8,128)(2,1)S(1)} %add.85), channel_id=1, source_target_pairs={{0,1},{1,0},{2,3},{3,2},{4,5},{5,4},{6,7},{7,6},{8,9},{9,8},{10,11... | collective-permute-start | bytes 49160 | tf_op jit(solution)/shard_map/ppermute | solution.py:438
  67.6 7.1 %collective-permute-start.8 = (bf16[4,4,16,128]{3,2,1,0:T(8,128)(2,1)S(1)}, bf16[4,4,16,128]{3,2,1,0:T(8,128)(2,1)S(1)}, u32[]{:S(2)}, u32[]{:S(2)}) collective-permute-start(bf16[4,4,16,128]{3,2,1,0:T(8,128)(2,1)S(1)} %pad_maximum_fusion.tokens), channel_id=1, source_target_pairs={{0,4},{1,5},{2,6},{3,7},{4,0},{5,1},{6,2},{7,3},{8,12},{9,13},{10,... | collective-permute-start | bytes 196616 | tf_op jit(solution)/shard_map/ppermute | solution.py:438

commit v4 on v3

--- a/solution.py
+++ b/solution.py
@@ -276,12 +276,10 @@
 def mix_kernel(left, qkv_w, qkv_b, mix, rows):
     product = dot(left[...], qkv_w[...])
     cols = product.shape[1]
-    empty = jnp.zeros((64, cols), bf16)
     for clip in range(2):
         at = clip * 128
         high, low = split2(product[at : at + 64] + product[at + 64 : at + 128])
-        mix[clip, 0] = jnp.concatenate([high, empty, low, empty], axis=0)
-        mix[clip, 1] = jnp.concatenate([empty, high, empty, low], axis=0)
+        mix[clip] = jnp.concatenate([high, low], axis=0)
     tail = product[256:272]
     rows[...] = jnp.concatenate(
         [tail[0:2] + tail[2:4], tail[4:6] + qkv_b[...], jnp.zeros((4, cols), f32)], axis=0
@@ -300,11 +298,11 @@
             pl.BlockSpec((1, cols), lambda n: (0, n)),
         ],
         out_specs=[
-            pl.BlockSpec((2, 2, 256, cols), lambda n: (0, 0, 0, n)),
+            pl.BlockSpec((2, 128, cols), lambda n: (0, 0, n)),
             pl.BlockSpec((8, cols), lambda n: (0, n)),
         ],
         out_shape=[
-            jax.ShapeDtypeStruct((2, 2, 256, 768), bf16),
+            jax.ShapeDtypeStruct((2, 128, 768), bf16),
             jax.ShapeDtypeStruct((8, 768), f32),
         ],
         compiler_params=pltpu.CompilerParams(vmem_limit_bytes=12 * MIB),
@@ -318,7 +316,6 @@
     gains = q_gain[...] * factor, k_gain[...]
     count = own.shape[0]
     later = iota((count, 1), 0) // 16 % 4 >= lead
-    twice = jnp.concatenate([own, own], axis=1)
     spread = dot(own, gram[0]) + dot(own, gram[1]) + dot(own, gram[2])
     terms = (spread + gvec[0:1, :]) * own.astype(f32)
     low_lane = iota((count, 128), 1) < 64
@@ -328,7 +325,9 @@
         mine = jnp.where(low_lane == (half == 0), terms, 0.0)
         variance = jnp.sum(mine, axis=1, keepdims=True) + gvec[1:2, 0:1]
         scale = lax.rsqrt(jnp.maximum(variance, 0.0) + norm_eps)
-        mixed = jnp.where(later, dot(twice, mix[1, half]), dot(twice, mix[0, half]))
+        feats = own[:, half * 64 : half * 64 + 64]
+        twice = jnp.concatenate([feats, feats], axis=1)
+        mixed = jnp.where(later, dot(twice, mix[1]), dot(twice, mix[0]))
         qkv = scale * (mixed + slope) + offset
         for head in range(2):
             at = head * 384
@@ -339,71 +338,37 @@
             write(2, head, half, qkv[:, at + 256 : at + 384].astype(bf16))
 
 
-def project_kernel(table, tokens, mix, rows, gram, gvec, q_gain, k_gain, out):
-    bands = tokens.shape[0]
-
-    def write(kind, head, half, value):
-        for band in range(bands):
-            for frame in range(4):
-                at = (half * bands + band) * 16
-                out[kind, head, frame, at : at + 16, :] = value[
-                    (band * 4 + frame) * 16 : (band * 4 + frame) * 16 + 16
-                ]
-
-    own = tokens[...].reshape(bands * 64, 128)
-    project(table[20], own, mix, rows, gram, gvec, q_gain, k_gain, write)
-
-
-def project_near(table, tokens, mix, rows, gram, gvec, q_gain, k_gain):
-    smem = pl.BlockSpec(memory_space=pltpu.SMEM)
-    vmem = pl.BlockSpec(memory_space=pltpu.VMEM)
-    return pl.pallas_call(
-        project_kernel,
-        in_specs=[smem] + [vmem] * 7,
-        out_specs=vmem,
-        out_shape=jax.ShapeDtypeStruct((3, 2, 4, 128, 128), bf16),
-        compiler_params=pltpu.CompilerParams(vmem_limit_bytes=10 * MIB),
-        cost_estimate=pl.CostEstimate(flops=2 * 10**8, bytes_accessed=2 * 10**6, transcendentals=0),
-        name="project_near",
-    )(table, tokens, mix, rows, gram, gvec, q_gain, k_gain)
-
-
 def attend_kernel(
-    table, near, far, mix, rows, gram, gvec, q_gain, k_gain, out, parts
+    table, tokens, mix, rows, gram, gvec, q_gain, k_gain, out, parts
 ):
     lead = table[20]
-    own_band = lax.axis_index("head")
-    for kind in range(3):
-        for head in range(2):
+    def write(kind, head, half, value):
+        for band in range(8):
             for frame in range(4):
-                parts[kind, head, frame * 256 : frame * 256 + 128, :] = near[kind, head, frame]
-
-    def write(kind, head, half, value):
-        for band in range(4):
-            for frame in range(4):
-                at = frame * 256 + 128 + (half * 4 + band) * 16
+                at = frame * 256 + (half * 8 + band) * 16
                 parts[kind, head, at : at + 16, :] = value[
                     (band * 4 + frame) * 16 : (band * 4 + frame) * 16 + 16
                 ]
 
-    own = far[...].reshape(256, 128)
+    own = tokens[...].reshape(512, 128)
     project(lead, own, mix, rows, gram, gvec, q_gain, k_gain, write)
 
     def group(begin, end):
         for head in range(2):
             key = parts[1, head, begin * 256 : end * 256, :]
             value = parts[2, head, begin * 256 : end * 256, :]
+            wide = jnp.concatenate([value, jnp.ones_like(value)], axis=1)
             for frame in range(begin, end):
                 score = dot(parts[0, head, frame * 256 : frame * 256 + 256, :], key, NT)
                 top = jnp.max(score, axis=1, keepdims=True)
                 expo = jnp.exp2(score - top)
-                total = jnp.sum(expo, axis=1, keepdims=True)
-                result = (dot(expo.astype(bf16), value) / total).astype(bf16)
+                both = dot(expo.astype(bf16), wide)
+                result = (both[:, 0:128] / both[:, 128:256]).astype(bf16)
                 lanes = slice(head * 128, head * 128 + 128)
                 for half in range(2):
-                    for place in range(8):
-                        at = place // 4 * 128 + (half * 4 + place % 4) * 16
-                        out[own_band ^ place, frame, half, :, lanes] = result[at : at + 16]
+                    for band in range(8):
+                        at = (half * 8 + band) * 16
+                        out[7 - band, frame, half, :, lanes] = result[at : at + 16]
 
     for first in (1, 2, 3):
 
@@ -413,19 +378,19 @@
             group(first, 4)
 
 
-def attend(table, near, far, mix, rows, gram, gvec, q_gain, k_gain):
+def attend(table, tokens, mix, rows, gram, gvec, q_gain, k_gain):
     smem = pl.BlockSpec(memory_space=pltpu.SMEM)
     vmem = pl.BlockSpec(memory_space=pltpu.VMEM)
     return pl.pallas_call(
         attend_kernel,
-        in_specs=[smem] + [vmem] * 8,
+        in_specs=[smem] + [vmem] * 7,
         out_specs=vmem,
         out_shape=jax.ShapeDtypeStruct((8, 4, 2, 16, 256), bf16),
         scratch_shapes=[pltpu.VMEM((3, 2, 1024, 128), bf16)],
         compiler_params=pltpu.CompilerParams(vmem_limit_bytes=14 * MIB),
         cost_estimate=pl.CostEstimate(flops=10**9, bytes_accessed=3 * 10**6, transcendentals=1300000),
         name="attend",
-    )(table, near, far, mix, rows, gram, gvec, q_gain, k_gain)
+    )(table, tokens, mix, rows, gram, gvec, q_gain, k_gain)
 
 
 def neighbour(value, axis, step):
@@ -469,7 +434,9 @@
     latent_rows = latent_weight.T
 
     weight = conv_weight.transpose(0, 1, 2, 4, 3).reshape(27, conv_weight.shape[4], -1)
-    parts = lax.all_to_all(fold_tap(weight, latent_rows, heads), "head", 0, 0)
+    parts = lax.all_to_all(
+        fold_tap(weight, latent_rows, heads), "head", 0, 0, axis_index_groups=[list(range(heads))[::-1]]
+    )
     prev = neighbour(video_feat[2:], "seq", 1)
     tap = jnp.sum(parts.astype(f32), axis=0).astype(bf16)
 
@@ -497,7 +464,7 @@
 
     left, gram, gvec = scale_embedding(member, modulation, embed_weight, embed_bias)
 
-    tap, table, prev = lax.optimization_barrier((tap, table, prev))
+    tap, table = lax.optimization_barrier((tap, table))
     chips = seqs // 2
     cores = [[2 * chip + core for chip in range(chips)] for core in range(2)]
     over_chips = lambda value: lax.all_to_all(value, "seq", 0, 0, axis_index_groups=cores)
@@ -515,11 +482,11 @@
     mine, other = route(table, frames_all)
     mine, other, mixed = lax.optimization_barrier((mine, other, mixed))
     slots = mine + swap(other, "seq", 1)
-    near = jnp.stack(swap3(slots, "head", 1))
-    far = swap(near, "head", 4)
+    tokens = lax.all_to_all(
+        jnp.broadcast_to(slots[None], (heads,) + slots.shape), "head", 0, 0, axis_index_groups=[list(range(heads))[::-1]]
+    )
     gains = q_gain.reshape(1, -1), k_gain.reshape(1, -1)
-    ready = project_near(table, near, *mixed, *gains)
-    out = attend(table, ready, far, *mixed, *gains)
+    out = attend(table, tokens, *mixed, *gains)
     return out.reshape(heads * frames * 32, 256)
 
 

time: 81.7 us -> 77.6 us (0.950); the launches traced: 80.1 us -> 76.9 us
  waiting for transfers between devices: 11.1 us -> 8.57 us
  Pallas kernels: 15.9 us -> 13.8 us
  starting transfers between devices: 34 us -> 35.2 us
    ppermute x6 -> x2, starting transfers between devices: 16.4 us -> 7.53 us  [swap(): lax.ppermute(value, axis, [(i, i ^ mask) for i in range(lax.axis_size(axi...]
    all_to_all x1 -> x2, starting transfers between devices: 3.53 us -> 10.6 us  [per_device(): lax.all_to_all(value, 'seq', 0, 0, axis_index_groups=cores)]
    ppermute x6 -> x2, waiting for transfers between devices: 6.49 us -> 1.42 us  [swap(): lax.ppermute(value, axis, [(i, i ^ mask) for i in range(lax.axis_size(axi...]
    pallas_call x2 -> x1, Pallas kernels: 6.98 us -> 4.98 us  [attend(): pl.pallas_call(attend_kernel, in_specs=[smem] + [vmem] * 7, out_specs=vme...]
    all_to_all x1 -> x2, waiting for transfers between devices: 1.56 us -> 3.49 us  [per_device(): lax.all_to_all(value, 'seq', 0, 0, axis_index_groups=cores)]
    all_to_all x1, waiting for transfers between devices: 1.5 us -> 2.96 us  [per_device(): lax.all_to_all(fold_tap(weight, latent_rows, heads), 'head', 0, 0, axis_i...]
    ppermute x1, starting transfers between devices: 4.05 us -> 5.49 us  [neighbour(): return lax.ppermute(value, axis, pairs)]
  transfers between devices with their start and end apart: 11 -> 8, of which waited for: 8 -> 6; matrix products, arithmetic and copies ran while one was open for 3% -> 3% of each run, Pallas kernels for 7% -> 5%
where the time goes in v4:
time: 77.6 us; the launch traced here: 76.9 us
  starting transfers between devices  35.2 us (45%)
  Pallas kernels  13.8 us (18%)
  blocking collectives  13.8 us (18%)
  waiting for transfers between devices  8.57 us (11%)
  local copies, waits for them, and re-layouts  3.41 us (4%)
  other arithmetic  1.91 us (2%)
    all_to_all x1, blocking collectives, per_device(): lax.all_to_all(jnp.broadcast_to(slots[None], (heads,) + slots.shape), 'he...  13.8 us
    all_to_all x2, starting transfers between devices, per_device(): lax.all_to_all(value, 'seq', 0, 0, axis_index_groups=cores)  10.6 us
    all_to_all x1, starting transfers between devices, per_device(): lax.all_to_all(fold_tap(weight, latent_rows, heads), 'head', 0, 0, axis_i...  9.73 us
    ppermute x2, starting transfers between devices, swap(): lax.ppermute(value, axis, [(i, i ^ mask) for i in range(lax.axis_size(axi...  7.53 us
    ppermute x1, starting transfers between devices, neighbour(): return lax.ppermute(value, axis, pairs)  5.49 us
    pallas_call x1, Pallas kernels, attend(): pl.pallas_call(attend_kernel, in_specs=[smem] + [vmem] * 7, out_specs=vme...  4.98 us
    all_to_all x2, waiting for transfers between devices, per_device(): lax.all_to_all(value, 'seq', 0, 0, axis_index_groups=cores)  3.49 us
    all_to_all x1, waiting for transfers between devices, per_device(): lax.all_to_all(fold_tap(weight, latent_rows, heads), 'head', 0, 0, axis_i...  2.96 us
  transfers between devices with their start and end apart: 8, of which 6 were waited for; matrix products, arithmetic and copies ran while one was open for 3% of the time, Pallas kernels for 5%

profile of v4, /device:TPU:1, one launch (start us, length us, event | category | flops | bytes accessed | tf_op | source)
XLA Modules:
  0.0 76.9 jit_solution(8442141998376792121)
XLA Ops:
  0.0 1.7 %fold_tap.1 = bf16[8,16,512]{2,1,0:T(8,128)(2,1)} custom-call(bf16[27,64,512]{2,1,0:T(8,128)(2,1)} %bitcast.21, bf16[16,512]{1,0:T(8,128)(2,1)} %bitcast.15), custom_call_target="tpu_custom_call" | custom-call | flops 1000000 | bytes 150000 | tf_op jit(solution)/shard_map/fold_tap/pallas_call | solution.py:53
  1.8 9.7 %all-to-all-start = ((bf16[8,16,512]{2,1,0:T(8,128)(2,1)}), bf16[8,16,512]{2,1,0:T(8,128)(2,1)S(1)}, u32[]{:S(2)}, u32[]{:S(2)}) async-start(bf16[8,16,512]{2,1,0:T(8,128)(2,1)} %fold_tap.1), calls=%async_computation | async-start | bytes 262144 | tf_op jit(solution)/shard_map/all_to_all | solution.py:437
  12.8 0.6 pad_add_fusion.table
  13.4 3.0 %all-to-all-done = bf16[8,16,512]{2,1,0:T(8,128)(2,1)S(1)} async-done(((bf16[8,16,512]{2,1,0:T(8,128)(2,1)}), bf16[8,16,512]{2,1,0:T(8,128)(2,1)S(1)}, u32[]{:S(2)}, u32[]{:S(2)}) %all-to-all-start) | async-done | bytes 131104 | tf_op jit(solution)/shard_map/all_to_all | solution.py:437
  16.4 0.7 broadcast_in_dim.45
  17.1 6.8 %all-to-all-start.1 = ((bf16[16,16,512]{2,1,0:T(8,128)(2,1)}), bf16[16,16,512]{2,1,0:T(8,128)(2,1)S(1)}, u32[]{:S(2)}, u32[]{:S(2)}) async-start(bf16[16,16,512]{2,1,0:T(8,128)(2,1)} %broadcast_in_dim.45), calls=%async_computation.1 | async-start | bytes 524288 | tf_op jit(solution)/shard_map/all_to_all | solution.py:470
  23.9 5.5 %collective-permute-start = (bf16[2,2,64,512]{3,2,1,0:T(8,128)(2,1)S(1)}, bf16[2,2,64,512]{3,2,1,0:T(8,128)(2,1)S(1)}, u32[]{:S(2)}, u32[]{:S(2)}) collective-permute-start(bf16[2,2,64,512]{3,2,1,0:T(8,128)(2,1)S(1)} %slice.3), channel_id=1, source_target_pairs={{0,8},{8,16},{16,24},{24,32},{32,40},{40,48},{48,56},{56,64},{64,7... | collective-permute-start | bytes 786440 | tf_op jit(solution)/shard_map/ppermute | solution.py:399
  29.4 1.8 %all-to-all-done.1.same = bf16[16,16,512]{2,1,0:T(8,128)(2,1)S(1)} async-done(((bf16[16,16,512]{2,1,0:T(8,128)(2,1)}), bf16[16,16,512]{2,1,0:T(8,128)(2,1)S(1)}, u32[]{:S(2)}, u32[]{:S(2)}) %all-to-all-start.1) | async-done | bytes 262176 | tf_op jit(solution)/shard_map/all_to_all | solution.py:470
  31.2 3.2 %collective-permute-start.1 = (bf16[16,16,512]{2,1,0:T(8,128)(2,1)S(1)}, bf16[16,16,512]{2,1,0:T(8,128)(2,1)S(1)}, u32[]{:S(2)}, u32[]{:S(2)}) collective-permute-start(bf16[16,16,512]{2,1,0:T(8,128)(2,1)S(1)} %all-to-all-done.1.same), channel_id=1, source_target_pairs={{0,8},{8,0},{16,24},{24,16},{32,40},{40,32},{48,56},{56,48},{64,72... | collective-permute-start | bytes 786440 | tf_op jit(solution)/shard_map/ppermute | solution.py:403
  35.6 1.6 %convolve.1 = (f32[16,512]{1,0:T(8,128)S(1)}, f32[16,256]{1,0:T(8,128)S(1)}, f32[16,256]{1,0:T(8,128)S(1)}) custom-call(s32[21]{0:T(128)S(1)} %pad_add_fusion.table, bf16[768,512]{1,0:T(8,128)(2,1)S(1)} %get-tuple-element.26.act, bf16[16,16,512]{2,1,0:T(8,128)(2,1)S(1)} %all-to-all-done.1.same, bf16[16,16,512]{2,1,0:T(8,128)(2,1)S(1)} %collective-permute-done.1.other, ...), custom_call_target="tpu_custom_call" | custom-call | flops 400000000 | bytes 2000000 | tf_op jit(solution)/shard_map/convolve/pallas_call | solution.py:138
  37.2 1.2 %collective-permute-start.2 = (f32[16,256]{1,0:T(8,128)S(1)}, f32[16,256]{1,0:T(8,128)S(1)}, u32[]{:S(2)}, u32[]{:S(2)}) collective-permute-start(f32[16,256]{1,0:T(8,128)S(1)} %get-tuple-element.30), channel_id=1, source_target_pairs={{0,1},{2,3},{4,5},{6,7},{1,0},{3,2},{5,4},{7,6},{8,9},{10,11},{12,... | collective-permute-start | bytes 49160 | tf_op jit(solution)/shard_map/ppermute | solution.py:408
  38.4 0.7 collective-permute-start.3
  39.1 0.7 collective-permute-done.2.first
  39.8 1.2 %finish.1 = bf16[16,4,16,128]{3,2,1,0:T(8,128)(2,1)} custom-call(f32[16,512]{1,0:T(8,128)S(1)} %get-tuple-element.29.own, f32[16,256]{1,0:T(8,128)S(1)} %collective-permute-done.2.first, f32[16,256]{1,0:T(8,128)S(1)} %collective-permute-done.3.second), custom_call_target="tpu_custom_call" | custom-call | flops 10000000 | bytes 1000000 | tf_op jit(solution)/shard_map/finish/pallas_call | solution.py:177
  41.1 3.8 %all-to-all-start.2 = ((bf16[16,4,16,128]{3,2,1,0:T(8,128)(2,1)}), bf16[16,4,16,128]{3,2,1,0:T(8,128)(2,1)S(1)}, u32[]{:S(2)}, u32[]{:S(2)}) async-start(bf16[16,4,16,128]{3,2,1,0:T(8,128)(2,1)} %finish.1), calls=%async_computation.2 | async-start | bytes 524288 | tf_op jit(solution)/shard_map/all_to_all | solution.py:470
  45.0 1.0 %scale_embedding.1 = (bf16[272,3072]{1,0:T(8,128)(2,1)S(1)}, bf16[3,128,128]{2,1,0:T(8,128)(2,1)S(1)}, f32[8,128]{1,0:T(8,128)S(1)}) custom-call(bf16[8,64]{1,0:T(8,128)(2,1)S(1)} %add_convert_fusion.member, bf16[64,6144]{1,0:T(8,128)(2,1)S(1)} %copy-done.1, bf16[64,3072]{1,0:T(8,128)(2,1)S(1)} %copy-done.2, f32[1,3072]{1,0:T(1,128)S(1)} %bitcast.17), custom_call_target="tpu_custom_call" | custom-call | flops 100000000 | bytes 3000000 | tf_op jit(solution)/shard_map/scale_embedding/pallas_call | solution.py:261
  46.1 2.3 %copy-done = bf16[3072,768]{1,0:T(8,128)(2,1)S(1)} copy-done((bf16[3072,768]{1,0:T(8,128)(2,1)S(1)}, bf16[3072,768]{1,0:T(8,128)(2,1)}, u32[]{:S(2)}) %copy-start) | copy-done | bytes 4718616
  48.4 2.2 %mix_weights.1 = (bf16[2,128,768]{2,1,0:T(8,128)(2,1)S(1)}, f32[8,768]{1,0:T(8,128)S(1)}) custom-call(bf16[272,3072]{1,0:T(8,128)(2,1)S(1)} %get-tuple-element.34.left, bf16[3072,768]{1,0:T(8,128)(2,1)S(1)} %copy-done, f32[1,768]{1,0:T(1,128)S(1)} %reshape.62.qkv_b), custom_call_target="tpu_custom_call" | custom-call | flops 1300000000 | bytes 6000000 | tf_op jit(solution)/shard_map/mix_weights/pallas_call | solution.py:292
  50.6 1.7 %all-to-all-done.2.frames = bf16[16,4,16,128]{3,2,1,0:T(8,128)(2,1)S(1)} async-done(((bf16[16,4,16,128]{3,2,1,0:T(8,128)(2,1)}), bf16[16,4,16,128]{3,2,1,0:T(8,128)(2,1)S(1)}, u32[]{:S(2)}, u32[]{:S(2)}) %all-to-all-start.2) | async-done | bytes 262176 | tf_op jit(solution)/shard_map/all_to_all | solution.py:470
  52.2 0.7 route.1
  52.9 4.4 %collective-permute-start.4 = (bf16[4,16,128]{2,1,0:T(8,128)(2,1)S(1)}, bf16[4,16,128]{2,1,0:T(8,128)(2,1)S(1)}, u32[]{:S(2)}, u32[]{:S(2)}) collective-permute-start(bf16[4,16,128]{2,1,0:T(8,128)(2,1)S(1)} %get-tuple-element.40), channel_id=1, source_target_pairs={{0,8},{8,0},{16,24},{24,16},{32,40},{40,32},{48,56},{56,48},{64,72... | collective-permute-start | bytes 49160 | tf_op jit(solution)/shard_map/ppermute | solution.py:403
  57.3 0.8 %collective-permute-done.4 = bf16[4,16,128]{2,1,0:T(8,128)(2,1)S(1)} collective-permute-done((bf16[4,16,128]{2,1,0:T(8,128)(2,1)S(1)}, bf16[4,16,128]{2,1,0:T(8,128)(2,1)S(1)}, u32[]{:S(2)}, u32[]{:S(2)}) %collective-permute-start.4) | collective-permute-done | bytes 16416 | tf_op jit(solution)/shard_map/ppermute | solution.py:403
  58.2 13.8 %all_to_all.20.tokens = bf16[8,4,16,128]{3,2,1,0:T(8,128)(2,1)S(1)} all-to-all(bf16[8,4,16,128]{3,2,1,0:T(8,128)(2,1)S(1)} %broadcast_in_dim.75), channel_id=1, replica_groups={{7,6,5,4,3,2,1,0},{15,14,13,12,11,10,9,8},{23,22,21,20,19,18,17,16},{31..., dimensions={0} | all-to-all | bytes 262144 | tf_op jit(solution)/shard_map/all_to_all | solution.py:485
  72.0 5.0 %attend.1 = bf16[8,4,2,16,256]{4,3,2,1,0:T(8,128)(2,1)} custom-call(s32[21]{0:T(128)S(1)} %pad_add_fusion.table, bf16[8,4,16,128]{3,2,1,0:T(8,128)(2,1)S(1)} %all_to_all.20.tokens, bf16[2,128,768]{2,1,0:T(8,128)(2,1)S(1)} %get-tuple-element.41.mix, f32[8,768]{1,0:T(8,128)S(1)} %get-tuple-element.42.rows, bf16[3,128,128]{2,1,0:T(8,128)(2,1)S(1)} %get-tuple-element.43.gram, ...), custom_call_target="tpu_custom_call" | custom-call | flops 1000000000 | bytes 3000000 | tf_op jit(solution)/shard_map/attend/pallas_call | solution.py:384
  (48 shorter events, 2.7 us)
Async XLA Ops:
  0.0 11.5 %copy-start.11 = (s32[64]{0:T(128)S(1)}, s32[64]{0:T(128)}, u32[]{:S(2)}) copy-start(s32[64]{0:T(128)} %param.15) | copy-start | bytes 772
  0.0 12.0 %copy-start.9 = (s32[64]{0:T(128)S(1)}, s32[64]{0:T(128)}, u32[]{:S(2)}) copy-start(s32[64]{0:T(128)} %param.16) | copy-start | bytes 772
  0.0 23.9 %copy-start.3 = (bf16[4,2,64,512]{3,2,1,0:T(8,128)(2,1)S(1)}, bf16[4,2,64,512]{3,2,1,0:T(8,128)(2,1)}, u32[]{:S(2)}) copy-start(bf16[4,2,64,512]{3,2,1,0:T(8,128)(2,1)} %main.1) | copy-start | bytes 1572868
  0.0 34.4 %copy-start.12 = (f32[16]{0:T(128)S(1)}, f32[16]{0:T(128)}, u32[]{:S(2)}) copy-start(f32[16]{0:T(128)} %param.20) | copy-start | bytes 196
  0.0 34.5 %copy-start.4 = (bf16[512,16]{0,1:T(8,128)(2,1)S(1)}, bf16[512,16]{0,1:T(8,128)(2,1)}, u32[]{:S(2)}) copy-start(bf16[512,16]{0,1:T(8,128)(2,1)} %param.19) | copy-start | bytes 49156
  0.0 34.5 %copy-start.6 = (f32[512]{0:T(512)S(1)}, f32[512]{0:T(512)}, u32[]{:S(2)}) copy-start(f32[512]{0:T(512)} %param.18) | copy-start | bytes 6148
  1.8 14.6 %all-to-all-start = ((bf16[8,16,512]{2,1,0:T(8,128)(2,1)}), bf16[8,16,512]{2,1,0:T(8,128)(2,1)S(1)}, u32[]{:S(2)}, u32[]{:S(2)}) async-start(bf16[8,16,512]{2,1,0:T(8,128)(2,1)} %fold_tap.1), calls=%async_computation | async-start | bytes 262144 | tf_op jit(solution)/shard_map/all_to_all | solution.py:437
  17.1 14.1 %all-to-all-start.1 = ((bf16[16,16,512]{2,1,0:T(8,128)(2,1)}), bf16[16,16,512]{2,1,0:T(8,128)(2,1)S(1)}, u32[]{:S(2)}, u32[]{:S(2)}) async-start(bf16[16,16,512]{2,1,0:T(8,128)(2,1)} %broadcast_in_dim.45), calls=%async_computation.1 | async-start | bytes 524288 | tf_op jit(solution)/shard_map/all_to_all | solution.py:470
  23.9 15.3 %copy-start.10 = (f32[768]{0:T(1024)S(1)}, f32[768]{0:T(1024)}, u32[]{:S(2)}) copy-start(f32[768]{0:T(1024)} %param.25) | copy-start | bytes 9220
  23.9 10.6 %collective-permute-start = (bf16[2,2,64,512]{3,2,1,0:T(8,128)(2,1)S(1)}, bf16[2,2,64,512]{3,2,1,0:T(8,128)(2,1)S(1)}, u32[]{:S(2)}, u32[]{:S(2)}) collective-permute-start(bf16[2,2,64,512]{3,2,1,0:T(8,128)(2,1)S(1)} %slice.3), channel_id=1, source_target_pairs={{0,8},{8,16},{16,24},{24,32},{32,40},{40,48},{48,56},{56,64},{64,7... | collective-permute-start | bytes 786440 | tf_op jit(solution)/shard_map/ppermute | solution.py:399
  31.2 4.3 %collective-permute-start.1 = (bf16[16,16,512]{2,1,0:T(8,128)(2,1)S(1)}, bf16[16,16,512]{2,1,0:T(8,128)(2,1)S(1)}, u32[]{:S(2)}, u32[]{:S(2)}) collective-permute-start(bf16[16,16,512]{2,1,0:T(8,128)(2,1)S(1)} %all-to-all-done.1.same), channel_id=1, source_target_pairs={{0,8},{8,0},{16,24},{24,16},{32,40},{40,32},{48,56},{56,48},{64,72... | collective-permute-start | bytes 786440 | tf_op jit(solution)/shard_map/ppermute | solution.py:403
  34.5 10.5 %copy-start.1 = (bf16[64,6144]{1,0:T(8,128)(2,1)S(1)}, bf16[64,6144]{1,0:T(8,128)(2,1)}, u32[]{:S(2)}) copy-start(bf16[64,6144]{1,0:T(8,128)(2,1)} %modulation.1) | copy-start | bytes 2359300
  34.5 10.5 %copy-start.2 = (bf16[64,3072]{1,0:T(8,128)(2,1)S(1)}, bf16[64,3072]{1,0:T(8,128)(2,1)}, u32[]{:S(2)}) copy-start(bf16[64,3072]{1,0:T(8,128)(2,1)} %embed.1) | copy-start | bytes 1179652
  34.5 10.5 %copy-start.5 = (f32[3072]{0:T(1024)S(1)}, f32[3072]{0:T(1024)}, u32[]{:S(2)}) copy-start(f32[3072]{0:T(1024)} %param.22) | copy-start | bytes 36868
  37.2 2.7 %collective-permute-start.2 = (f32[16,256]{1,0:T(8,128)S(1)}, f32[16,256]{1,0:T(8,128)S(1)}, u32[]{:S(2)}, u32[]{:S(2)}) collective-permute-start(f32[16,256]{1,0:T(8,128)S(1)} %get-tuple-element.30), channel_id=1, source_target_pairs={{0,1},{2,3},{4,5},{6,7},{1,0},{3,2},{5,4},{7,6},{8,9},{10,11},{12,... | collective-permute-start | bytes 49160 | tf_op jit(solution)/shard_map/ppermute | solution.py:408
  38.4 1.5 %collective-permute-start.3 = (f32[16,256]{1,0:T(8,128)S(1)}, f32[16,256]{1,0:T(8,128)S(1)}, u32[]{:S(2)}, u32[]{:S(2)}) collective-permute-start(f32[16,256]{1,0:T(8,128)S(1)} %get-tuple-element.31), channel_id=1, source_target_pairs={{1,2},{3,4},{5,6},{2,1},{4,3},{6,5},{9,10},{11,12},{13,14},{10,9},... | collective-permute-start | bytes 49160 | tf_op jit(solution)/shard_map/ppermute | solution.py:408
  41.1 11.2 %all-to-all-start.2 = ((bf16[16,4,16,128]{3,2,1,0:T(8,128)(2,1)}), bf16[16,4,16,128]{3,2,1,0:T(8,128)(2,1)S(1)}, u32[]{:S(2)}, u32[]{:S(2)}) async-start(bf16[16,4,16,128]{3,2,1,0:T(8,128)(2,1)} %finish.1), calls=%async_computation.2 | async-start | bytes 524288 | tf_op jit(solution)/shard_map/all_to_all | solution.py:470
  46.0 2.3 %copy-start = (bf16[3072,768]{1,0:T(8,128)(2,1)S(1)}, bf16[3072,768]{1,0:T(8,128)(2,1)}, u32[]{:S(2)}) copy-start(bf16[3072,768]{1,0:T(8,128)(2,1)} %qkv_w.1) | copy-start | bytes 14155780
  48.4 23.6 %copy-start.7 = (f32[128]{0:T(128)S(1)}, f32[128]{0:T(128)}, u32[]{:S(2)}) copy-start(f32[128]{0:T(128)} %param.26) | copy-start | bytes 1540
  48.4 23.6 %copy-start.8 = (f32[128]{0:T(128)S(1)}, f32[128]{0:T(128)}, u32[]{:S(2)}) copy-start(f32[128]{0:T(128)} %param.27) | copy-start | bytes 1540
  52.9 5.2 %collective-permute-start.4 = (bf16[4,16,128]{2,1,0:T(8,128)(2,1)S(1)}, bf16[4,16,128]{2,1,0:T(8,128)(2,1)S(1)}, u32[]{:S(2)}, u32[]{:S(2)}) collective-permute-start(bf16[4,16,128]{2,1,0:T(8,128)(2,1)S(1)} %get-tuple-element.40), channel_id=1, source_target_pairs={{0,8},{8,0},{16,24},{24,16},{32,40},{40,32},{48,56},{56,48},{64,72... | collective-permute-start | bytes 49160 | tf_op jit(solution)/shard_map/ppermute | solution.py:403

commit v5 on v4

--- a/solution.py
+++ b/solution.py
@@ -103,8 +103,10 @@
         pair_at = pl.multiple_of(chip * 32 + 16 - core * 16, 16)
         weight[pl.ds(own_at, 16), :] = same[chip]
         weight[pl.ds(pair_at, 16), :] = other[chip]
-    for frame in range(6):
-        taps[frame] = dot(weight[0:432, :], act[frame * 128 : frame * 128 + 128, :], NT)
+    for frame in range(0, 6, 2):
+        pair = dot(weight[0:432, :], act[frame * 128 : frame * 128 + 256, :], NT)
+        taps[frame] = pair[:, 0:128]
+        taps[frame + 1] = pair[:, 128:256]
     column = iota((16, 128), 1) % 64
 
     def across(parts):
@@ -313,7 +315,7 @@
 
 def project(lead, own, mix, rows, gram, gvec, q_gain, k_gain, write):
     factor = math.log2(math.e) / math.sqrt(128)
-    gains = q_gain[...] * factor, k_gain[...]
+    gain = q_gain[...] * k_gain[...] * factor
     count = own.shape[0]
     later = iota((count, 1), 0) // 16 % 4 >= lead
     spread = dot(own, gram[0]) + dot(own, gram[1]) + dot(own, gram[2])
@@ -334,7 +336,8 @@
             for kind in range(2):
                 part = qkv[:, at + kind * 128 : at + kind * 128 + 128]
                 norm = lax.rsqrt(jnp.mean(part * part, axis=1, keepdims=True) + norm_eps)
-                write(kind, head, half, (part * norm * gains[kind]).astype(bf16))
+                part = part * norm
+                write(kind, head, half, (part * gain if kind == 0 else part).astype(bf16))
             write(2, head, half, qkv[:, at + 256 : at + 384].astype(bf16))
 
 
@@ -469,9 +472,10 @@
     cores = [[2 * chip + core for chip in range(chips)] for core in range(2)]
     over_chips = lambda value: lax.all_to_all(value, "seq", 0, 0, axis_index_groups=cores)
     same = over_chips(jnp.broadcast_to(tap[None], (chips,) + tap.shape))
-    folded = same, swap(same, "seq", 1)
     mix, rows = mix_weights(left, qkv_weight, qkv_bias)
     mixed = mix, rows, gram, gvec
+    same, mixed = lax.optimization_barrier((same, mixed))
+    folded = same, swap(same, "seq", 1)
     act, base = prepare(video_feat, prev, latent_rows, conv_bias, latent_bias)
 
     own, first, second = convolve(table, act, folded, base)
@@ -480,7 +484,6 @@
     pieces = finish(own, first, second, chips)
     frames_all = over_chips(pieces)
     mine, other = route(table, frames_all)
-    mine, other, mixed = lax.optimization_barrier((mine, other, mixed))
     slots = mine + swap(other, "seq", 1)
     tokens = lax.all_to_all(
         jnp.broadcast_to(slots[None], (heads,) + slots.shape), "head", 0, 0, axis_index_groups=[list(range(heads))[::-1]]

time: 77.6 us -> 75.7 us (0.976)
  blocking collectives: 13.8 us -> 25.4 us
  starting transfers between devices: 35.2 us -> 27.2 us
  waiting for transfers between devices: 8.57 us -> 4.04 us
  Pallas kernels: 13.8 us -> 12.4 us
    all_to_all x0 -> x1, blocking collectives: none -> 11.2 us  [per_device(): lax.all_to_all(value, 'seq', 0, 0, axis_index_groups=cores)]
    all_to_all x2 -> x1, starting transfers between devices: 10.6 us -> 6.46 us  [per_device(): lax.all_to_all(value, 'seq', 0, 0, axis_index_groups=cores)]
    all_to_all x1, waiting for transfers between devices: 2.96 us -> 0.01 us  [per_device(): lax.all_to_all(fold_tap(weight, latent_rows, heads), 'head', 0, 0, axis_i...]
    ppermute x2, starting transfers between devices: 7.53 us -> 5.03 us  [swap(): lax.ppermute(value, axis, [(i, i ^ mask) for i in range(lax.axis_size(axi...]
    all_to_all x2 -> x1, waiting for transfers between devices: 3.49 us -> 1.82 us  [per_device(): lax.all_to_all(value, 'seq', 0, 0, axis_index_groups=cores)]
    ppermute x1, starting transfers between devices: 5.49 us -> 4.05 us  [neighbour(): return lax.ppermute(value, axis, pairs)]
  transfers between devices with their start and end apart: 8 -> 7, of which waited for: 6 -> 4; matrix products, arithmetic and copies ran while one was open for 3% -> 4% of each run, Pallas kernels for 5% -> 5%
where the time goes in v5:
time: 75.7 us; the launch traced here: 74.8 us
  starting transfers between devices  27.2 us (36%)
  blocking collectives  25.4 us (34%)
  Pallas kernels  12.4 us (16%)
  waiting for transfers between devices  4.04 us (5%)
  local copies, waits for them, and re-layouts  3.4 us (4%)
  other arithmetic  2.08 us (3%)
    all_to_all x1, blocking collectives, per_device(): lax.all_to_all(jnp.broadcast_to(slots[None], (heads,) + slots.shape), 'he...  14.2 us
    all_to_all x1, blocking collectives, per_device(): lax.all_to_all(value, 'seq', 0, 0, axis_index_groups=cores)  11.2 us
    all_to_all x1, starting transfers between devices, per_device(): lax.all_to_all(fold_tap(weight, latent_rows, heads), 'head', 0, 0, axis_i...  9.73 us
    all_to_all x1, starting transfers between devices, per_device(): lax.all_to_all(value, 'seq', 0, 0, axis_index_groups=cores)  6.46 us
    ppermute x2, starting transfers between devices, swap(): lax.ppermute(value, axis, [(i, i ^ mask) for i in range(lax.axis_size(axi...  5.03 us
    pallas_call x1, Pallas kernels, attend(): pl.pallas_call(attend_kernel, in_specs=[smem] + [vmem] * 7, out_specs=vme...  4.52 us
    ppermute x1, starting transfers between devices, neighbour(): return lax.ppermute(value, axis, pairs)  4.05 us
    unnamed x26, local copies, waits for them, and re-layouts  2.38 us
  transfers between devices with their start and end apart: 7, of which 4 were waited for; matrix products, arithmetic and copies ran while one was open for 4% of the time, Pallas kernels for 5%

profile of v5, /device:TPU:1, one launch (start us, length us, event | category | flops | bytes accessed | tf_op | source)
XLA Modules:
  0.0 74.8 jit_solution(18129223163334809811)
XLA Ops:
  0.0 1.8 %fold_tap.1 = bf16[8,16,512]{2,1,0:T(8,128)(2,1)} custom-call(bf16[27,64,512]{2,1,0:T(8,128)(2,1)} %bitcast.21, bf16[16,512]{1,0:T(8,128)(2,1)} %bitcast.15), custom_call_target="tpu_custom_call" | custom-call | flops 1000000 | bytes 150000 | tf_op jit(solution)/shard_map/fold_tap/pallas_call | solution.py:53
  1.8 9.7 %all-to-all-start = ((bf16[8,16,512]{2,1,0:T(8,128)(2,1)}), bf16[8,16,512]{2,1,0:T(8,128)(2,1)S(1)}, u32[]{:S(2)}, u32[]{:S(2)}) async-start(bf16[8,16,512]{2,1,0:T(8,128)(2,1)} %fold_tap.1), calls=%async_computation | async-start | bytes 262144 | tf_op jit(solution)/shard_map/all_to_all | solution.py:440
  11.6 4.0 %collective-permute-start = (bf16[2,2,64,512]{3,2,1,0:T(8,128)(2,1)S(1)}, bf16[2,2,64,512]{3,2,1,0:T(8,128)(2,1)S(1)}, u32[]{:S(2)}, u32[]{:S(2)}) collective-permute-start(bf16[2,2,64,512]{3,2,1,0:T(8,128)(2,1)S(1)} %slice.3), channel_id=1, source_target_pairs={{0,8},{8,16},{16,24},{24,32},{32,40},{40,48},{48,56},{56,64},{64,7... | collective-permute-start | bytes 786440 | tf_op jit(solution)/shard_map/ppermute | solution.py:402
  15.8 0.7 fusion.1
  17.0 0.7 pad_add_fusion.table
  17.9 0.7 broadcast_in_dim.45
  18.6 6.5 %all-to-all-start.1 = ((bf16[16,16,512]{2,1,0:T(8,128)(2,1)}), bf16[16,16,512]{2,1,0:T(8,128)(2,1)S(1)}, u32[]{:S(2)}, u32[]{:S(2)}) async-start(bf16[16,16,512]{2,1,0:T(8,128)(2,1)} %broadcast_in_dim.45), calls=%async_computation.1 | async-start | bytes 524288 | tf_op jit(solution)/shard_map/all_to_all | solution.py:473
  25.2 1.0 %scale_embedding.1 = (bf16[272,3072]{1,0:T(8,128)(2,1)S(1)}, bf16[3,128,128]{2,1,0:T(8,128)(2,1)S(1)}, f32[8,128]{1,0:T(8,128)S(1)}) custom-call(bf16[8,64]{1,0:T(8,128)(2,1)S(1)} %add_convert_fusion.member, bf16[64,6144]{1,0:T(8,128)(2,1)S(1)} %copy-done.1, bf16[64,3072]{1,0:T(8,128)(2,1)S(1)} %copy-done.2, f32[1,3072]{1,0:T(1,128)S(1)} %bitcast.17), custom_call_target="tpu_custom_call" | custom-call | flops 100000000 | bytes 3000000 | tf_op jit(solution)/shard_map/scale_embedding/pallas_call | solution.py:263
  26.2 2.3 %copy-done = bf16[3072,768]{1,0:T(8,128)(2,1)S(1)} copy-done((bf16[3072,768]{1,0:T(8,128)(2,1)S(1)}, bf16[3072,768]{1,0:T(8,128)(2,1)}, u32[]{:S(2)}) %copy-start) | copy-done | bytes 4718616
  28.5 2.2 %mix_weights.1 = (bf16[2,128,768]{2,1,0:T(8,128)(2,1)S(1)}, f32[8,768]{1,0:T(8,128)S(1)}) custom-call(bf16[272,3072]{1,0:T(8,128)(2,1)S(1)} %get-tuple-element.27.left, bf16[3072,768]{1,0:T(8,128)(2,1)S(1)} %copy-done, f32[1,768]{1,0:T(1,128)S(1)} %reshape.62.qkv_b), custom_call_target="tpu_custom_call" | custom-call | flops 1300000000 | bytes 6000000 | tf_op jit(solution)/shard_map/mix_weights/pallas_call | solution.py:294
  30.7 1.8 %all-to-all-done.1.same = bf16[16,16,512]{2,1,0:T(8,128)(2,1)S(1)} async-done(((bf16[16,16,512]{2,1,0:T(8,128)(2,1)}), bf16[16,16,512]{2,1,0:T(8,128)(2,1)S(1)}, u32[]{:S(2)}, u32[]{:S(2)}) %all-to-all-start.1) | async-done | bytes 262176 | tf_op jit(solution)/shard_map/all_to_all | solution.py:473
  32.6 2.0 %collective-permute-start.1 = (bf16[16,16,512]{2,1,0:T(8,128)(2,1)S(1)}, bf16[16,16,512]{2,1,0:T(8,128)(2,1)S(1)}, u32[]{:S(2)}, u32[]{:S(2)}) collective-permute-start(bf16[16,16,512]{2,1,0:T(8,128)(2,1)S(1)} %all-to-all-done.1.same), channel_id=1, source_target_pairs={{0,8},{8,0},{16,24},{24,16},{32,40},{40,32},{48,56},{56,48},{64,72... | collective-permute-start | bytes 786440 | tf_op jit(solution)/shard_map/ppermute | solution.py:406
  35.1 0.6 collective-permute-done.1.other
  35.7 1.3 %convolve.1 = (f32[16,512]{1,0:T(8,128)S(1)}, f32[16,256]{1,0:T(8,128)S(1)}, f32[16,256]{1,0:T(8,128)S(1)}) custom-call(s32[21]{0:T(128)S(1)} %pad_add_fusion.table, bf16[768,512]{1,0:T(8,128)(2,1)S(1)} %get-tuple-element.25.act, bf16[16,16,512]{2,1,0:T(8,128)(2,1)S(1)} %all-to-all-done.1.same, bf16[16,16,512]{2,1,0:T(8,128)(2,1)S(1)} %collective-permute-done.1.other, ...), custom_call_target="tpu_custom_call" | custom-call | flops 400000000 | bytes 2000000 | tf_op jit(solution)/shard_map/convolve/pallas_call | solution.py:140
  37.0 1.2 %collective-permute-start.2 = (f32[16,256]{1,0:T(8,128)S(1)}, f32[16,256]{1,0:T(8,128)S(1)}, u32[]{:S(2)}, u32[]{:S(2)}) collective-permute-start(f32[16,256]{1,0:T(8,128)S(1)} %get-tuple-element.35), channel_id=1, source_target_pairs={{0,1},{2,3},{4,5},{6,7},{1,0},{3,2},{5,4},{7,6},{8,9},{10,11},{12,... | collective-permute-start | bytes 49160 | tf_op jit(solution)/shard_map/ppermute | solution.py:411
  38.3 0.7 collective-permute-start.3
  38.9 0.8 %collective-permute-done.2.first = f32[16,256]{1,0:T(8,128)S(1)} collective-permute-done((f32[16,256]{1,0:T(8,128)S(1)}, f32[16,256]{1,0:T(8,128)S(1)}, u32[]{:S(2)}, u32[]{:S(2)}) %collective-permute-start.2) | collective-permute-done | bytes 16416 | tf_op jit(solution)/shard_map/ppermute | solution.py:411
  39.7 0.5 finish.1
  40.2 11.2 %all_to_all.20.frames = bf16[16,4,16,128]{3,2,1,0:T(8,128)(2,1)S(1)} all-to-all(bf16[16,4,16,128]{3,2,1,0:T(8,128)(2,1)S(1)} %finish.1), channel_id=1, replica_groups={{0,16,32,48,64,80,96,112,128,144,160,176,192,208,224,240},{8,24,40,56,7..., dimensions={0} | all-to-all | bytes 524288 | tf_op jit(solution)/shard_map/all_to_all | solution.py:473
  51.5 0.7 route.1
  52.1 3.0 %collective-permute-start.4 = (bf16[4,16,128]{2,1,0:T(8,128)(2,1)S(1)}, bf16[4,16,128]{2,1,0:T(8,128)(2,1)S(1)}, u32[]{:S(2)}, u32[]{:S(2)}) collective-permute-start(bf16[4,16,128]{2,1,0:T(8,128)(2,1)S(1)} %get-tuple-element.38), channel_id=1, source_target_pairs={{0,8},{8,0},{16,24},{24,16},{32,40},{40,32},{48,56},{56,48},{64,72... | collective-permute-start | bytes 49160 | tf_op jit(solution)/shard_map/ppermute | solution.py:406
  55.2 0.8 %collective-permute-done.4 = bf16[4,16,128]{2,1,0:T(8,128)(2,1)S(1)} collective-permute-done((bf16[4,16,128]{2,1,0:T(8,128)(2,1)S(1)}, bf16[4,16,128]{2,1,0:T(8,128)(2,1)S(1)}, u32[]{:S(2)}, u32[]{:S(2)}) %collective-permute-start.4) | collective-permute-done | bytes 16416 | tf_op jit(solution)/shard_map/ppermute | solution.py:406
  56.0 14.2 %all_to_all.21.tokens = bf16[8,4,16,128]{3,2,1,0:T(8,128)(2,1)S(1)} all-to-all(bf16[8,4,16,128]{3,2,1,0:T(8,128)(2,1)S(1)} %broadcast_in_dim.75), channel_id=1, replica_groups={{7,6,5,4,3,2,1,0},{15,14,13,12,11,10,9,8},{23,22,21,20,19,18,17,16},{31..., dimensions={0} | all-to-all | bytes 262144 | tf_op jit(solution)/shard_map/all_to_all | solution.py:488
  70.2 4.5 %attend.1 = bf16[8,4,2,16,256]{4,3,2,1,0:T(8,128)(2,1)} custom-call(s32[21]{0:T(128)S(1)} %pad_add_fusion.table, bf16[8,4,16,128]{3,2,1,0:T(8,128)(2,1)S(1)} %all_to_all.21.tokens, bf16[2,128,768]{2,1,0:T(8,128)(2,1)S(1)} %get-tuple-element.39.mix, f32[8,768]{1,0:T(8,128)S(1)} %get-tuple-element.40.rows, bf16[3,128,128]{2,1,0:T(8,128)(2,1)S(1)} %get-tuple-element.41.gram, ...), custom_call_target="tpu_custom_call" | custom-call | flops 1000000000 | bytes 3000000 | tf_op jit(solution)/shard_map/attend/pallas_call | solution.py:387
  (47 shorter events, 1.5 us)
Async XLA Ops:
  0.0 11.6 %copy-start.3 = (bf16[4,2,64,512]{3,2,1,0:T(8,128)(2,1)S(1)}, bf16[4,2,64,512]{3,2,1,0:T(8,128)(2,1)}, u32[]{:S(2)}) copy-start(bf16[4,2,64,512]{3,2,1,0:T(8,128)(2,1)} %main.1) | copy-start | bytes 1572868
  0.0 15.7 %copy-start.11 = (s32[64]{0:T(128)S(1)}, s32[64]{0:T(128)}, u32[]{:S(2)}) copy-start(s32[64]{0:T(128)} %param.15) | copy-start | bytes 772
  0.0 15.8 %copy-start.9 = (s32[64]{0:T(128)S(1)}, s32[64]{0:T(128)}, u32[]{:S(2)}) copy-start(s32[64]{0:T(128)} %param.16) | copy-start | bytes 772
  0.0 17.8 %copy-start.10 = (f32[768]{0:T(1024)S(1)}, f32[768]{0:T(1024)}, u32[]{:S(2)}) copy-start(f32[768]{0:T(1024)} %param.25) | copy-start | bytes 9220
  0.0 25.1 %copy-start.1 = (bf16[64,6144]{1,0:T(8,128)(2,1)S(1)}, bf16[64,6144]{1,0:T(8,128)(2,1)}, u32[]{:S(2)}) copy-start(bf16[64,6144]{1,0:T(8,128)(2,1)} %modulation.1) | copy-start | bytes 2359300
  0.0 25.1 %copy-start.2 = (bf16[64,3072]{1,0:T(8,128)(2,1)S(1)}, bf16[64,3072]{1,0:T(8,128)(2,1)}, u32[]{:S(2)}) copy-start(bf16[64,3072]{1,0:T(8,128)(2,1)} %embed.1) | copy-start | bytes 1179652
  0.0 25.1 %copy-start.5 = (f32[3072]{0:T(1024)S(1)}, f32[3072]{0:T(1024)}, u32[]{:S(2)}) copy-start(f32[3072]{0:T(1024)} %param.22) | copy-start | bytes 36868
  1.8 16.0 %all-to-all-start = ((bf16[8,16,512]{2,1,0:T(8,128)(2,1)}), bf16[8,16,512]{2,1,0:T(8,128)(2,1)S(1)}, u32[]{:S(2)}, u32[]{:S(2)}) async-start(bf16[8,16,512]{2,1,0:T(8,128)(2,1)} %fold_tap.1), calls=%async_computation | async-start | bytes 262144 | tf_op jit(solution)/shard_map/all_to_all | solution.py:440
  11.6 23.1 %collective-permute-start = (bf16[2,2,64,512]{3,2,1,0:T(8,128)(2,1)S(1)}, bf16[2,2,64,512]{3,2,1,0:T(8,128)(2,1)S(1)}, u32[]{:S(2)}, u32[]{:S(2)}) collective-permute-start(bf16[2,2,64,512]{3,2,1,0:T(8,128)(2,1)S(1)} %slice.3), channel_id=1, source_target_pairs={{0,8},{8,16},{16,24},{24,32},{32,40},{40,48},{48,56},{56,64},{64,7... | collective-permute-start | bytes 786440 | tf_op jit(solution)/shard_map/ppermute | solution.py:402
  18.6 13.9 %all-to-all-start.1 = ((bf16[16,16,512]{2,1,0:T(8,128)(2,1)}), bf16[16,16,512]{2,1,0:T(8,128)(2,1)S(1)}, u32[]{:S(2)}, u32[]{:S(2)}) async-start(bf16[16,16,512]{2,1,0:T(8,128)(2,1)} %broadcast_in_dim.45), calls=%async_computation.1 | async-start | bytes 524288 | tf_op jit(solution)/shard_map/all_to_all | solution.py:473
  26.2 2.3 %copy-start = (bf16[3072,768]{1,0:T(8,128)(2,1)S(1)}, bf16[3072,768]{1,0:T(8,128)(2,1)}, u32[]{:S(2)}) copy-start(bf16[3072,768]{1,0:T(8,128)(2,1)} %qkv_w.1) | copy-start | bytes 14155780
  28.5 6.0 %copy-start.12 = (f32[16]{0:T(128)S(1)}, f32[16]{0:T(128)}, u32[]{:S(2)}) copy-start(f32[16]{0:T(128)} %param.20) | copy-start | bytes 196
  28.5 6.1 %copy-start.4 = (bf16[512,16]{0,1:T(8,128)(2,1)S(1)}, bf16[512,16]{0,1:T(8,128)(2,1)}, u32[]{:S(2)}) copy-start(bf16[512,16]{0,1:T(8,128)(2,1)} %param.19) | copy-start | bytes 49156
  28.5 6.1 %copy-start.6 = (f32[512]{0:T(512)S(1)}, f32[512]{0:T(512)}, u32[]{:S(2)}) copy-start(f32[512]{0:T(512)} %param.18) | copy-start | bytes 6148
  32.6 3.2 %collective-permute-start.1 = (bf16[16,16,512]{2,1,0:T(8,128)(2,1)S(1)}, bf16[16,16,512]{2,1,0:T(8,128)(2,1)S(1)}, u32[]{:S(2)}, u32[]{:S(2)}) collective-permute-start(bf16[16,16,512]{2,1,0:T(8,128)(2,1)S(1)} %all-to-all-done.1.same), channel_id=1, source_target_pairs={{0,8},{8,0},{16,24},{24,16},{32,40},{40,32},{48,56},{56,48},{64,72... | collective-permute-start | bytes 786440 | tf_op jit(solution)/shard_map/ppermute | solution.py:406
  35.1 35.2 %copy-start.7 = (f32[128]{0:T(128)S(1)}, f32[128]{0:T(128)}, u32[]{:S(2)}) copy-start(f32[128]{0:T(128)} %param.26) | copy-start | bytes 1540
  35.1 35.2 %copy-start.8 = (f32[128]{0:T(128)S(1)}, f32[128]{0:T(128)}, u32[]{:S(2)}) copy-start(f32[128]{0:T(128)} %param.27) | copy-start | bytes 1540
  37.0 2.7 %collective-permute-start.2 = (f32[16,256]{1,0:T(8,128)S(1)}, f32[16,256]{1,0:T(8,128)S(1)}, u32[]{:S(2)}, u32[]{:S(2)}) collective-permute-start(f32[16,256]{1,0:T(8,128)S(1)} %get-tuple-element.35), channel_id=1, source_target_pairs={{0,1},{2,3},{4,5},{6,7},{1,0},{3,2},{5,4},{7,6},{8,9},{10,11},{12,... | collective-permute-start | bytes 49160 | tf_op jit(solution)/shard_map/ppermute | solution.py:411
  38.3 1.4 %collective-permute-start.3 = (f32[16,256]{1,0:T(8,128)S(1)}, f32[16,256]{1,0:T(8,128)S(1)}, u32[]{:S(2)}, u32[]{:S(2)}) collective-permute-start(f32[16,256]{1,0:T(8,128)S(1)} %get-tuple-element.36), channel_id=1, source_target_pairs={{1,2},{3,4},{5,6},{2,1},{4,3},{6,5},{9,10},{11,12},{13,14},{10,9},... | collective-permute-start | bytes 49160 | tf_op jit(solution)/shard_map/ppermute | solution.py:411
  52.1 3.9 %collective-permute-start.4 = (bf16[4,16,128]{2,1,0:T(8,128)(2,1)S(1)}, bf16[4,16,128]{2,1,0:T(8,128)(2,1)S(1)}, u32[]{:S(2)}, u32[]{:S(2)}) collective-permute-start(bf16[4,16,128]{2,1,0:T(8,128)(2,1)S(1)} %get-tuple-element.38), channel_id=1, source_target_pairs={{0,8},{8,0},{16,24},{24,16},{32,40},{40,32},{48,56},{56,48},{64,72... | collective-permute-start | bytes 49160 | tf_op jit(solution)/shard_map/ppermute | solution.py:406

commit v6 on v5

--- a/solution.py
+++ b/solution.py
@@ -313,48 +313,41 @@
     )(left, qkv_weight, qkv_bias.reshape(1, -1))
 
 
-def project(lead, own, mix, rows, gram, gvec, q_gain, k_gain, write):
+def project(clip, begin, end, tokens, mix, rows, gram, gvec, q_gain, k_gain, parts):
     factor = math.log2(math.e) / math.sqrt(128)
     gain = q_gain[...] * k_gain[...] * factor
-    count = own.shape[0]
-    later = iota((count, 1), 0) // 16 % 4 >= lead
+    own = jnp.concatenate([tokens[:, frame].reshape(128, 128) for frame in range(begin, end)], axis=0)
     spread = dot(own, gram[0]) + dot(own, gram[1]) + dot(own, gram[2])
     terms = (spread + gvec[0:1, :]) * own.astype(f32)
-    low_lane = iota((count, 128), 1) < 64
-    slope = jnp.where(later, rows[1:2, :], rows[0:1, :])
-    offset = jnp.where(later, rows[3:4, :], rows[2:3, :])
+    low_lane = iota(own.shape, 1) < 64
     for half in range(2):
         mine = jnp.where(low_lane == (half == 0), terms, 0.0)
         variance = jnp.sum(mine, axis=1, keepdims=True) + gvec[1:2, 0:1]
         scale = lax.rsqrt(jnp.maximum(variance, 0.0) + norm_eps)
         feats = own[:, half * 64 : half * 64 + 64]
         twice = jnp.concatenate([feats, feats], axis=1)
-        mixed = jnp.where(later, dot(twice, mix[1]), dot(twice, mix[0]))
-        qkv = scale * (mixed + slope) + offset
+        qkv = scale * (dot(twice, mix[clip]) + rows[clip : clip + 1, :]) + rows[clip + 2 : clip + 3, :]
         for head in range(2):
             at = head * 384
-            for kind in range(2):
+            for kind in range(3):
                 part = qkv[:, at + kind * 128 : at + kind * 128 + 128]
-                norm = lax.rsqrt(jnp.mean(part * part, axis=1, keepdims=True) + norm_eps)
-                part = part * norm
-                write(kind, head, half, (part * gain if kind == 0 else part).astype(bf16))
-            write(2, head, half, qkv[:, at + 256 : at + 384].astype(bf16))
+                if kind < 2:
+                    part = part * lax.rsqrt(jnp.mean(part * part, axis=1, keepdims=True) + norm_eps)
+                if kind == 0:
+                    part = part * gain
+                part = part.astype(bf16)
+                for frame in range(begin, end):
+                    place = frame * 256 + half * 128
+                    parts[kind, head, place : place + 128, :] = part[
+                        (frame - begin) * 128 : (frame - begin) * 128 + 128
+                    ]
 
 
 def attend_kernel(
     table, tokens, mix, rows, gram, gvec, q_gain, k_gain, out, parts
 ):
     lead = table[20]
-    def write(kind, head, half, value):
-        for band in range(8):
-            for frame in range(4):
-                at = frame * 256 + (half * 8 + band) * 16
-                parts[kind, head, at : at + 16, :] = value[
-                    (band * 4 + frame) * 16 : (band * 4 + frame) * 16 + 16
-                ]
-
-    own = tokens[...].reshape(512, 128)
-    project(lead, own, mix, rows, gram, gvec, q_gain, k_gain, write)
+    shared = (tokens, mix, rows, gram, gvec, q_gain, k_gain, parts)
 
     def group(begin, end):
         for head in range(2):
@@ -377,6 +370,8 @@
 
         @pl.when(lead == first)
         def _(first=first):
+            project(0, 0, first, *shared)
+            project(1, first, 4, *shared)
             group(0, first)
             group(first, 4)
 

time: 75.7 us -> 75.1 us (level)
  no operation moved by 1% of the time
where the time goes in v6:
time: 75.1 us; the launch traced here: 74.3 us
  starting transfers between devices  27.2 us (36%)
  blocking collectives  25.4 us (34%)
  Pallas kernels  11.9 us (16%)
  waiting for transfers between devices  4.04 us (5%)
  local copies, waits for them, and re-layouts  3.4 us (5%)
  other arithmetic  2.08 us (3%)
    all_to_all x1, blocking collectives, per_device(): lax.all_to_all(jnp.broadcast_to(slots[None], (heads,) + slots.shape), 'he...  14.2 us
    all_to_all x1, blocking collectives, per_device(): lax.all_to_all(value, 'seq', 0, 0, axis_index_groups=cores)  11.2 us
    all_to_all x1, starting transfers between devices, per_device(): lax.all_to_all(fold_tap(weight, latent_rows, heads), 'head', 0, 0, axis_i...  9.73 us
    all_to_all x1, starting transfers between devices, per_device(): lax.all_to_all(value, 'seq', 0, 0, axis_index_groups=cores)  6.46 us
    ppermute x2, starting transfers between devices, swap(): lax.ppermute(value, axis, [(i, i ^ mask) for i in range(lax.axis_size(axi...  5.03 us
    ppermute x1, starting transfers between devices, neighbour(): return lax.ppermute(value, axis, pairs)  4.05 us
    pallas_call x1, Pallas kernels, attend(): pl.pallas_call(attend_kernel, in_specs=[smem] + [vmem] * 7, out_specs=vme...  4.01 us
    unnamed x26, local copies, waits for them, and re-layouts  2.38 us
  transfers between devices with their start and end apart: 7, of which 4 were waited for; matrix products, arithmetic and copies ran while one was open for 4% of the time, Pallas kernels for 5%

profile of v6, /device:TPU:1, one launch (start us, length us, event | category | flops | bytes accessed | tf_op | source)
XLA Modules:
  0.0 74.3 jit_solution(14467480442825806559)
XLA Ops:
  0.0 1.8 %fold_tap.1 = bf16[8,16,512]{2,1,0:T(8,128)(2,1)} custom-call(bf16[27,64,512]{2,1,0:T(8,128)(2,1)} %bitcast.21, bf16[16,512]{1,0:T(8,128)(2,1)} %bitcast.15), custom_call_target="tpu_custom_call" | custom-call | flops 1000000 | bytes 150000 | tf_op jit(solution)/shard_map/fold_tap/pallas_call | solution.py:53
  1.8 9.7 %all-to-all-start = ((bf16[8,16,512]{2,1,0:T(8,128)(2,1)}), bf16[8,16,512]{2,1,0:T(8,128)(2,1)S(1)}, u32[]{:S(2)}, u32[]{:S(2)}) async-start(bf16[8,16,512]{2,1,0:T(8,128)(2,1)} %fold_tap.1), calls=%async_computation | async-start | bytes 262144 | tf_op jit(solution)/shard_map/all_to_all | solution.py:435
  11.6 4.0 %collective-permute-start = (bf16[2,2,64,512]{3,2,1,0:T(8,128)(2,1)S(1)}, bf16[2,2,64,512]{3,2,1,0:T(8,128)(2,1)S(1)}, u32[]{:S(2)}, u32[]{:S(2)}) collective-permute-start(bf16[2,2,64,512]{3,2,1,0:T(8,128)(2,1)S(1)} %slice.3), channel_id=1, source_target_pairs={{0,8},{8,16},{16,24},{24,32},{32,40},{40,48},{48,56},{56,64},{64,7... | collective-permute-start | bytes 786440 | tf_op jit(solution)/shard_map/ppermute | solution.py:397
  15.8 0.7 fusion.1
  17.0 0.7 pad_add_fusion.table
  17.9 0.7 broadcast_in_dim.45
  18.6 6.5 %all-to-all-start.1 = ((bf16[16,16,512]{2,1,0:T(8,128)(2,1)}), bf16[16,16,512]{2,1,0:T(8,128)(2,1)S(1)}, u32[]{:S(2)}, u32[]{:S(2)}) async-start(bf16[16,16,512]{2,1,0:T(8,128)(2,1)} %broadcast_in_dim.45), calls=%async_computation.1 | async-start | bytes 524288 | tf_op jit(solution)/shard_map/all_to_all | solution.py:468
  25.2 1.0 %scale_embedding.1 = (bf16[272,3072]{1,0:T(8,128)(2,1)S(1)}, bf16[3,128,128]{2,1,0:T(8,128)(2,1)S(1)}, f32[8,128]{1,0:T(8,128)S(1)}) custom-call(bf16[8,64]{1,0:T(8,128)(2,1)S(1)} %add_convert_fusion.member, bf16[64,6144]{1,0:T(8,128)(2,1)S(1)} %copy-done.1, bf16[64,3072]{1,0:T(8,128)(2,1)S(1)} %copy-done.2, f32[1,3072]{1,0:T(1,128)S(1)} %bitcast.17), custom_call_target="tpu_custom_call" | custom-call | flops 100000000 | bytes 3000000 | tf_op jit(solution)/shard_map/scale_embedding/pallas_call | solution.py:263
  26.2 2.3 %copy-done = bf16[3072,768]{1,0:T(8,128)(2,1)S(1)} copy-done((bf16[3072,768]{1,0:T(8,128)(2,1)S(1)}, bf16[3072,768]{1,0:T(8,128)(2,1)}, u32[]{:S(2)}) %copy-start) | copy-done | bytes 4718616
  28.6 2.2 %mix_weights.1 = (bf16[2,128,768]{2,1,0:T(8,128)(2,1)S(1)}, f32[8,768]{1,0:T(8,128)S(1)}) custom-call(bf16[272,3072]{1,0:T(8,128)(2,1)S(1)} %get-tuple-element.27.left, bf16[3072,768]{1,0:T(8,128)(2,1)S(1)} %copy-done, f32[1,768]{1,0:T(1,128)S(1)} %reshape.62.qkv_b), custom_call_target="tpu_custom_call" | custom-call | flops 1300000000 | bytes 6000000 | tf_op jit(solution)/shard_map/mix_weights/pallas_call | solution.py:294
  30.7 1.8 %all-to-all-done.1.same = bf16[16,16,512]{2,1,0:T(8,128)(2,1)S(1)} async-done(((bf16[16,16,512]{2,1,0:T(8,128)(2,1)}), bf16[16,16,512]{2,1,0:T(8,128)(2,1)S(1)}, u32[]{:S(2)}, u32[]{:S(2)}) %all-to-all-start.1) | async-done | bytes 262176 | tf_op jit(solution)/shard_map/all_to_all | solution.py:468
  32.6 2.0 %collective-permute-start.1 = (bf16[16,16,512]{2,1,0:T(8,128)(2,1)S(1)}, bf16[16,16,512]{2,1,0:T(8,128)(2,1)S(1)}, u32[]{:S(2)}, u32[]{:S(2)}) collective-permute-start(bf16[16,16,512]{2,1,0:T(8,128)(2,1)S(1)} %all-to-all-done.1.same), channel_id=1, source_target_pairs={{0,8},{8,0},{16,24},{24,16},{32,40},{40,32},{48,56},{56,48},{64,72... | collective-permute-start | bytes 786440 | tf_op jit(solution)/shard_map/ppermute | solution.py:401
  35.1 0.6 collective-permute-done.1.other
  35.7 1.3 %convolve.1 = (f32[16,512]{1,0:T(8,128)S(1)}, f32[16,256]{1,0:T(8,128)S(1)}, f32[16,256]{1,0:T(8,128)S(1)}) custom-call(s32[21]{0:T(128)S(1)} %pad_add_fusion.table, bf16[768,512]{1,0:T(8,128)(2,1)S(1)} %get-tuple-element.25.act, bf16[16,16,512]{2,1,0:T(8,128)(2,1)S(1)} %all-to-all-done.1.same, bf16[16,16,512]{2,1,0:T(8,128)(2,1)S(1)} %collective-permute-done.1.other, ...), custom_call_target="tpu_custom_call" | custom-call | flops 400000000 | bytes 2000000 | tf_op jit(solution)/shard_map/convolve/pallas_call | solution.py:140
  37.0 1.2 %collective-permute-start.2 = (f32[16,256]{1,0:T(8,128)S(1)}, f32[16,256]{1,0:T(8,128)S(1)}, u32[]{:S(2)}, u32[]{:S(2)}) collective-permute-start(f32[16,256]{1,0:T(8,128)S(1)} %get-tuple-element.35), channel_id=1, source_target_pairs={{0,1},{2,3},{4,5},{6,7},{1,0},{3,2},{5,4},{7,6},{8,9},{10,11},{12,... | collective-permute-start | bytes 49160 | tf_op jit(solution)/shard_map/ppermute | solution.py:406
  38.3 0.7 collective-permute-start.3
  38.9 0.8 %collective-permute-done.2.first = f32[16,256]{1,0:T(8,128)S(1)} collective-permute-done((f32[16,256]{1,0:T(8,128)S(1)}, f32[16,256]{1,0:T(8,128)S(1)}, u32[]{:S(2)}, u32[]{:S(2)}) %collective-permute-start.2) | collective-permute-done | bytes 16416 | tf_op jit(solution)/shard_map/ppermute | solution.py:406
  39.7 0.5 finish.1
  40.2 11.2 %all_to_all.20.frames = bf16[16,4,16,128]{3,2,1,0:T(8,128)(2,1)S(1)} all-to-all(bf16[16,4,16,128]{3,2,1,0:T(8,128)(2,1)S(1)} %finish.1), channel_id=1, replica_groups={{0,16,32,48,64,80,96,112,128,144,160,176,192,208,224,240},{8,24,40,56,7..., dimensions={0} | all-to-all | bytes 524288 | tf_op jit(solution)/shard_map/all_to_all | solution.py:468
  51.5 0.7 route.1
  52.1 3.0 %collective-permute-start.4 = (bf16[4,16,128]{2,1,0:T(8,128)(2,1)S(1)}, bf16[4,16,128]{2,1,0:T(8,128)(2,1)S(1)}, u32[]{:S(2)}, u32[]{:S(2)}) collective-permute-start(bf16[4,16,128]{2,1,0:T(8,128)(2,1)S(1)} %get-tuple-element.38), channel_id=1, source_target_pairs={{0,8},{8,0},{16,24},{24,16},{32,40},{40,32},{48,56},{56,48},{64,72... | collective-permute-start | bytes 49160 | tf_op jit(solution)/shard_map/ppermute | solution.py:401
  55.2 0.8 %collective-permute-done.4 = bf16[4,16,128]{2,1,0:T(8,128)(2,1)S(1)} collective-permute-done((bf16[4,16,128]{2,1,0:T(8,128)(2,1)S(1)}, bf16[4,16,128]{2,1,0:T(8,128)(2,1)S(1)}, u32[]{:S(2)}, u32[]{:S(2)}) %collective-permute-start.4) | collective-permute-done | bytes 16416 | tf_op jit(solution)/shard_map/ppermute | solution.py:401
  56.0 14.2 %all_to_all.21.tokens = bf16[8,4,16,128]{3,2,1,0:T(8,128)(2,1)S(1)} all-to-all(bf16[8,4,16,128]{3,2,1,0:T(8,128)(2,1)S(1)} %broadcast_in_dim.75), channel_id=1, replica_groups={{7,6,5,4,3,2,1,0},{15,14,13,12,11,10,9,8},{23,22,21,20,19,18,17,16},{31..., dimensions={0} | all-to-all | bytes 262144 | tf_op jit(solution)/shard_map/all_to_all | solution.py:483
  70.2 4.0 %attend.1 = bf16[8,4,2,16,256]{4,3,2,1,0:T(8,128)(2,1)} custom-call(s32[21]{0:T(128)S(1)} %pad_add_fusion.table, bf16[8,4,16,128]{3,2,1,0:T(8,128)(2,1)S(1)} %all_to_all.21.tokens, bf16[2,128,768]{2,1,0:T(8,128)(2,1)S(1)} %get-tuple-element.39.mix, f32[8,768]{1,0:T(8,128)S(1)} %get-tuple-element.40.rows, bf16[3,128,128]{2,1,0:T(8,128)(2,1)S(1)} %get-tuple-element.41.gram, ...), custom_call_target="tpu_custom_call" | custom-call | flops 1000000000 | bytes 3000000 | tf_op jit(solution)/shard_map/attend/pallas_call | solution.py:382
  (47 shorter events, 1.5 us)
Async XLA Ops:
  0.0 11.6 %copy-start.3 = (bf16[4,2,64,512]{3,2,1,0:T(8,128)(2,1)S(1)}, bf16[4,2,64,512]{3,2,1,0:T(8,128)(2,1)}, u32[]{:S(2)}) copy-start(bf16[4,2,64,512]{3,2,1,0:T(8,128)(2,1)} %main.1) | copy-start | bytes 1572868
  0.0 15.7 %copy-start.11 = (s32[64]{0:T(128)S(1)}, s32[64]{0:T(128)}, u32[]{:S(2)}) copy-start(s32[64]{0:T(128)} %param.15) | copy-start | bytes 772
  0.0 15.8 %copy-start.9 = (s32[64]{0:T(128)S(1)}, s32[64]{0:T(128)}, u32[]{:S(2)}) copy-start(s32[64]{0:T(128)} %param.16) | copy-start | bytes 772
  0.0 17.8 %copy-start.10 = (f32[768]{0:T(1024)S(1)}, f32[768]{0:T(1024)}, u32[]{:S(2)}) copy-start(f32[768]{0:T(1024)} %param.25) | copy-start | bytes 9220
  0.0 25.1 %copy-start.1 = (bf16[64,6144]{1,0:T(8,128)(2,1)S(1)}, bf16[64,6144]{1,0:T(8,128)(2,1)}, u32[]{:S(2)}) copy-start(bf16[64,6144]{1,0:T(8,128)(2,1)} %modulation.1) | copy-start | bytes 2359300
  0.0 25.1 %copy-start.2 = (bf16[64,3072]{1,0:T(8,128)(2,1)S(1)}, bf16[64,3072]{1,0:T(8,128)(2,1)}, u32[]{:S(2)}) copy-start(bf16[64,3072]{1,0:T(8,128)(2,1)} %embed.1) | copy-start | bytes 1179652
  0.0 25.1 %copy-start.5 = (f32[3072]{0:T(1024)S(1)}, f32[3072]{0:T(1024)}, u32[]{:S(2)}) copy-start(f32[3072]{0:T(1024)} %param.22) | copy-start | bytes 36868
  1.8 16.0 %all-to-all-start = ((bf16[8,16,512]{2,1,0:T(8,128)(2,1)}), bf16[8,16,512]{2,1,0:T(8,128)(2,1)S(1)}, u32[]{:S(2)}, u32[]{:S(2)}) async-start(bf16[8,16,512]{2,1,0:T(8,128)(2,1)} %fold_tap.1), calls=%async_computation | async-start | bytes 262144 | tf_op jit(solution)/shard_map/all_to_all | solution.py:435
  11.6 23.1 %collective-permute-start = (bf16[2,2,64,512]{3,2,1,0:T(8,128)(2,1)S(1)}, bf16[2,2,64,512]{3,2,1,0:T(8,128)(2,1)S(1)}, u32[]{:S(2)}, u32[]{:S(2)}) collective-permute-start(bf16[2,2,64,512]{3,2,1,0:T(8,128)(2,1)S(1)} %slice.3), channel_id=1, source_target_pairs={{0,8},{8,16},{16,24},{24,32},{32,40},{40,48},{48,56},{56,64},{64,7... | collective-permute-start | bytes 786440 | tf_op jit(solution)/shard_map/ppermute | solution.py:397
  18.6 13.9 %all-to-all-start.1 = ((bf16[16,16,512]{2,1,0:T(8,128)(2,1)}), bf16[16,16,512]{2,1,0:T(8,128)(2,1)S(1)}, u32[]{:S(2)}, u32[]{:S(2)}) async-start(bf16[16,16,512]{2,1,0:T(8,128)(2,1)} %broadcast_in_dim.45), calls=%async_computation.1 | async-start | bytes 524288 | tf_op jit(solution)/shard_map/all_to_all | solution.py:468
  26.2 2.3 %copy-start = (bf16[3072,768]{1,0:T(8,128)(2,1)S(1)}, bf16[3072,768]{1,0:T(8,128)(2,1)}, u32[]{:S(2)}) copy-start(bf16[3072,768]{1,0:T(8,128)(2,1)} %qkv_w.1) | copy-start | bytes 14155780
  28.5 6.0 %copy-start.12 = (f32[16]{0:T(128)S(1)}, f32[16]{0:T(128)}, u32[]{:S(2)}) copy-start(f32[16]{0:T(128)} %param.20) | copy-start | bytes 196
  28.5 6.1 %copy-start.4 = (bf16[512,16]{0,1:T(8,128)(2,1)S(1)}, bf16[512,16]{0,1:T(8,128)(2,1)}, u32[]{:S(2)}) copy-start(bf16[512,16]{0,1:T(8,128)(2,1)} %param.19) | copy-start | bytes 49156
  28.5 6.1 %copy-start.6 = (f32[512]{0:T(512)S(1)}, f32[512]{0:T(512)}, u32[]{:S(2)}) copy-start(f32[512]{0:T(512)} %param.18) | copy-start | bytes 6148
  32.6 3.2 %collective-permute-start.1 = (bf16[16,16,512]{2,1,0:T(8,128)(2,1)S(1)}, bf16[16,16,512]{2,1,0:T(8,128)(2,1)S(1)}, u32[]{:S(2)}, u32[]{:S(2)}) collective-permute-start(bf16[16,16,512]{2,1,0:T(8,128)(2,1)S(1)} %all-to-all-done.1.same), channel_id=1, source_target_pairs={{0,8},{8,0},{16,24},{24,16},{32,40},{40,32},{48,56},{56,48},{64,72... | collective-permute-start | bytes 786440 | tf_op jit(solution)/shard_map/ppermute | solution.py:401
  35.1 35.2 %copy-start.7 = (f32[128]{0:T(128)S(1)}, f32[128]{0:T(128)}, u32[]{:S(2)}) copy-start(f32[128]{0:T(128)} %param.26) | copy-start | bytes 1540
  35.1 35.2 %copy-start.8 = (f32[128]{0:T(128)S(1)}, f32[128]{0:T(128)}, u32[]{:S(2)}) copy-start(f32[128]{0:T(128)} %param.27) | copy-start | bytes 1540
  37.0 2.7 %collective-permute-start.2 = (f32[16,256]{1,0:T(8,128)S(1)}, f32[16,256]{1,0:T(8,128)S(1)}, u32[]{:S(2)}, u32[]{:S(2)}) collective-permute-start(f32[16,256]{1,0:T(8,128)S(1)} %get-tuple-element.35), channel_id=1, source_target_pairs={{0,1},{2,3},{4,5},{6,7},{1,0},{3,2},{5,4},{7,6},{8,9},{10,11},{12,... | collective-permute-start | bytes 49160 | tf_op jit(solution)/shard_map/ppermute | solution.py:406
  38.3 1.4 %collective-permute-start.3 = (f32[16,256]{1,0:T(8,128)S(1)}, f32[16,256]{1,0:T(8,128)S(1)}, u32[]{:S(2)}, u32[]{:S(2)}) collective-permute-start(f32[16,256]{1,0:T(8,128)S(1)} %get-tuple-element.36), channel_id=1, source_target_pairs={{1,2},{3,4},{5,6},{2,1},{4,3},{6,5},{9,10},{11,12},{13,14},{10,9},... | collective-permute-start | bytes 49160 | tf_op jit(solution)/shard_map/ppermute | solution.py:406
  52.1 3.9 %collective-permute-start.4 = (bf16[4,16,128]{2,1,0:T(8,128)(2,1)S(1)}, bf16[4,16,128]{2,1,0:T(8,128)(2,1)S(1)}, u32[]{:S(2)}, u32[]{:S(2)}) collective-permute-start(bf16[4,16,128]{2,1,0:T(8,128)(2,1)S(1)} %get-tuple-element.38), channel_id=1, source_target_pairs={{0,8},{8,0},{16,24},{24,16},{32,40},{40,32},{48,56},{56,48},{64,72... | collective-permute-start | bytes 49160 | tf_op jit(solution)/shard_map/ppermute | solution.py:401

commit v7 on v6

--- a/solution.py
+++ b/solution.py
@@ -275,39 +275,41 @@
     )(member, modulation, embed_weight, embed_bias.reshape(1, -1))
 
 
-def mix_kernel(left, qkv_w, qkv_b, mix, rows):
-    product = dot(left[...], qkv_w[...])
-    cols = product.shape[1]
+def mix_kernel(left, qkv_w, qkv_b, mix, rows, held, sems):
+    parts, depth = held.shape[0], held.shape[1]
+    copies = [
+        pltpu.make_async_copy(qkv_w.at[pl.ds(k * depth, depth)], held.at[k], sems.at[k])
+        for k in range(parts)
+    ]
+    for copy in copies:
+        copy.start()
+    product = None
+    for k in range(parts):
+        copies[k].wait()
+        term = dot(left[:, k * depth : k * depth + depth], held[k])
+        product = term if product is None else product + term
     for clip in range(2):
         at = clip * 128
         high, low = split2(product[at : at + 64] + product[at + 64 : at + 128])
         mix[clip] = jnp.concatenate([high, low], axis=0)
     tail = product[256:272]
     rows[...] = jnp.concatenate(
-        [tail[0:2] + tail[2:4], tail[4:6] + qkv_b[...], jnp.zeros((4, cols), f32)], axis=0
+        [tail[0:2] + tail[2:4], tail[4:6] + qkv_b[...], jnp.zeros((4, 768), f32)], axis=0
     )
 
 
 def mix_weights(left, qkv_weight, qkv_bias):
-    width = left.shape[1]
-    cols = 256
+    vmem = pl.BlockSpec(memory_space=pltpu.VMEM)
     return pl.pallas_call(
         mix_kernel,
-        grid=(qkv_weight.shape[1] // cols,),
-        in_specs=[
-            pl.BlockSpec(left.shape, lambda n: (0, 0)),
-            pl.BlockSpec((width, cols), lambda n: (0, n)),
-            pl.BlockSpec((1, cols), lambda n: (0, n)),
-        ],
-        out_specs=[
-            pl.BlockSpec((2, 128, cols), lambda n: (0, 0, n)),
-            pl.BlockSpec((8, cols), lambda n: (0, n)),
-        ],
+        in_specs=[vmem, pl.BlockSpec(memory_space=pl.ANY), vmem],
+        out_specs=[vmem, vmem],
         out_shape=[
             jax.ShapeDtypeStruct((2, 128, 768), bf16),
             jax.ShapeDtypeStruct((8, 768), f32),
         ],
-        compiler_params=pltpu.CompilerParams(vmem_limit_bytes=12 * MIB),
+        scratch_shapes=[pltpu.VMEM((4, 768, 768), bf16), pltpu.SemaphoreType.DMA((4,))],
+        compiler_params=pltpu.CompilerParams(vmem_limit_bytes=56 * MIB),
         cost_estimate=pl.CostEstimate(flops=13 * 10**8, bytes_accessed=6 * 10**6, transcendentals=0),
         name="mix_weights",
     )(left, qkv_weight, qkv_bias.reshape(1, -1))

time: 75.1 us -> 78.1 us (1.040)
  Pallas kernels: 11.9 us -> 16.2 us
  blocking collectives: 25.4 us -> 27.7 us
  waiting for transfers between devices: 4.04 us -> 2.19 us
  starting transfers between devices: 27.2 us -> 26.4 us
    pallas_call x1, Pallas kernels: 2.18 us -> 5.86 us  [mix_weights(): pl.pallas_call(mix_kernel, in_specs=[vmem, pl.BlockSpec(memory_space=pl.A...]
    all_to_all x1, blocking collectives: 11.2 us -> 13.4 us  [per_device(): lax.all_to_all(value, 'seq', 0, 0, axis_index_groups=cores)]
    all_to_all x1, waiting for transfers between devices: 1.82 us -> 0.01 us  [per_device(): lax.all_to_all(value, 'seq', 0, 0, axis_index_groups=cores)]
    unnamed x26 -> x30, local copies, waits for them, and re-layouts: 2.38 us -> 1.26 us
  transfers between devices with their start and end apart: 7 -> 7, of which waited for: 4 -> 3; matrix products, arithmetic and copies ran while one was open for 4% -> 5% of each run, Pallas kernels for 5% -> 9%
where the time goes in v7:
time: 78.1 us; the launch traced here: 77.5 us
  blocking collectives  27.7 us (35%)
  starting transfers between devices  26.4 us (34%)
  Pallas kernels  16.2 us (21%)
  local copies, waits for them, and re-layouts  2.88 us (4%)
  waiting for transfers between devices  2.19 us (3%)
  other arithmetic  1.91 us (2%)
    all_to_all x1, blocking collectives, per_device(): lax.all_to_all(jnp.broadcast_to(slots[None], (heads,) + slots.shape), 'he...  14.4 us
    all_to_all x1, blocking collectives, per_device(): lax.all_to_all(value, 'seq', 0, 0, axis_index_groups=cores)  13.4 us
    all_to_all x1, starting transfers between devices, per_device(): lax.all_to_all(fold_tap(weight, latent_rows, heads), 'head', 0, 0, axis_i...  9.73 us
    all_to_all x1, starting transfers between devices, per_device(): lax.all_to_all(value, 'seq', 0, 0, axis_index_groups=cores)  6.46 us
    pallas_call x1, Pallas kernels, mix_weights(): pl.pallas_call(mix_kernel, in_specs=[vmem, pl.BlockSpec(memory_space=pl.A...  5.86 us
    pallas_call x1, Pallas kernels, attend(): pl.pallas_call(attend_kernel, in_specs=[smem] + [vmem] * 7, out_specs=vme...  4.57 us
    ppermute x2, starting transfers between devices, swap(): lax.ppermute(value, axis, [(i, i ^ mask) for i in range(lax.axis_size(axi...  4.31 us
    ppermute x1, starting transfers between devices, neighbour(): return lax.ppermute(value, axis, pairs)  4.05 us
  transfers between devices with their start and end apart: 7, of which 3 were waited for; matrix products, arithmetic and copies ran while one was open for 5% of the time, Pallas kernels for 9%

profile of v7, /device:TPU:1, one launch (start us, length us, event | category | flops | bytes accessed | tf_op | source)
XLA Modules:
  0.0 77.5 jit_solution(2229975477280828360)
XLA Ops:
  0.0 1.8 %fold_tap.1 = bf16[8,16,512]{2,1,0:T(8,128)(2,1)} custom-call(bf16[27,64,512]{2,1,0:T(8,128)(2,1)} %bitcast.21, bf16[16,512]{1,0:T(8,128)(2,1)} %bitcast.15), custom_call_target="tpu_custom_call" | custom-call | flops 1000000 | bytes 150000 | tf_op jit(solution)/shard_map/fold_tap/pallas_call | solution.py:53
  1.8 9.7 %all-to-all-start = ((bf16[8,16,512]{2,1,0:T(8,128)(2,1)}), bf16[8,16,512]{2,1,0:T(8,128)(2,1)S(1)}, u32[]{:S(2)}, u32[]{:S(2)}) async-start(bf16[8,16,512]{2,1,0:T(8,128)(2,1)} %fold_tap.1), calls=%async_computation | async-start | bytes 262144 | tf_op jit(solution)/shard_map/all_to_all | solution.py:437
  11.6 4.0 %collective-permute-start = (bf16[2,2,64,512]{3,2,1,0:T(8,128)(2,1)S(1)}, bf16[2,2,64,512]{3,2,1,0:T(8,128)(2,1)S(1)}, u32[]{:S(2)}, u32[]{:S(2)}) collective-permute-start(bf16[2,2,64,512]{3,2,1,0:T(8,128)(2,1)S(1)} %slice.3), channel_id=1, source_target_pairs={{0,8},{8,16},{16,24},{24,32},{32,40},{40,48},{48,56},{56,64},{64,7... | collective-permute-start | bytes 786440 | tf_op jit(solution)/shard_map/ppermute | solution.py:399
  15.8 0.6 fusion.1
  17.0 0.6 pad_add_fusion.table
  17.7 0.6 reshape.62.qkv_b
  18.3 0.7 broadcast_in_dim.45
  19.0 6.5 %all-to-all-start.1 = ((bf16[16,16,512]{2,1,0:T(8,128)(2,1)}), bf16[16,16,512]{2,1,0:T(8,128)(2,1)S(1)}, u32[]{:S(2)}, u32[]{:S(2)}) async-start(bf16[16,16,512]{2,1,0:T(8,128)(2,1)} %broadcast_in_dim.45), calls=%async_computation.1 | async-start | bytes 524288 | tf_op jit(solution)/shard_map/all_to_all | solution.py:470
  25.6 1.0 %scale_embedding.1 = (bf16[272,3072]{1,0:T(8,128)(2,1)S(1)}, bf16[3,128,128]{2,1,0:T(8,128)(2,1)S(1)}, f32[8,128]{1,0:T(8,128)S(1)}) custom-call(bf16[8,64]{1,0:T(8,128)(2,1)S(1)} %add_convert_fusion.member, bf16[64,6144]{1,0:T(8,128)(2,1)S(1)} %copy-done.1, bf16[64,3072]{1,0:T(8,128)(2,1)S(1)} %copy-done.2, f32[1,3072]{1,0:T(1,128)S(1)} %bitcast.17), custom_call_target="tpu_custom_call" | custom-call | flops 100000000 | bytes 3000000 | tf_op jit(solution)/shard_map/scale_embedding/pallas_call | solution.py:263
  26.6 1.2 %copy-done = bf16[272,3072]{1,0:T(8,128)(2,1)} copy-done((bf16[272,3072]{1,0:T(8,128)(2,1)}, bf16[272,3072]{1,0:T(8,128)(2,1)S(1)}, u32[]{:S(2)}) %copy-start) | copy-done | bytes 1671192
  27.8 5.9 %mix_weights.1 = (bf16[2,128,768]{2,1,0:T(8,128)(2,1)}, f32[8,768]{1,0:T(8,128)}) custom-call(bf16[272,3072]{1,0:T(8,128)(2,1)} %copy-done, bf16[3072,768]{1,0:T(8,128)(2,1)} %qkv_w.1, f32[1,768]{1,0:T(1,128)} %reshape.62.qkv_b), custom_call_target="tpu_custom_call" | custom-call | flops 1300000000 | bytes 6000000 | tf_op jit(solution)/shard_map/mix_weights/pallas_call | solution.py:303
  33.7 1.3 %collective-permute-start.1 = (bf16[16,16,512]{2,1,0:T(8,128)(2,1)S(1)}, bf16[16,16,512]{2,1,0:T(8,128)(2,1)S(1)}, u32[]{:S(2)}, u32[]{:S(2)}) collective-permute-start(bf16[16,16,512]{2,1,0:T(8,128)(2,1)S(1)} %all-to-all-done.1.same), channel_id=1, source_target_pairs={{0,8},{8,0},{16,24},{24,16},{32,40},{40,32},{48,56},{56,48},{64,72... | collective-permute-start | bytes 786440 | tf_op jit(solution)/shard_map/ppermute | solution.py:403
  35.5 0.6 collective-permute-done.1.other
  36.1 1.3 %convolve.1 = (f32[16,512]{1,0:T(8,128)S(1)}, f32[16,256]{1,0:T(8,128)S(1)}, f32[16,256]{1,0:T(8,128)S(1)}) custom-call(s32[21]{0:T(128)S(1)} %pad_add_fusion.table, bf16[768,512]{1,0:T(8,128)(2,1)S(1)} %get-tuple-element.25.act, bf16[16,16,512]{2,1,0:T(8,128)(2,1)S(1)} %all-to-all-done.1.same, bf16[16,16,512]{2,1,0:T(8,128)(2,1)S(1)} %collective-permute-done.1.other, ...), custom_call_target="tpu_custom_call" | custom-call | flops 400000000 | bytes 2000000 | tf_op jit(solution)/shard_map/convolve/pallas_call | solution.py:140
  37.4 1.2 %collective-permute-start.2 = (f32[16,256]{1,0:T(8,128)S(1)}, f32[16,256]{1,0:T(8,128)S(1)}, u32[]{:S(2)}, u32[]{:S(2)}) collective-permute-start(f32[16,256]{1,0:T(8,128)S(1)} %get-tuple-element.35), channel_id=1, source_target_pairs={{0,1},{2,3},{4,5},{6,7},{1,0},{3,2},{5,4},{7,6},{8,9},{10,11},{12,... | collective-permute-start | bytes 49160 | tf_op jit(solution)/shard_map/ppermute | solution.py:408
  38.7 0.7 collective-permute-start.3
  39.3 0.8 collective-permute-done.2.first
  40.1 0.5 finish.1
  40.6 13.4 %all_to_all.20.frames = bf16[16,4,16,128]{3,2,1,0:T(8,128)(2,1)S(1)} all-to-all(bf16[16,4,16,128]{3,2,1,0:T(8,128)(2,1)S(1)} %finish.1), channel_id=1, replica_groups={{0,16,32,48,64,80,96,112,128,144,160,176,192,208,224,240},{8,24,40,56,7..., dimensions={0} | all-to-all | bytes 524288 | tf_op jit(solution)/shard_map/all_to_all | solution.py:470
  54.0 0.7 route.1
  54.7 3.0 %collective-permute-start.4 = (bf16[4,16,128]{2,1,0:T(8,128)(2,1)S(1)}, bf16[4,16,128]{2,1,0:T(8,128)(2,1)S(1)}, u32[]{:S(2)}, u32[]{:S(2)}) collective-permute-start(bf16[4,16,128]{2,1,0:T(8,128)(2,1)S(1)} %get-tuple-element.38), channel_id=1, source_target_pairs={{0,8},{8,0},{16,24},{24,16},{32,40},{40,32},{48,56},{56,48},{64,72... | collective-permute-start | bytes 49160 | tf_op jit(solution)/shard_map/ppermute | solution.py:403
  57.7 0.8 %collective-permute-done.4 = bf16[4,16,128]{2,1,0:T(8,128)(2,1)S(1)} collective-permute-done((bf16[4,16,128]{2,1,0:T(8,128)(2,1)S(1)}, bf16[4,16,128]{2,1,0:T(8,128)(2,1)S(1)}, u32[]{:S(2)}, u32[]{:S(2)}) %collective-permute-start.4) | collective-permute-done | bytes 16416 | tf_op jit(solution)/shard_map/ppermute | solution.py:403
  58.6 14.4 %all_to_all.21.tokens = bf16[8,4,16,128]{3,2,1,0:T(8,128)(2,1)S(1)} all-to-all(bf16[8,4,16,128]{3,2,1,0:T(8,128)(2,1)S(1)} %broadcast_in_dim.75), channel_id=1, replica_groups={{7,6,5,4,3,2,1,0},{15,14,13,12,11,10,9,8},{23,22,21,20,19,18,17,16},{31..., dimensions={0} | all-to-all | bytes 262144 | tf_op jit(solution)/shard_map/all_to_all | solution.py:485
  73.0 4.6 %attend.1 = bf16[8,4,2,16,256]{4,3,2,1,0:T(8,128)(2,1)} custom-call(s32[21]{0:T(128)S(1)} %pad_add_fusion.table, bf16[8,4,16,128]{3,2,1,0:T(8,128)(2,1)S(1)} %all_to_all.21.tokens, bf16[2,128,768]{2,1,0:T(8,128)(2,1)S(1)} %copy-done.6, f32[8,768]{1,0:T(8,128)S(1)} %copy-done.7, bf16[3,128,128]{2,1,0:T(8,128)(2,1)S(1)} %get-tuple-element.41.gram, ...), custom_call_target="tpu_custom_call" | custom-call | flops 1000000000 | bytes 3000000 | tf_op jit(solution)/shard_map/attend/pallas_call | solution.py:384
  (51 shorter events, 1.5 us)
Async XLA Ops:
  0.0 11.6 %copy-start.3 = (bf16[4,2,64,512]{3,2,1,0:T(8,128)(2,1)S(1)}, bf16[4,2,64,512]{3,2,1,0:T(8,128)(2,1)}, u32[]{:S(2)}) copy-start(bf16[4,2,64,512]{3,2,1,0:T(8,128)(2,1)} %main.1) | copy-start | bytes 1572868
  0.0 15.7 %copy-start.13 = (s32[64]{0:T(128)S(1)}, s32[64]{0:T(128)}, u32[]{:S(2)}) copy-start(s32[64]{0:T(128)} %param.15) | copy-start | bytes 772
  0.0 15.8 %copy-start.11 = (s32[64]{0:T(128)S(1)}, s32[64]{0:T(128)}, u32[]{:S(2)}) copy-start(s32[64]{0:T(128)} %param.16) | copy-start | bytes 772
  0.0 17.7 %copy-start.12 = (f32[768]{0:T(1024)S(1)}, f32[768]{0:T(1024)}, u32[]{:S(2)}) copy-start(f32[768]{0:T(1024)} %param.25) | copy-start | bytes 9220
  0.0 25.6 %copy-start.1 = (bf16[64,6144]{1,0:T(8,128)(2,1)S(1)}, bf16[64,6144]{1,0:T(8,128)(2,1)}, u32[]{:S(2)}) copy-start(bf16[64,6144]{1,0:T(8,128)(2,1)} %modulation.1) | copy-start | bytes 2359300
  0.0 25.6 %copy-start.2 = (bf16[64,3072]{1,0:T(8,128)(2,1)S(1)}, bf16[64,3072]{1,0:T(8,128)(2,1)}, u32[]{:S(2)}) copy-start(bf16[64,3072]{1,0:T(8,128)(2,1)} %embed.1) | copy-start | bytes 1179652
  0.0 25.5 %copy-start.5 = (f32[3072]{0:T(1024)S(1)}, f32[3072]{0:T(1024)}, u32[]{:S(2)}) copy-start(f32[3072]{0:T(1024)} %param.22) | copy-start | bytes 36868
  1.8 16.4 %all-to-all-start = ((bf16[8,16,512]{2,1,0:T(8,128)(2,1)}), bf16[8,16,512]{2,1,0:T(8,128)(2,1)S(1)}, u32[]{:S(2)}, u32[]{:S(2)}) async-start(bf16[8,16,512]{2,1,0:T(8,128)(2,1)} %fold_tap.1), calls=%async_computation | async-start | bytes 262144 | tf_op jit(solution)/shard_map/all_to_all | solution.py:437
  11.6 23.5 %collective-permute-start = (bf16[2,2,64,512]{3,2,1,0:T(8,128)(2,1)S(1)}, bf16[2,2,64,512]{3,2,1,0:T(8,128)(2,1)S(1)}, u32[]{:S(2)}, u32[]{:S(2)}) collective-permute-start(bf16[2,2,64,512]{3,2,1,0:T(8,128)(2,1)S(1)} %slice.3), channel_id=1, source_target_pairs={{0,8},{8,16},{16,24},{24,32},{32,40},{40,48},{48,56},{56,64},{64,7... | collective-permute-start | bytes 786440 | tf_op jit(solution)/shard_map/ppermute | solution.py:399
  19.0 14.6 %all-to-all-start.1 = ((bf16[16,16,512]{2,1,0:T(8,128)(2,1)}), bf16[16,16,512]{2,1,0:T(8,128)(2,1)S(1)}, u32[]{:S(2)}, u32[]{:S(2)}) async-start(bf16[16,16,512]{2,1,0:T(8,128)(2,1)} %broadcast_in_dim.45), calls=%async_computation.1 | async-start | bytes 524288 | tf_op jit(solution)/shard_map/all_to_all | solution.py:470
  26.6 1.2 %copy-start = (bf16[272,3072]{1,0:T(8,128)(2,1)}, bf16[272,3072]{1,0:T(8,128)(2,1)S(1)}, u32[]{:S(2)}) copy-start(bf16[272,3072]{1,0:T(8,128)(2,1)S(1)} %get-tuple-element.27.left) | copy-start | bytes 5013508
  27.8 7.2 %copy-start.14 = (f32[16]{0:T(128)S(1)}, f32[16]{0:T(128)}, u32[]{:S(2)}) copy-start(f32[16]{0:T(128)} %param.20) | copy-start | bytes 196
  27.8 7.2 %copy-start.4 = (bf16[512,16]{0,1:T(8,128)(2,1)S(1)}, bf16[512,16]{0,1:T(8,128)(2,1)}, u32[]{:S(2)}) copy-start(bf16[512,16]{0,1:T(8,128)(2,1)} %param.19) | copy-start | bytes 49156
  27.8 7.2 %copy-start.8 = (f32[512]{0:T(512)S(1)}, f32[512]{0:T(512)}, u32[]{:S(2)}) copy-start(f32[512]{0:T(512)} %param.18) | copy-start | bytes 6148
  33.7 2.4 %collective-permute-start.1 = (bf16[16,16,512]{2,1,0:T(8,128)(2,1)S(1)}, bf16[16,16,512]{2,1,0:T(8,128)(2,1)S(1)}, u32[]{:S(2)}, u32[]{:S(2)}) collective-permute-start(bf16[16,16,512]{2,1,0:T(8,128)(2,1)S(1)} %all-to-all-done.1.same), channel_id=1, source_target_pairs={{0,8},{8,0},{16,24},{24,16},{32,40},{40,32},{48,56},{56,48},{64,72... | collective-permute-start | bytes 786440 | tf_op jit(solution)/shard_map/ppermute | solution.py:403
  35.5 37.4 %copy-start.6 = (bf16[2,128,768]{2,1,0:T(8,128)(2,1)S(1)}, bf16[2,128,768]{2,1,0:T(8,128)(2,1)}, u32[]{:S(2)}) copy-start(bf16[2,128,768]{2,1,0:T(8,128)(2,1)} %get-tuple-element.39.mix) | copy-start | bytes 1179652
  35.5 37.4 %copy-start.7 = (f32[8,768]{1,0:T(8,128)S(1)}, f32[8,768]{1,0:T(8,128)}, u32[]{:S(2)}) copy-start(f32[8,768]{1,0:T(8,128)} %get-tuple-element.40.rows) | copy-start | bytes 73732
  35.5 37.4 %copy-start.9 = (f32[128]{0:T(128)S(1)}, f32[128]{0:T(128)}, u32[]{:S(2)}) copy-start(f32[128]{0:T(128)} %param.26) | copy-start | bytes 1540
  35.5 37.4 %copy-start.10 = (f32[128]{0:T(128)S(1)}, f32[128]{0:T(128)}, u32[]{:S(2)}) copy-start(f32[128]{0:T(128)} %param.27) | copy-start | bytes 1540
  37.4 2.7 %collective-permute-start.2 = (f32[16,256]{1,0:T(8,128)S(1)}, f32[16,256]{1,0:T(8,128)S(1)}, u32[]{:S(2)}, u32[]{:S(2)}) collective-permute-start(f32[16,256]{1,0:T(8,128)S(1)} %get-tuple-element.35), channel_id=1, source_target_pairs={{0,1},{2,3},{4,5},{6,7},{1,0},{3,2},{5,4},{7,6},{8,9},{10,11},{12,... | collective-permute-start | bytes 49160 | tf_op jit(solution)/shard_map/ppermute | solution.py:408
  38.7 1.4 %collective-permute-start.3 = (f32[16,256]{1,0:T(8,128)S(1)}, f32[16,256]{1,0:T(8,128)S(1)}, u32[]{:S(2)}, u32[]{:S(2)}) collective-permute-start(f32[16,256]{1,0:T(8,128)S(1)} %get-tuple-element.36), channel_id=1, source_target_pairs={{1,2},{3,4},{5,6},{2,1},{4,3},{6,5},{9,10},{11,12},{13,14},{10,9},... | collective-permute-start | bytes 49160 | tf_op jit(solution)/shard_map/ppermute | solution.py:408
  54.7 3.9 %collective-permute-start.4 = (bf16[4,16,128]{2,1,0:T(8,128)(2,1)S(1)}, bf16[4,16,128]{2,1,0:T(8,128)(2,1)S(1)}, u32[]{:S(2)}, u32[]{:S(2)}) collective-permute-start(bf16[4,16,128]{2,1,0:T(8,128)(2,1)S(1)} %get-tuple-element.38), channel_id=1, source_target_pairs={{0,8},{8,0},{16,24},{24,16},{32,40},{40,32},{48,56},{56,48},{64,72... | collective-permute-start | bytes 49160 | tf_op jit(solution)/shard_map/ppermute | solution.py:403
